TPU v7x, 32 devices: a whole 2x2x4 slice. The times are simulated.
32 devices in a mesh: rep: 2 (over y), tp: 8 (over z, x), dp: 2 (over core).
Axes of the slice: x: 2, y: 2, z: 4, core: 2. Of those that a mesh axis runs over, the one named last changes fastest.
Arguments:
- tokens: bfloat16 [4096, 8192], P(('rep', 'dp'), 'tp'), parts along dimension 0, may hold values from -6 to 6
- query_weight: bfloat16 [8192, 8192], P('dp', 'tp'), may hold values from -0.0625 to 0.0625
- shrink_factors: bfloat16 [8192, 2048], P(None, ('rep', 'tp')), parts along dimension 1, may hold values from -0.0625 to 0.0625
- expand_factors: bfloat16 [2048, 8192], P(('rep', 'tp')), parts along dimension 0, may hold values from -1.5 to 1.5
- row_adapter_index: int32 [4096, 1], P(('rep', 'dp')), parts along dimension 0, may hold values from 0 to 63, as said below
- adapter_storage_block: int32 [128], P('rep'), parts along dimension 0, may hold values from 0 to 63, as said below
Outputs:
- query: bfloat16 [4096, 8192], P(('rep', 'dp'), 'tp'), parts along dimension 0
There are 2 independent parts, one for each index of `rep`. A program takes and returns all parts, laid end to end along the dimension named above; an argument that names none is the same for every part. Nothing has to cross between parts.
Inputs may be any that keep to these rules, and one draw needn't show every extreme that they name: adapter_storage_block is a permutation of 0 to 63; storage block p lies on tp index p // 8. `row_adapter_index`: in each aligned block of 1024 rows, at most 256 rows use adapters whose storage blocks lie on one tp index, and in every block some tp index has exactly 256 such rows.
All inputs are finite; a program needn't handle non-finite values.
Results may differ from a plain program's by a relative error of at most 0.0051.
Values may be sent and summed in bfloat16 or wider, within the bound.
No kernel may reach another device: no remote copies, remote signals or barrier semaphores. Data moves between devices by JAX's collectives and lax.ppermute only.
A program may use at most 192 MiB of HBM per device.

v0:
```python
import jax
import jax.numpy as jnp
from jax import lax
from jax.sharding import PartitionSpec as P

ADAPTER_RANK = 16


def body(
    tokens, query_weight, shrink_factors, expand_factors, row_adapter_index, adapter_storage_block
):
    holder_count = lax.axis_size("tp")
    own_index = lax.axis_index("tp")
    row_count = tokens.shape[0]
    capacity = 2 * row_count // holder_count
    rows_per_holder = shrink_factors.shape[1] // ADAPTER_RANK
    full_rows = lax.all_gather(tokens, "tp", axis=1, tiled=True)
    weight = lax.all_gather(query_weight, "dp", axis=0, tiled=True)
    base_output = jnp.dot(full_rows, weight, preferred_element_type=jnp.float32)
    storage_weights = jnp.take(adapter_storage_block, row_adapter_index[:, 0])
    owner_of = storage_weights // rows_per_holder
    local_of = storage_weights % rows_per_holder
    onehot = (owner_of[:, None] == jnp.arange(holder_count)[None, :]).astype(jnp.int32)
    rank_in_owner = jnp.sum(jnp.cumsum(onehot, axis=0) * onehot, axis=1) - 1
    select = (owner_of[None, :] == own_index) & (
        rank_in_owner[None, :] == jnp.arange(capacity)[:, None]
    )
    selected_rows = jnp.dot(
        select.astype(jnp.bfloat16), full_rows, preferred_element_type=jnp.float32
    ).astype(jnp.bfloat16)
    picked_local = jnp.sum(select.astype(jnp.int32) * local_of[None, :], axis=1)
    reduced_rows = jnp.dot(selected_rows, shrink_factors, preferred_element_type=jnp.float32)
    column_block = jnp.arange(rows_per_holder * ADAPTER_RANK) // ADAPTER_RANK
    keep_mask = column_block[None, :] == picked_local[:, None]
    masked = jnp.where(keep_mask, reduced_rows, 0.0)
    compact = jnp.sum(masked.reshape(capacity, rows_per_holder, ADAPTER_RANK), axis=1)
    spread = jnp.dot(select.T.astype(jnp.float32), compact, precision=lax.Precision.HIGHEST)
    shrink_all = lax.psum(spread, "tp").astype(jnp.bfloat16)
    columns = lax.all_to_all(
        expand_factors.reshape(rows_per_holder * ADAPTER_RANK, holder_count, -1),
        "tp",
        split_axis=1,
        concat_axis=0,
        tiled=True,
    )
    columns = columns.reshape(holder_count * rows_per_holder, ADAPTER_RANK, -1)
    factor_rows = jnp.take(columns, storage_weights, axis=0)
    adapter_output = jnp.einsum(
        "tr,trc->tc", shrink_all, factor_rows, preferred_element_type=jnp.float32
    ).astype(jnp.bfloat16)
    adapter_output = lax.optimization_barrier(adapter_output)
    return (base_output + adapter_output.astype(jnp.float32)).astype(jnp.bfloat16)


def solution(mesh):
    placed = (
        P(("rep", "dp"), "tp"),
        P("dp", "tp"),
        P(None, ("rep", "tp")),
        P(("rep", "tp"), None),
        P(("rep", "dp"), None),
        P("rep"),
    )
    return jax.shard_map(
        body, mesh=mesh, in_specs=placed, out_specs=P(("rep", "dp"), "tp"), check_vma=False
    )
```

profile of v0, /device:TPU:0, one launch (start us, length us, event | category | flops | bytes accessed | tf_op | source)
XLA Modules:
  0.0 371.8 jit_solution(9067728770260617781)
XLA Ops:
  6.5 0.7 all-gather.3.cloned.1.call-update
  7.3 0.7 all-gather.5.cloned.1.call-update
  8.0 4.1 %copy.11 = bf16[128,8192]{0,1:T(8,128)(2,1)} copy(bf16[128,8192]{1,0:T(8,128)(2,1)} %param.9) | data formatting | bytes 4194304 | tf_op args[3]
  12.1 7.3 %all-to-all-start = ((bf16[128,8,1024]{0,2,1:T(8,128)(2,1)}), bf16[128,8,1024]{0,2,1:T(8,128)(2,1)}, u32[]{:S(2)}, u32[]{:S(2)}) async-start(bf16[128,8,1024]{0,2,1:T(8,128)(2,1)} %bitcast.108), calls=%async_computation | async-start | bytes 4194304 | tf_op jit(solution)/shard_map/all_to_all | solution.py:39
  19.4 0.7 fusion.22
  20.0 0.7 fusion.19
  20.8 0.7 fusion.20
  21.5 0.7 fusion.21
  22.2 4.2 %compare_select_fusion.1 = (s32[1024,1]{0,1:T(1,128)S(1)}, s32[1024,1]{0,1:T(1,128)S(1)}) fusion(s32[]{:T(128)} %bitcast.57, s32[]{:T(128)} %bitcast.58, s32[]{:T(128)} %bitcast.59, s32[]{:T(128)} %bitcast.60, s32[]{:T(128)} %bitcast.61, s32[]{:T(128)} %bitcast.63, s32[]{:T(128)} %bitcast.62, s32[1024,1]{0,1:T(1,128)S(1)} %copy-done.3), kind=kLoop, calls=%fused_computation.84 | loop fusion | flops 15360 | bytes 12316 | tf_op jit(solution)/shard_map/jit(_take)/gather | solution.py:20
  26.4 0.7 fusion.18
  27.2 35.8 %add_select_fusion = (s32[1024]{0:T(1024)S(1)}, s32[1024]{0:T(1024)S(1)}) fusion(pred[1024]{0:T(1024)(128)(4,1)S(1)} %get-tuple-element.5, pred[1024]{0:T(1024)(128)(4,1)S(1)} %get-tuple-element.61, pred[1024]{0:T(1024)(128)(4,1)S(1)} %get-tuple-element.60, pred[1024]{0:T(1024)(128)(4,1)S(1)} %get-tuple-element.62, ...), kind=kLoop, calls=%fused_computation.97 | loop fusion | flops 70656 | bytes 71908 | tf_op jit(solution)/shard_map/jit(remainder)/select_n | solution.py:22
  63.1 2.3 reduce-window.6
  65.9 0.3 select_reduce_fusion
  66.3 52.1 %all-to-all-done = bf16[128,8,1024]{0,2,1:T(8,128)(2,1)} async-done(((bf16[128,8,1024]{0,2,1:T(8,128)(2,1)}), bf16[128,8,1024]{0,2,1:T(8,128)(2,1)}, u32[]{:S(2)}, u32[]{:S(2)}) %all-to-all-start) | async-done | bytes 2097184 | tf_op jit(solution)/shard_map/all_to_all | solution.py:39
  118.4 3.9 %copy.12 = bf16[8,128,1,1024]{3,1,0,2:T(8,128)(2,1)} copy(bf16[8,128,1,1024]{1,3,0,2:T(8,128)(2,1)} %bitcast.73) | data formatting | bytes 4194304 | tf_op jit(solution)/shard_map/all_to_all | solution.py:39
  122.3 20.4 %gather_fusion = bf16[1024,16,1024]{2,1,0:T(8,128)(2,1)} fusion(bf16[64,16,1024]{2,1,0:T(8,128)(2,1)} %bitcast.107, s32[1024]{0:T(1024)S(1)} %broadcast_clamp_fusion), kind=kCustom, calls=%fused_computation | custom fusion | bytes 67112960 | tf_op jit(solution)/shard_map/jit(_take)/gather | solution.py:47
  142.7 138.2 %all-gather.3.cloned.1.call-done = bf16[1024,8192]{1,0:T(8,128)(2,1)} async-done(((bf16[1024,1024]{1,0:T(8,128)(2,1)}), bf16[1024,8192]{1,0:T(8,128)(2,1)}) %all-gather.3.cloned.1.call-update) | async-done | bytes 16777232 | tf_op jit(solution)/shard_map/all_gather | solution.py:17
  280.9 9.5 %convolution_select_fusion = f32[256,128]{0,1:T(8,128)S(1)} fusion(bf16[8192,128]{1,0:T(8,128)(2,1)S(1)} %copy-done, s32[256]{0:T(256)S(1)} %select_reduce_fusion, s32[128]{0:T(128)S(1)} %and_select_fusion.1, bf16[1024,8192]{1,0:T(8,128)(2,1)} %all-gather.3.cloned.1.call-done, s32[1024]{0:T(1024)S(1)} %broadcast_add_fusion, pred[1024]{0:T(1024)(128)(4,1)S(1)} %fusion.15), kind=kOutput, calls=%fused_computation.8 | convolution fusion | flops 4834525184 | bytes 19012096 | tf_op jit(solution)/shard_map/dot_general | solution.py:32
  290.4 0.5 fusion.5
  290.9 34.6 %psum.7 = bf16[1024,16]{0,1:T(8,128)(2,1)S(1)} all-reduce(f32[1024,16]{0,1:T(8,128)S(1)} %fusion.5), channel_id=1, replica_groups=mesh['rep'=2,'tp'=8,'dp'=2] {'tp'}, use_global_device_ids=true, to_apply=%region_5.6 | all-reduce | flops 16384 | bytes 98304 | tf_op jit(solution)/shard_map/psum | solution.py:38
  325.5 0.4 copy.13
  325.9 12.9 %fusion = bf16[1024,1,1024]{2,1,0:T(2,128)(2,1)S(1)} fusion(bf16[1024,16,1]{1,2,0:T(2,128)(2,1)S(1)} %copy.13, bf16[1024,16,1024]{2,1,0:T(8,128)(2,1)} %gather_fusion, pred[1024]{0:T(1024)(128)(4,1)S(1)} %get-tuple-element.63), kind=kOutput, calls=%fused_computation.1 | convolution fusion | flops 50331648 | bytes 35685376 | tf_op jit(solution)/shard_map/tr,trc->tc/dot_general | solution.py:48
  338.8 2.1 copy.18
  340.9 24.1 %add_convert_fusion = bf16[1024,1024]{1,0:T(8,128)(2,1)} fusion(bf16[1024,1024]{1,0:T(8,128)(2,1)} %bitcast.109, bf16[1024,8192]{1,0:T(8,128)(2,1)} %all-gather.3.cloned.1.call-done, bf16[8192,1024]{1,0:T(8,128)(2,1)} %all-gather.5.cloned.1.call-done), kind=kOutput, calls=%fused_computation.7 | convolution fusion | flops 17183014912 | bytes 37748736 | tf_op jit(solution)/shard_map/dot_general | solution.py:19
  (23 shorter events, 0.7 us)
Async XLA Ops:
  6.5 274.3 %copy-start = (bf16[8192,128]{1,0:T(8,128)(2,1)S(1)}, bf16[8192,128]{1,0:T(8,128)(2,1)}, u32[]{:S(2)}) copy-start(bf16[8192,128]{1,0:T(8,128)(2,1)} %param.8) | copy-start | bytes 6291460
  6.5 274.3 %all-gather.3.cloned.1.call-start = ((), (), s32[]{:S(2)}) async-start(), calls=%async_computation.1 | async-start | bytes 18874368 | tf_op jit(solution)/shard_map/all_gather | solution.py:17
  7.3 12.1 %copy-start.2 = (s32[64]{0:T(128)S(1)}, s32[64]{0:T(128)}, u32[]{:S(2)}) copy-start(s32[64]{0:T(128)} %param.11) | copy-start | bytes 772
  7.3 15.0 %copy-start.3 = (s32[1024,1]{0,1:T(1,128)S(1)}, s32[1024,1]{0,1:T(1,128)}, u32[]{:S(2)}) copy-start(s32[1024,1]{0,1:T(1,128)} %param.10) | copy-start | bytes 12292
  7.3 333.6 %all-gather.5.cloned.1.call-start = ((), (), s32[]{:S(2)}) async-start(), calls=%async_computation.2 | async-start | bytes 25165824 | tf_op jit(solution)/shard_map/all_gather | solution.py:18
  12.1 106.3 %all-to-all-start = ((bf16[128,8,1024]{0,2,1:T(8,128)(2,1)}), bf16[128,8,1024]{0,2,1:T(8,128)(2,1)}, u32[]{:S(2)}, u32[]{:S(2)}) async-start(bf16[128,8,1024]{0,2,1:T(8,128)(2,1)} %bitcast.108), calls=%async_computation | async-start | bytes 4194304 | tf_op jit(solution)/shard_map/all_to_all | solution.py:39
  340.9 24.1 %copy-start.1 = (bf16[8192,128]{1,0:T(8,128)(2,1)S(1)}, bf16[8192,128]{1,0:T(8,128)(2,1)}, u32[]{:S(2)}) copy-start(bf16[8192,128]{1,0:T(8,128)(2,1)} %param.8) | copy-start | bytes 6291460
Sparse Core Ops, SparseCore 0:
  9.5 271.2 all-gather.2
  282.4 28.2 all-gather.4
where the time goes:
time: 373 us; the launch traced here: 372 us
  waiting for transfers between devices  192 us (51%)
  matrix products  46.9 us (13%)
  other arithmetic  43.7 us (12%)
  blocking collectives  34.6 us (9%)
  local copies, waits for them, and re-layouts  34.1 us (9%)
  between operations  13.5 us (4%)
  starting transfers between devices  7.29 us (2%)
    all_gather x1, waiting for transfers between devices, body(): full_rows = lax.all_gather(tokens, 'tp', axis=1, tiled=True)  138 us
    all_to_all x1, waiting for transfers between devices, body(): lax.all_to_all(expand_factors.reshape(rows_per_holder * ADAPTER_RANK, hol...  52.1 us
    select_n x1, other arithmetic, body(): local_of = storage_weights % rows_per_holder  35.8 us
    psum x1, blocking collectives, body(): shrink_all = lax.psum(spread, 'tp').astype(jnp.bfloat16)  34.6 us
    dot_general x1, matrix products, body(): base_output = jnp.dot(full_rows, weight, preferred_element_type=jnp.float32)  24.1 us
    gather x1, local copies, waits for them, and re-layouts, body(): factor_rows = jnp.take(columns, storage_weights, axis=0)  20.4 us
    dot_general x1, matrix products, body(): jnp.einsum('tr,trc->tc', shrink_all, factor_rows, preferred_element_type=...  12.9 us
    dot_general x1, matrix products, body(): jnp.dot(selected_rows, shrink_factors, preferred_element_type=jnp.float32)  9.5 us
  transfers between devices with their start and end apart: 3, of which 2 were waited for; matrix products, arithmetic and copies ran while one was open for 27% of the time, Pallas kernels for 0%

commit v1 on v0

--- a/solution.py
+++ b/solution.py
@@ -4,16 +4,17 @@
 from jax.sharding import PartitionSpec as P
 
 ADAPTER_RANK = 16
+ROW_CHUNKS = (256, 256, 256, 256)
 
 
-def body(
+def general_body(
     tokens, query_weight, shrink_factors, expand_factors, row_adapter_index, adapter_storage_block
 ):
     holder_count = lax.axis_size("tp")
     own_index = lax.axis_index("tp")
+    rows_per_holder = shrink_factors.shape[1] // ADAPTER_RANK
     row_count = tokens.shape[0]
     capacity = 2 * row_count // holder_count
-    rows_per_holder = shrink_factors.shape[1] // ADAPTER_RANK
     full_rows = lax.all_gather(tokens, "tp", axis=1, tiled=True)
     weight = lax.all_gather(query_weight, "dp", axis=0, tiled=True)
     base_output = jnp.dot(full_rows, weight, preferred_element_type=jnp.float32)
@@ -52,6 +53,131 @@
     return (base_output + adapter_output.astype(jnp.float32)).astype(jnp.bfloat16)
 
 
+def dot(a, b):
+    return jnp.dot(a, b, preferred_element_type=jnp.float32)
+
+
+def pick(a, j):
+    return lax.dynamic_index_in_dim(a, j, 0, keepdims=False)
+
+
+def line_body(
+    tokens, query_weight, shrink_factors, expand_factors, row_adapter_index, adapter_storage_block
+):
+    tp = lax.axis_size("tp")
+    planes = tp // 2
+    own = lax.axis_index("tp")
+    z, x = own // 2, own % 2
+    r, d = lax.axis_index("rep"), lax.axis_index("dp")
+    rows, depth = tokens.shape
+    width = query_weight.shape[1]
+    holder_columns = shrink_factors.shape[1]
+    holder_adapters = holder_columns // ADAPTER_RANK
+    half = holder_columns // 2
+    across = [(i, i ^ 1) for i in range(tp)]
+    swap = [(0, 1), (1, 0)]
+
+    def up(h):
+        return [(i, i + 2) for i in range(2 * (h - 1), tp - 2)]
+
+    def down(h):
+        return [(i + 2, i) for i in range(0, tp - 2 * h)]
+
+    def place(plane):
+        return 2 * ((plane // 2) ^ d) + ((plane % 2) ^ r)
+
+    def plane_at(p):
+        return 2 * ((p // 2) ^ d) + ((p % 2) ^ r)
+
+    blocks = query_weight.reshape(planes, depth, width)
+    outgoing = pick(blocks, 2 * r + (1 - x))
+    near, far = [], []
+    for part in jnp.split(outgoing, 2):
+        got = lax.ppermute(part, "tp", across)
+        near.append(got)
+        far.append(lax.ppermute(got, "rep", swap))
+    own_half = jnp.concatenate([pick(blocks, 2 * r + x), pick(blocks, 2 * (1 - r) + x)])
+    other_half = jnp.concatenate(near + far)
+    weight_own = jnp.concatenate([own_half, lax.ppermute(own_half, "dp", swap)])
+    weight_other = jnp.concatenate([other_half, lax.ppermute(other_half, "dp", swap)])
+
+    factors = shrink_factors.reshape(planes, 2, depth, holder_columns)
+    shrink_own = jnp.concatenate([pick(pick(factors, plane_at(p)), x) for p in range(planes)])
+    leaving = jnp.concatenate([pick(pick(factors, plane_at(p)), 1 - x) for p in range(planes // 2)])
+    shrink_near = lax.ppermute(leaving, "tp", across)
+    shrink_other = jnp.concatenate([shrink_near, lax.ppermute(shrink_near, "dp", swap)])
+    shrink = jnp.concatenate([shrink_own, shrink_other], axis=1)
+
+    expand_half = lax.dynamic_slice_in_dim(expand_factors, d * half, half, 0)
+    expand_half = expand_half.reshape(half, tp, width).transpose(1, 0, 2)
+    expand_half = lax.all_to_all(expand_half, "tp", split_axis=0, concat_axis=0, tiled=True)
+    expand_half = expand_half.reshape(tp * half, width)
+    expand = jnp.concatenate([expand_half, lax.ppermute(expand_half, "dp", swap)])
+
+    known = jnp.arange(adapter_storage_block.shape[0])
+    stored = jnp.sum(
+        jnp.where(row_adapter_index == known[None, :], adapter_storage_block[None, :], 0),
+        axis=1,
+        keepdims=True,
+    )
+    column = jnp.arange(2 * holder_columns)
+    column_adapter = (own ^ (column // holder_columns)) * holder_adapters + (
+        column % holder_columns
+    ) // ADAPTER_RANK
+    fold = (column[:, None] % ADAPTER_RANK == jnp.arange(ADAPTER_RANK)[None, :]).astype(jnp.bfloat16)
+    entry = jnp.arange(tp * holder_columns)
+    within = entry % (tp * half)
+    entry_adapter = (within // half) * holder_adapters + (
+        ((entry // (tp * half)) ^ d) * half + within % half
+    ) // ADAPTER_RANK
+    unfold = (jnp.arange(ADAPTER_RANK)[:, None] == entry[None, :] % ADAPTER_RANK).astype(jnp.bfloat16)
+
+    def lora(parts, first, count):
+        shrunk = jnp.concatenate(parts)
+        everyone = jnp.broadcast_to(shrunk[None], (tp,) + shrunk.shape)
+        everyone = lax.all_to_all(everyone, "tp", split_axis=0, concat_axis=0, tiled=True)
+        total = jnp.sum(everyone.astype(jnp.float32), axis=0).astype(jnp.bfloat16)
+        spread = dot(total, unfold)
+        mine = stored[first : first + count] == entry_adapter[None, :]
+        return jnp.where(mine, spread, 0.0).astype(jnp.bfloat16)
+
+    chunks = []
+    first = 0
+    gates = []
+    for number, count in enumerate(ROW_CHUNKS):
+        piece = tokens[first : first + count]
+        if number >= 2:
+            piece, _ = lax.optimization_barrier((piece, gates[number - 2]))
+        upward, downward = {0: piece}, {0: piece}
+        for h in range(1, planes):
+            upward[h] = lax.ppermute(upward[h - 1], "tp", up(h))
+            downward[h] = lax.ppermute(downward[h - 1], "tp", down(h))
+        gates.append(downward[2])
+        line = jnp.zeros((count, planes * depth), tokens.dtype)
+        line = lax.dynamic_update_slice(line, piece, (0, place(z) * depth))
+        for j in range(1, planes):
+            block = jnp.where(z + j < planes, downward[j], upward[planes - j])
+            line = lax.dynamic_update_slice(line, block, (0, place((z + j) % planes) * depth))
+        partial = dot(line, weight_other).astype(jnp.bfloat16)
+        partial = lax.ppermute(partial, "tp", across)
+        reduced = dot(line, shrink)
+        mine = stored[first : first + count] == column_adapter[None, :]
+        shrunk = dot(jnp.where(mine, reduced, 0.0).astype(jnp.bfloat16), fold).astype(jnp.bfloat16)
+        base = dot(line, weight_own)
+        chunks.append((first, count, base, partial, shrunk))
+        first += count
+
+    outs = []
+    for group in (chunks[:-1], chunks[-1:]):
+        start = group[0][0]
+        size = sum(c[1] for c in group)
+        spread = lora([c[4] for c in group], start, size)
+        for first, count, base, partial, _ in group:
+            added = dot(spread[first - start : first - start + count], expand)
+            outs.append((base + partial.astype(jnp.float32) + added).astype(jnp.bfloat16))
+    return jnp.concatenate(outs)
+
+
 def solution(mesh):
     placed = (
         P(("rep", "dp"), "tp"),
@@ -61,6 +187,11 @@
         P(("rep", "dp"), None),
         P("rep"),
     )
+    lined = dict(mesh.shape) == {"rep": 2, "tp": 8, "dp": 2}
     return jax.shard_map(
-        body, mesh=mesh, in_specs=placed, out_specs=P(("rep", "dp"), "tp"), check_vma=False
+        line_body if lined else general_body,
+        mesh=mesh,
+        in_specs=placed,
+        out_specs=P(("rep", "dp"), "tp"),
+        check_vma=False,
     )

time: 373 us -> 286 us (0.77)
  waiting for transfers between devices: 192 us -> 76.6 us
  starting transfers between devices: 7.29 us -> 88.1 us
  blocking collectives: 34.6 us -> 0 us
  other arithmetic: 43.7 us -> 28.7 us
  between operations: 13.5 us -> 0.77 us
  matrix products: 46.9 us -> 55.1 us
    all_gather x2 -> x0, waiting for transfers between devices: 138 us -> none  [the longest x1 138 us: body(): full_rows = lax.all_gather(tokens, 'tp', axis=1, tiled=True)]
    ppermute x0 -> x37, waiting for transfers between devices: none -> 73.5 us  [the longest x12 51.9 us: line_body(): downward[h] = lax.ppermute(downward[h - 1], 'tp', down(h))]
    ppermute x0 -> x37, starting transfers between devices: none -> 71.9 us  [the longest x12 43 us: line_body(): upward[h] = lax.ppermute(upward[h - 1], 'tp', up(h))]
    all_to_all x1 -> x3, waiting for transfers between devices: 52.1 us -> 3.08 us  [the longest x2 3.07 us: lora(): lax.all_to_all(everyone, 'tp', split_axis=0, concat_axis=0, tiled=True)]
    select_n x3 -> x2, other arithmetic: 35.9 us -> 0.02 us  [the longest x1 0.01 us: line_body(): entry[None, :] % ADAPTER_RANK]
    psum x1 -> x0, blocking collectives: 34.6 us -> none  [body(): shrink_all = lax.psum(spread, 'tp').astype(jnp.bfloat16)]
    gather x5 -> x0, local copies, waits for them, and re-layouts: 23.3 us -> none  [the longest x1 20.4 us: body(): factor_rows = jnp.take(columns, storage_weights, axis=0)]
    dynamic_update_slice x0 -> x12, other arithmetic: none -> 19.6 us  [line_body(): lax.dynamic_update_slice(line, block, (0, place((z + j) % planes) * depth))]
  transfers between devices with their start and end apart: 3 -> 40, of which waited for: 2 -> 14; matrix products, arithmetic and copies ran while one was open for 27% -> 38% of each run, Pallas kernels for 0% -> 0%
where the time goes in v1:
time: 286 us; the launch traced here: 285 us
  starting transfers between devices  88.1 us (31%)
  waiting for transfers between devices  76.6 us (27%)
  matrix products  55.1 us (19%)
  local copies, waits for them, and re-layouts  35.3 us (12%)
  other arithmetic  28.7 us (10%)
    dot_general x17, matrix products, dot(): return jnp.dot(a, b, preferred_element_type=jnp.float32)  55.1 us
    ppermute x12, waiting for transfers between devices, line_body(): downward[h] = lax.ppermute(downward[h - 1], 'tp', down(h))  51.9 us
    ppermute x12, starting transfers between devices, line_body(): upward[h] = lax.ppermute(upward[h - 1], 'tp', up(h))  43 us
    dynamic_update_slice x12, other arithmetic, line_body(): lax.dynamic_update_slice(line, block, (0, place((z + j) % planes) * depth))  19.6 us
    ppermute x12, starting transfers between devices, line_body(): downward[h] = lax.ppermute(downward[h - 1], 'tp', down(h))  15.7 us
    ppermute x4, waiting for transfers between devices, line_body(): partial = lax.ppermute(partial, 'tp', across)  13.7 us
    all_to_all x2, starting transfers between devices, lora(): lax.all_to_all(everyone, 'tp', split_axis=0, concat_axis=0, tiled=True)  12 us
    unnamed x45, local copies, waits for them, and re-layouts  10.4 us
  transfers between devices with their start and end apart: 40, of which 14 were waited for; matrix products, arithmetic and copies ran while one was open for 38% of the time, Pallas kernels for 0%

profile of v1, /device:TPU:0, one launch (start us, length us, event | category | flops | bytes accessed | tf_op | source)
XLA Modules:
  0.0 284.6 jit_solution(1245851749224601761)
XLA Ops:
  5.5 6.4 %collective-permute-start.16 = (bf16[256,1024]{1,0:T(8,128)(2,1)}, bf16[256,1024]{1,0:T(8,128)(2,1)}, u32[]{:S(2)}, u32[]{:S(2)}) collective-permute-start(bf16[256,1024]{1,0:T(8,128)(2,1)} %get-tuple-element.14), channel_id=1, source_target_pairs={{0,4},{2,6},{4,8},{6,10},{8,12},{10,14},{1,5},{3,7},{5,9},{7,11},{... | collective-permute-start | bytes 1572872 | tf_op jit(solution)/shard_map/ppermute | solution.py:153
  19.1 4.2 %all-to-all-start.1 = ((bf16[8,64,1024]{2,1,0:T(8,128)(2,1)}), bf16[8,64,1024]{2,1,0:T(8,128)(2,1)}, u32[]{:S(2)}, u32[]{:S(2)}) async-start(bf16[8,64,1024]{2,1,0:T(8,128)(2,1)} %copy.12), calls=%async_computation.1 | async-start | bytes 2097152 | tf_op jit(solution)/shard_map/all_to_all | solution.py:113
  39.0 14.8 %collective-permute-done = bf16[256,1024]{1,0:T(8,128)(2,1)} collective-permute-done((bf16[256,1024]{1,0:T(8,128)(2,1)}, bf16[256,1024]{1,0:T(8,128)(2,1)}, u32[]{:S(2)}, u32[]{:S(2)}) %collective-permute-start) | collective-permute-done | bytes 524320 | tf_op jit(solution)/shard_map/ppermute | solution.py:154
  53.8 10.4 %collective-permute-start.1 = (bf16[256,1024]{1,0:T(8,128)(2,1)}, bf16[256,1024]{1,0:T(8,128)(2,1)S(1)}, u32[]{:S(2)}, u32[]{:S(2)}) collective-permute-start(bf16[256,1024]{1,0:T(8,128)(2,1)} %get-tuple-element.15), channel_id=1, source_target_pairs={{0,4},{2,6},{4,8},{6,10},{8,12},{10,14},{1,5},{3,7},{5,9},{7,11},{... | collective-permute-start | bytes 1572872 | tf_op jit(solution)/shard_map/ppermute | solution.py:153
  72.8 3.6 %collective-permute-done.4 = bf16[256,1024]{1,0:T(8,128)(2,1)S(1)} collective-permute-done((bf16[256,1024]{1,0:T(8,128)(2,1)}, bf16[256,1024]{1,0:T(8,128)(2,1)S(1)}, u32[]{:S(2)}, u32[]{:S(2)}) %collective-permute-start.4) | collective-permute-done | bytes 524320 | tf_op jit(solution)/shard_map/ppermute | solution.py:154
  86.0 10.7 %collective-permute-start.31 = (bf16[256,1024]{1,0:T(8,128)(2,1)}, bf16[256,1024]{1,0:T(8,128)(2,1)}, u32[]{:S(2)}, u32[]{:S(2)}) collective-permute-start(bf16[256,1024]{1,0:T(8,128)(2,1)} %get-tuple-element.8), channel_id=1, source_target_pairs={{0,4},{2,6},{4,8},{6,10},{8,12},{10,14},{1,5},{3,7},{5,9},{7,11},{... | collective-permute-start | bytes 1572872 | tf_op jit(solution)/shard_map/ppermute | solution.py:153
  103.4 12.2 %collective-permute-done.20 = bf16[256,1024]{1,0:T(8,128)(2,1)S(1)} collective-permute-done((bf16[256,1024]{1,0:T(8,128)(2,1)S(1)}, bf16[256,1024]{1,0:T(8,128)(2,1)S(1)}, u32[]{:S(2)}, u32[]{:S(2)}) %collective-permute-start.20) | collective-permute-done | bytes 524320 | tf_op jit(solution)/shard_map/ppermute | solution.py:154
  130.0 7.1 %collective-permute-done.5 = bf16[256,1024]{1,0:T(8,128)(2,1)S(1)} collective-permute-done((bf16[256,1024]{1,0:T(8,128)(2,1)}, bf16[256,1024]{1,0:T(8,128)(2,1)S(1)}, u32[]{:S(2)}, u32[]{:S(2)}) %collective-permute-start.5) | collective-permute-done | bytes 524320 | tf_op jit(solution)/shard_map/ppermute | solution.py:154
  139.4 5.3 %collective-permute-start.22 = (bf16[256,1024]{1,0:T(8,128)(2,1)}, bf16[256,1024]{1,0:T(8,128)(2,1)}, u32[]{:S(2)}, u32[]{:S(2)}) collective-permute-start(bf16[256,1024]{1,0:T(8,128)(2,1)} %get-tuple-element.7), channel_id=1, source_target_pairs={{0,4},{2,6},{4,8},{6,10},{8,12},{10,14},{1,5},{3,7},{5,9},{7,11},{... | collective-permute-start | bytes 1572872 | tf_op jit(solution)/shard_map/ppermute | solution.py:153
  155.6 6.2 %collective-permute-done.10 = bf16[512,1024]{1,0:T(8,128)(2,1)} collective-permute-done((bf16[512,1024]{1,0:T(8,128)(2,1)}, bf16[512,1024]{1,0:T(8,128)(2,1)}, u32[]{:S(2)}, u32[]{:S(2)}) %collective-permute-start.10) | collective-permute-done | bytes 1048608 | tf_op jit(solution)/shard_map/ppermute | solution.py:98
  163.1 3.6 %pad_maximum_fusion.2 = bf16[2048,1024]{1,0:T(8,128)(2,1)} fusion(bf16[512,1024]{1,0:T(8,128)(2,1)} %collective-permute-done.10, bf16[512,1024]{1,0:T(8,128)(2,1)} %collective-permute-done.9, bf16[512,1024]{1,0:T(8,128)(2,1)} %collective-permute-done.8, bf16[512,1024]{1,0:T(8,128)(2,1)S(1)} %collective-permute-done.7), kind=kLoop, calls=%fused_computation.2 | loop fusion | flops 16777216 | bytes 8388608 | tf_op jit(solution)/shard_map/concatenate | solution.py:100
  172.6 6.1 %collective-permute-done.25 = bf16[256,1024]{1,0:T(8,128)(2,1)} collective-permute-done((bf16[256,1024]{1,0:T(8,128)(2,1)}, bf16[256,1024]{1,0:T(8,128)(2,1)}, u32[]{:S(2)}, u32[]{:S(2)}) %collective-permute-start.25) | collective-permute-done | bytes 524320 | tf_op jit(solution)/shard_map/ppermute | solution.py:154
  180.2 6.5 %collective-permute-done.35 = bf16[256,1024]{1,0:T(8,128)(2,1)S(1)} collective-permute-done((bf16[256,1024]{1,0:T(8,128)(2,1)}, bf16[256,1024]{1,0:T(8,128)(2,1)S(1)}, u32[]{:S(2)}, u32[]{:S(2)}) %collective-permute-start.35) | collective-permute-done | bytes 524320 | tf_op jit(solution)/shard_map/ppermute | solution.py:154
  192.5 5.0 %all-to-all-start.2 = ((bf16[8,256,16]{1,2,0:T(8,128)(2,1)}), bf16[8,256,16]{1,2,0:T(8,128)(2,1)S(1)}, u32[]{:S(2)}, u32[]{:S(2)}) async-start(bf16[8,256,16]{1,2,0:T(8,128)(2,1)} %broadcast_in_dim.57), calls=%async_computation.2 | async-start | bytes 131072 | tf_op jit(solution)/shard_map/all_to_all | solution.py:138
  206.1 7.0 %all-to-all-start = ((bf16[8,768,16]{1,2,0:T(8,128)(2,1)}), bf16[8,768,16]{1,2,0:T(8,128)(2,1)S(1)}, u32[]{:S(2)}, u32[]{:S(2)}) async-start(bf16[8,768,16]{1,2,0:T(8,128)(2,1)} %broadcast_in_dim.33), calls=%async_computation | async-start | bytes 393216 | tf_op jit(solution)/shard_map/all_to_all | solution.py:138
  231.4 4.2 %convolution_convert_fusion = bf16[256,1024]{1,0:T(8,128)(2,1)S(1)} fusion(bf16[256,4096]{1,0:T(8,128)(2,1)} %select_dynamic-update-slice_fusion, bf16[4096,1024]{1,0:T(8,128)(2,1)S(1)} %constant_dynamic-update-slice_fusion), kind=kOutput, calls=%fused_computation.23 | convolution fusion | flops 2147745792 | bytes 11010048 | tf_op jit(solution)/shard_map/dot_general | solution.py:57
  240.1 4.0 %convolution_convert_fusion.2 = bf16[256,1024]{1,0:T(8,128)(2,1)S(1)} fusion(bf16[256,4096]{1,0:T(8,128)(2,1)} %select_dynamic-update-slice_fusion.6, bf16[4096,1024]{1,0:T(8,128)(2,1)S(1)} %constant_dynamic-update-slice_fusion), kind=kOutput, calls=%fused_computation.25 | convolution fusion | flops 2147745792 | bytes 11010048 | tf_op jit(solution)/shard_map/dot_general | solution.py:57
  244.2 4.1 %convolution_convert_fusion.3 = bf16[256,1024]{1,0:T(8,128)(2,1)S(1)} fusion(bf16[256,4096]{1,0:T(8,128)(2,1)} %select_dynamic-update-slice_fusion.9, bf16[4096,1024]{1,0:T(8,128)(2,1)S(1)} %constant_dynamic-update-slice_fusion), kind=kOutput, calls=%fused_computation.26 | convolution fusion | flops 2147745792 | bytes 11010048 | tf_op jit(solution)/shard_map/dot_general | solution.py:57
  250.5 4.8 %fusion.7 = bf16[256,1024]{1,0:T(8,128)(2,1)S(1)} fusion(f32[256,1024]{1,0:T(8,128)S(1)} %fusion.9, bf16[256,4096]{1,0:T(8,128)(2,1)} %select_dynamic-update-slice_fusion, bf16[256,1024]{1,0:T(8,128)(2,1)S(1)} %collective-permute-done.36, bf16[2048,1024]{1,0:T(8,128)(2,1)} %collective-permute-done.6, bf16[1024,1024]{1,0:T(8,128)(2,1)S(1)} %copy-done.4, ...), kind=kOutput, calls=%fused_computation.21 | convolution fusion | flops 2173698048 | bytes 12582912 | tf_op jit(solution)/shard_map/dot_general | solution.py:57
  255.3 6.4 %collective-permute-done.29 = bf16[256,1024]{1,0:T(8,128)(2,1)S(1)} collective-permute-done((bf16[256,1024]{1,0:T(8,128)(2,1)S(1)}, bf16[256,1024]{1,0:T(8,128)(2,1)S(1)}, u32[]{:S(2)}, u32[]{:S(2)}) %collective-permute-start.29) | collective-permute-done | bytes 524320 | tf_op jit(solution)/shard_map/ppermute | solution.py:162
  261.7 4.2 %fusion.6 = bf16[256,1024]{1,0:T(8,128)(2,1)S(1)} fusion(f32[256,1024]{1,0:T(8,128)S(1)} %fusion.23, bf16[256,4096]{1,0:T(8,128)(2,1)S(1)} %copy-done.7, bf16[256,1024]{1,0:T(8,128)(2,1)S(1)} %collective-permute-done.29, bf16[2048,1024]{1,0:T(8,128)(2,1)} %collective-permute-done.6, bf16[1024,1024]{1,0:T(8,128)(2,1)S(1)} %copy-done.4, ...), kind=kOutput, calls=%fused_computation.20 | convolution fusion | flops 2173698048 | bytes 12582912 | tf_op jit(solution)/shard_map/dot_general | solution.py:57
  265.9 6.3 %collective-permute-done.28 = bf16[256,1024]{1,0:T(8,128)(2,1)S(1)} collective-permute-done((bf16[256,1024]{1,0:T(8,128)(2,1)S(1)}, bf16[256,1024]{1,0:T(8,128)(2,1)S(1)}, u32[]{:S(2)}, u32[]{:S(2)}) %collective-permute-start.28) | collective-permute-done | bytes 524320 | tf_op jit(solution)/shard_map/ppermute | solution.py:162
  272.2 4.8 %fusion.5 = bf16[256,1024]{1,0:T(8,128)(2,1)S(1)} fusion(f32[256,1024]{1,0:T(8,128)S(1)} %fusion.25, bf16[256,4096]{1,0:T(8,128)(2,1)} %select_dynamic-update-slice_fusion.6, bf16[256,1024]{1,0:T(8,128)(2,1)S(1)} %collective-permute-done.28, bf16[2048,1024]{1,0:T(8,128)(2,1)} %collective-permute-done.6, bf16[1024,1024]{1,0:T(8,128)(2,1)S(1)} %copy-done.4, ...), kind=kOutput, calls=%fused_computation.19 | convolution fusion | flops 2173698048 | bytes 12582912 | tf_op jit(solution)/shard_map/dot_general | solution.py:57
  277.8 5.3 %fusion.4 = bf16[256,1024]{1,0:T(8,128)(2,1)S(1)} fusion(f32[256,1024]{1,0:T(8,128)S(1)} %fusion.27, bf16[256,4096]{1,0:T(8,128)(2,1)} %select_dynamic-update-slice_fusion.9, bf16[256,1024]{1,0:T(8,128)(2,1)S(1)} %collective-permute-done.12, bf16[2048,1024]{1,0:T(8,128)(2,1)} %collective-permute-done.6, bf16[1024,1024]{1,0:T(8,128)(2,1)S(1)} %copy-done.4, ...), kind=kOutput, calls=%fused_computation.18 | convolution fusion | flops 2173698048 | bytes 12582912 | tf_op jit(solution)/shard_map/dot_general | solution.py:57
  (158 shorter events, 130.5 us)
Async XLA Ops:
  4.2 28.9 %collective-permute-start.15 = (bf16[256,1024]{1,0:T(8,128)(2,1)}, bf16[256,1024]{1,0:T(8,128)(2,1)}, u32[]{:S(2)}, u32[]{:S(2)}) collective-permute-start(bf16[256,1024]{1,0:T(8,128)(2,1)} %get-tuple-element.14), channel_id=1, source_target_pairs={{4,0},{6,2},{8,4},{10,6},{12,8},{14,10},{5,1},{7,3},{9,5},{11,7},{... | collective-permute-start | bytes 1572872 | tf_op jit(solution)/shard_map/ppermute | solution.py:154
  5.5 58.8 %collective-permute-start.16 = (bf16[256,1024]{1,0:T(8,128)(2,1)}, bf16[256,1024]{1,0:T(8,128)(2,1)}, u32[]{:S(2)}, u32[]{:S(2)}) collective-permute-start(bf16[256,1024]{1,0:T(8,128)(2,1)} %get-tuple-element.14), channel_id=1, source_target_pairs={{0,4},{2,6},{4,8},{6,10},{8,12},{10,14},{1,5},{3,7},{5,9},{7,11},{... | collective-permute-start | bytes 1572872 | tf_op jit(solution)/shard_map/ppermute | solution.py:153
  14.9 21.4 %collective-permute-start.13 = (bf16[2048,128]{1,0:T(8,128)(2,1)}, bf16[2048,128]{1,0:T(8,128)(2,1)}, u32[]{:S(2)}, u32[]{:S(2)}) collective-permute-start(bf16[2048,128]{1,0:T(8,128)(2,1)} %pad_maximum_fusion.5), channel_id=1, source_target_pairs={{0,2},{2,0},{4,6},{6,4},{8,10},{10,8},{12,14},{14,12},{1,3},{3,1},... | collective-permute-start | bytes 1572872 | tf_op jit(solution)/shard_map/ppermute | solution.py:107
  19.1 153.0 %all-to-all-start.1 = ((bf16[8,64,1024]{2,1,0:T(8,128)(2,1)}), bf16[8,64,1024]{2,1,0:T(8,128)(2,1)}, u32[]{:S(2)}, u32[]{:S(2)}) async-start(bf16[8,64,1024]{2,1,0:T(8,128)(2,1)} %copy.12), calls=%async_computation.1 | async-start | bytes 2097152 | tf_op jit(solution)/shard_map/all_to_all | solution.py:113
  26.4 57.0 %collective-permute-start.7 = (bf16[512,1024]{1,0:T(8,128)(2,1)}, bf16[512,1024]{1,0:T(8,128)(2,1)S(1)}, u32[]{:S(2)}, u32[]{:S(2)}) collective-permute-start(bf16[512,1024]{1,0:T(8,128)(2,1)} %get-tuple-element.12), channel_id=1, source_target_pairs={{0,2},{2,0},{4,6},{6,4},{8,10},{10,8},{12,14},{14,12},{1,3},{3,1},... | collective-permute-start | bytes 3145736 | tf_op jit(solution)/shard_map/ppermute | solution.py:96
  28.3 25.6 %collective-permute-start = (bf16[256,1024]{1,0:T(8,128)(2,1)}, bf16[256,1024]{1,0:T(8,128)(2,1)}, u32[]{:S(2)}, u32[]{:S(2)}) collective-permute-start(bf16[256,1024]{1,0:T(8,128)(2,1)} %get-tuple-element.15), channel_id=1, source_target_pairs={{4,0},{6,2},{8,4},{10,6},{12,8},{14,10},{5,1},{7,3},{9,5},{11,7},{... | collective-permute-start | bytes 1572872 | tf_op jit(solution)/shard_map/ppermute | solution.py:154
  33.0 32.6 %collective-permute-start.19 = (bf16[256,1024]{1,0:T(8,128)(2,1)}, bf16[256,1024]{1,0:T(8,128)(2,1)S(1)}, u32[]{:S(2)}, u32[]{:S(2)}) collective-permute-start(bf16[256,1024]{1,0:T(8,128)(2,1)} %collective-permute-done.15), channel_id=1, source_target_pairs={{4,0},{6,2},{8,4},{10,6},{5,1},{7,3},{9,5},{11,7},{20,16},{22,18},... | collective-permute-start | bytes 1572872 | tf_op jit(solution)/shard_map/ppermute | solution.py:154
  36.3 49.7 %collective-permute-start.8 = (bf16[512,1024]{1,0:T(8,128)(2,1)}, bf16[512,1024]{1,0:T(8,128)(2,1)}, u32[]{:S(2)}, u32[]{:S(2)}) collective-permute-start(bf16[512,1024]{1,0:T(8,128)(2,1)} %get-tuple-element.11), channel_id=1, source_target_pairs={{0,2},{2,0},{4,6},{6,4},{8,10},{10,8},{12,14},{14,12},{1,3},{3,1},... | collective-permute-start | bytes 3145736 | tf_op jit(solution)/shard_map/ppermute | solution.py:96
  72.8 45.4 %collective-permute-start.14 = (bf16[2048,128]{1,0:T(8,128)(2,1)}, bf16[2048,128]{1,0:T(8,128)(2,1)S(1)}, u32[]{:S(2)}, u32[]{:S(2)}) collective-permute-start(bf16[2048,128]{1,0:T(8,128)(2,1)} %collective-permute-done.13), channel_id=1, source_target_pairs={{0,1},{1,0},{2,3},{3,2},{4,5},{5,4},{6,7},{7,6},{8,9},{9,8},{10,11... | collective-permute-start | bytes 1572872 | tf_op jit(solution)/shard_map/ppermute | solution.py:108
  76.5 42.2 %collective-permute-start.2 = (bf16[256,1024]{1,0:T(8,128)(2,1)S(1)}, bf16[256,1024]{1,0:T(8,128)(2,1)}, u32[]{:S(2)}, u32[]{:S(2)}) collective-permute-start(bf16[256,1024]{1,0:T(8,128)(2,1)S(1)} %collective-permute-done.1), channel_id=1, source_target_pairs={{4,8},{6,10},{8,12},{10,14},{5,9},{7,11},{9,13},{11,15},{20,24},{2... | collective-permute-start | bytes 1572872 | tf_op jit(solution)/shard_map/ppermute | solution.py:153
  77.9 21.0 %collective-permute-start.18 = (bf16[256,1024]{1,0:T(8,128)(2,1)S(1)}, bf16[256,1024]{1,0:T(8,128)(2,1)S(1)}, u32[]{:S(2)}, u32[]{:S(2)}) collective-permute-start(bf16[256,1024]{1,0:T(8,128)(2,1)S(1)} %collective-permute-done.17), channel_id=1, source_target_pairs={{8,12},{10,14},{9,13},{11,15},{24,28},{26,30},{25,29},{27,31}} | collective-permute-start | bytes 1572872 | tf_op jit(solution)/shard_map/ppermute | solution.py:153
  83.4 56.0 %collective-permute-start.30 = (bf16[256,1024]{1,0:T(8,128)(2,1)}, bf16[256,1024]{1,0:T(8,128)(2,1)}, u32[]{:S(2)}, u32[]{:S(2)}) collective-permute-start(bf16[256,1024]{1,0:T(8,128)(2,1)} %get-tuple-element.8), channel_id=1, source_target_pairs={{4,0},{6,2},{8,4},{10,6},{12,8},{14,10},{5,1},{7,3},{9,5},{11,7},{... | collective-permute-start | bytes 1572872 | tf_op jit(solution)/shard_map/ppermute | solution.py:154
  86.0 37.0 %collective-permute-start.31 = (bf16[256,1024]{1,0:T(8,128)(2,1)}, bf16[256,1024]{1,0:T(8,128)(2,1)}, u32[]{:S(2)}, u32[]{:S(2)}) collective-permute-start(bf16[256,1024]{1,0:T(8,128)(2,1)} %get-tuple-element.8), channel_id=1, source_target_pairs={{0,4},{2,6},{4,8},{6,10},{8,12},{10,14},{1,5},{3,7},{5,9},{7,11},{... | collective-permute-start | bytes 1572872 | tf_op jit(solution)/shard_map/ppermute | solution.py:153
  115.6 30.5 %collective-permute-start.9 = (bf16[512,1024]{1,0:T(8,128)(2,1)S(1)}, bf16[512,1024]{1,0:T(8,128)(2,1)}, u32[]{:S(2)}, u32[]{:S(2)}) collective-permute-start(bf16[512,1024]{1,0:T(8,128)(2,1)S(1)} %collective-permute-done.7), channel_id=1, source_target_pairs={{0,16},{16,0},{1,17},{17,1},{2,18},{18,2},{3,19},{19,3},{4,20},{20... | collective-permute-start | bytes 3145736 | tf_op jit(solution)/shard_map/ppermute | solution.py:98
  118.2 43.7 %collective-permute-start.10 = (bf16[512,1024]{1,0:T(8,128)(2,1)}, bf16[512,1024]{1,0:T(8,128)(2,1)}, u32[]{:S(2)}, u32[]{:S(2)}) collective-permute-start(bf16[512,1024]{1,0:T(8,128)(2,1)} %collective-permute-done.8), channel_id=1, source_target_pairs={{0,16},{16,0},{1,17},{17,1},{2,18},{18,2},{3,19},{19,3},{4,20},{20... | collective-permute-start | bytes 3145736 | tf_op jit(solution)/shard_map/ppermute | solution.py:98
  124.4 20.4 %collective-permute-start.32 = (bf16[256,1024]{1,0:T(8,128)(2,1)}, bf16[256,1024]{1,0:T(8,128)(2,1)}, u32[]{:S(2)}, u32[]{:S(2)}) collective-permute-start(bf16[256,1024]{1,0:T(8,128)(2,1)} %collective-permute-done.31), channel_id=1, source_target_pairs={{4,8},{6,10},{8,12},{10,14},{5,9},{7,11},{9,13},{11,15},{20,24},{2... | collective-permute-start | bytes 1572872 | tf_op jit(solution)/shard_map/ppermute | solution.py:153
  144.8 22.0 %collective-permute-start.34 = (bf16[256,1024]{1,0:T(8,128)(2,1)}, bf16[256,1024]{1,0:T(8,128)(2,1)}, u32[]{:S(2)}, u32[]{:S(2)}) collective-permute-start(bf16[256,1024]{1,0:T(8,128)(2,1)} %collective-permute-done.30), channel_id=1, source_target_pairs={{4,0},{6,2},{8,4},{10,6},{5,1},{7,3},{9,5},{11,7},{20,16},{22,18},... | collective-permute-start | bytes 1572872 | tf_op jit(solution)/shard_map/ppermute | solution.py:154
  146.1 20.7 %collective-permute-start.33 = (bf16[256,1024]{1,0:T(8,128)(2,1)}, bf16[256,1024]{1,0:T(8,128)(2,1)}, u32[]{:S(2)}, u32[]{:S(2)}) collective-permute-start(bf16[256,1024]{1,0:T(8,128)(2,1)} %collective-permute-done.32), channel_id=1, source_target_pairs={{8,12},{10,14},{9,13},{11,15},{24,28},{26,30},{25,29},{27,31}} | collective-permute-start | bytes 1572872 | tf_op jit(solution)/shard_map/ppermute | solution.py:153
  154.2 96.1 %collective-permute-start.6 = (bf16[2048,1024]{1,0:T(8,128)(2,1)}, bf16[2048,1024]{1,0:T(8,128)(2,1)}, u32[]{:S(2)}, u32[]{:S(2)}) collective-permute-start(bf16[2048,1024]{1,0:T(8,128)(2,1)} %pad_maximum_fusion.1), channel_id=1, source_target_pairs={{0,1},{1,0},{2,3},{3,2},{4,5},{5,4},{6,7},{7,6},{8,9},{9,8},{10,11... | collective-permute-start | bytes 12582920 | tf_op jit(solution)/shard_map/ppermute | solution.py:101
  166.7 62.0 %collective-permute-start.11 = (bf16[2048,1024]{1,0:T(8,128)(2,1)}, bf16[2048,1024]{1,0:T(8,128)(2,1)}, u32[]{:S(2)}, u32[]{:S(2)}) collective-permute-start(bf16[2048,1024]{1,0:T(8,128)(2,1)} %pad_maximum_fusion.2), channel_id=1, source_target_pairs={{0,1},{1,0},{2,3},{3,2},{4,5},{5,4},{6,7},{7,6},{8,9},{9,8},{10,11... | collective-permute-start | bytes 12582920 | tf_op jit(solution)/shard_map/ppermute | solution.py:102
  172.1 43.3 %collective-permute-start.27 = (bf16[512,1024]{1,0:T(8,128)(2,1)}, bf16[512,1024]{1,0:T(8,128)(2,1)}, u32[]{:S(2)}, u32[]{:S(2)}) collective-permute-start(bf16[512,1024]{1,0:T(8,128)(2,1)} %bitcast.14), channel_id=1, source_target_pairs={{0,1},{1,0},{2,3},{3,2},{4,5},{5,4},{6,7},{7,6},{8,9},{9,8},{10,11... | collective-permute-start | bytes 3145736 | tf_op jit(solution)/shard_map/ppermute | solution.py:115
  238.0 23.7 %collective-permute-start.29 = (bf16[256,1024]{1,0:T(8,128)(2,1)S(1)}, bf16[256,1024]{1,0:T(8,128)(2,1)S(1)}, u32[]{:S(2)}, u32[]{:S(2)}) collective-permute-start(bf16[256,1024]{1,0:T(8,128)(2,1)S(1)} %convolution_convert_fusion.1), channel_id=1, source_target_pairs={{0,2},{2,0},{4,6},{6,4},{8,10},{10,8},{12,14},{14,12},{1,3},{3,1},... | collective-permute-start | bytes 1572872 | tf_op jit(solution)/shard_map/ppermute | solution.py:162
  244.1 28.1 %collective-permute-start.28 = (bf16[256,1024]{1,0:T(8,128)(2,1)S(1)}, bf16[256,1024]{1,0:T(8,128)(2,1)S(1)}, u32[]{:S(2)}, u32[]{:S(2)}) collective-permute-start(bf16[256,1024]{1,0:T(8,128)(2,1)S(1)} %convolution_convert_fusion.2), channel_id=1, source_target_pairs={{0,2},{2,0},{4,6},{6,4},{8,10},{10,8},{12,14},{14,12},{1,3},{3,1},... | collective-permute-start | bytes 1572872 | tf_op jit(solution)/shard_map/ppermute | solution.py:162
  248.3 29.5 %collective-permute-start.12 = (bf16[256,1024]{1,0:T(8,128)(2,1)S(1)}, bf16[256,1024]{1,0:T(8,128)(2,1)S(1)}, u32[]{:S(2)}, u32[]{:S(2)}) collective-permute-start(bf16[256,1024]{1,0:T(8,128)(2,1)S(1)} %convolution_convert_fusion.3), channel_id=1, source_target_pairs={{0,2},{2,0},{4,6},{6,4},{8,10},{10,8},{12,14},{14,12},{1,3},{3,1},... | collective-permute-start | bytes 1572872 | tf_op jit(solution)/shard_map/ppermute | solution.py:162
  (36 other events, 587.0 us)

commit v2 on v1

v2 whole, which is shorter than its diff:
```python
import jax
import jax.numpy as jnp
from jax import lax
from jax.experimental import pallas as pl
from jax.experimental.pallas import tpu as pltpu
from jax.sharding import PartitionSpec as P

ADAPTER_RANK = 16
ROW_CHUNKS = (640, 384)
ROW_STEP = 128
SOURCES = 6
VMEM_BYTES = 56 * 1024 * 1024


def general_body(
    tokens, query_weight, shrink_factors, expand_factors, row_adapter_index, adapter_storage_block
):
    holder_count = lax.axis_size("tp")
    own_index = lax.axis_index("tp")
    rows_per_holder = shrink_factors.shape[1] // ADAPTER_RANK
    row_count = tokens.shape[0]
    capacity = 2 * row_count // holder_count
    full_rows = lax.all_gather(tokens, "tp", axis=1, tiled=True)
    weight = lax.all_gather(query_weight, "dp", axis=0, tiled=True)
    base_output = jnp.dot(full_rows, weight, preferred_element_type=jnp.float32)
    storage_weights = jnp.take(adapter_storage_block, row_adapter_index[:, 0])
    owner_of = storage_weights // rows_per_holder
    local_of = storage_weights % rows_per_holder
    onehot = (owner_of[:, None] == jnp.arange(holder_count)[None, :]).astype(jnp.int32)
    rank_in_owner = jnp.sum(jnp.cumsum(onehot, axis=0) * onehot, axis=1) - 1
    select = (owner_of[None, :] == own_index) & (
        rank_in_owner[None, :] == jnp.arange(capacity)[:, None]
    )
    selected_rows = jnp.dot(
        select.astype(jnp.bfloat16), full_rows, preferred_element_type=jnp.float32
    ).astype(jnp.bfloat16)
    picked_local = jnp.sum(select.astype(jnp.int32) * local_of[None, :], axis=1)
    reduced_rows = jnp.dot(selected_rows, shrink_factors, preferred_element_type=jnp.float32)
    column_block = jnp.arange(rows_per_holder * ADAPTER_RANK) // ADAPTER_RANK
    keep_mask = column_block[None, :] == picked_local[:, None]
    masked = jnp.where(keep_mask, reduced_rows, 0.0)
    compact = jnp.sum(masked.reshape(capacity, rows_per_holder, ADAPTER_RANK), axis=1)
    spread = jnp.dot(select.T.astype(jnp.float32), compact, precision=lax.Precision.HIGHEST)
    shrink_all = lax.psum(spread, "tp").astype(jnp.bfloat16)
    columns = lax.all_to_all(
        expand_factors.reshape(rows_per_holder * ADAPTER_RANK, holder_count, -1),
        "tp",
        split_axis=1,
        concat_axis=0,
        tiled=True,
    )
    columns = columns.reshape(holder_count * rows_per_holder, ADAPTER_RANK, -1)
    factor_rows = jnp.take(columns, storage_weights, axis=0)
    adapter_output = jnp.einsum(
        "tr,trc->tc", shrink_all, factor_rows, preferred_element_type=jnp.float32
    ).astype(jnp.bfloat16)
    adapter_output = lax.optimization_barrier(adapter_output)
    return (base_output + adapter_output.astype(jnp.float32)).astype(jnp.bfloat16)


def dot(a, b):
    return jnp.dot(a, b, preferred_element_type=jnp.float32)


def pick(a, j):
    return lax.dynamic_index_in_dim(a, j, 0, keepdims=False)


def early_kernel(sel, place, *refs):
    sources, refs = refs[: SOURCES - 1], refs[SOURCES - 1 :]
    pieces, refs = refs[:4], refs[4:]
    factors, (total, line, weight, sems) = refs[:3], refs[3:]
    depth, width = pieces[0].shape
    columns, half = factors[0].shape[1], factors[1].shape[0]
    steps = sel.shape[0]

    def arrive(j, source, piece, tail):
        own_rows = pl.ds(pl.multiple_of(place[j] * depth, depth), depth)
        tail_rows = pl.ds(pl.multiple_of(lax.rem(place[j], 2) * depth, depth), depth)
        return [
            pltpu.make_async_copy(source, line.at[j], sems.at[j, 0]),
            pltpu.make_async_copy(piece, weight.at[j, :, pl.ds(0, width)], sems.at[j, 1]),
            pltpu.make_async_copy(
                factors[0].at[own_rows], weight.at[j, :, pl.ds(width, columns)], sems.at[j, 2]
            ),
            pltpu.make_async_copy(
                tail.at[tail_rows], weight.at[j, :, pl.ds(width + columns, columns)], sems.at[j, 3]
            ),
        ]

    for j in range(steps):
        for number, source in enumerate(sources):

            @pl.when(sel[j] == number)
            def _():
                arrive(j, source, pieces[0], factors[1])[0].start()

        for number, piece in enumerate(pieces):

            @pl.when((place[j] == number) & (sel[j] < SOURCES - 1))
            def _():
                for copy in arrive(j, sources[0], piece, factors[1 + number // 2])[1:]:
                    copy.start()

    for j in range(steps):

        @pl.when(sel[j] < SOURCES - 1)
        def _():
            for copy in arrive(j, sources[0], pieces[0], factors[1]):
                copy.wait()
            term = dot(line[j], weight[j])
            if j == 0:
                total[...] = term
            else:
                total[...] += term


def rest_kernel(farthest, total, block, *refs):
    pieces, refs = refs[:4], refs[4:]
    factors, refs = refs[:3], refs[3:]
    stored, adapter, fold, partial, shrunk, weight, sems = refs
    depth, width = pieces[0].shape
    columns = factors[0].shape[1]
    own_rows = pl.ds(pl.multiple_of(farthest[0] * depth, depth), depth)
    tail_rows = pl.ds(pl.multiple_of(lax.rem(farthest[0], 2) * depth, depth), depth)

    def arrive(piece, tail):
        return [
            pltpu.make_async_copy(piece, weight.at[:, pl.ds(0, width)], sems.at[0]),
            pltpu.make_async_copy(
                factors[0].at[own_rows], weight.at[:, pl.ds(width, columns)], sems.at[1]
            ),
            pltpu.make_async_copy(
                tail.at[tail_rows], weight.at[:, pl.ds(width + columns, columns)], sems.at[2]
            ),
        ]

    for number, piece in enumerate(pieces):

        @pl.when(farthest[0] == number)
        def _():
            for copy in arrive(piece, factors[1 + number // 2]):
                copy.start()

    for copy in arrive(pieces[0], factors[1]):
        copy.wait()
    full = total[...] + dot(block[...], weight[...])
    partial[...] = full[:, :width].astype(partial.dtype)
    kept = jnp.where(stored[...] == adapter[...], full[:, width:], 0.0).astype(jnp.bfloat16)
    across = (((1,), (1,)), ((), ()))
    shrunk[...] = lax.dot_general(
        fold[...], kept, across, preferred_element_type=jnp.float32
    ).astype(shrunk.dtype)


def own_kernel(sel, place, *refs):
    sources, refs = refs[: SOURCES - 1], refs[SOURCES - 1 :]
    halves, (base, line, weight, sems) = refs[:2], refs[2:]
    depth = sources[0].shape[1]
    steps = sel.shape[0]

    def copies(j, source, half):
        rows = pl.ds(pl.multiple_of(lax.rem(place[j], 2) * depth, depth), depth)
        return [
            pltpu.make_async_copy(source, line.at[j], sems.at[j, 0]),
            pltpu.make_async_copy(half.at[rows], weight.at[j], sems.at[j, 1]),
        ]

    for j in range(steps):
        for number, source in enumerate(sources):

            @pl.when(sel[j] == number)
            def _():
                copies(j, source, halves[0])[0].start()

        for number, half in enumerate(halves):

            @pl.when((place[j] // 2 == number) & (sel[j] < SOURCES - 1))
            def _():
                copies(j, sources[0], half)[1].start()

    for j in range(steps):

        @pl.when(sel[j] < SOURCES - 1)
        def _():
            for copy in copies(j, sources[0], halves[0]):
                copy.wait()
            term = dot(line[j], weight[j])
            if j == 0:
                base[...] = term
            else:
                base[...] += term


def lora_kernel(farthest, base, everyone, stored, adapter, unfold, *refs):
    expand, block, weights, refs = refs[:2], refs[2], refs[3:5], refs[5:]
    partials, (out, weight, sem) = refs[:-3], refs[-3:]
    depth = weight.shape[0]
    rows = pl.ds(pl.multiple_of(farthest[0] * depth, depth), depth)
    for number, half in enumerate(weights):

        @pl.when(farthest[1] == number)
        def _():
            pltpu.make_async_copy(half.at[rows], weight, sem).start()

    shrunk = jnp.sum(everyone[...].astype(jnp.float32), axis=0).astype(jnp.bfloat16)
    spread = lax.dot_general(
        shrunk, unfold[...], (((0,), (0,)), ((), ())), preferred_element_type=jnp.float32
    )
    spread = jnp.where(stored[...] == adapter[...], spread, 0.0).astype(jnp.bfloat16)
    half = spread.shape[1] // 2
    added = dot(spread[:, :half], expand[0][...]) + dot(spread[:, half:], expand[1][...])
    pltpu.make_async_copy(weights[0].at[rows], weight, sem).wait()
    added = base[...] + added + dot(block[...], weight[...])
    for partial in partials:
        added += partial[...].astype(jnp.float32)
    out[...] = added.astype(out.dtype)


def sum_kernel(base, partial, *refs):
    refs[-1][...] = (base[...] + partial[...].astype(jnp.float32)).astype(jnp.bfloat16)


def whole(shape):
    return pl.BlockSpec(shape, lambda n, *_: (0,) * len(shape))


def on_line(kernel, scalars, sources, weights, small, outs, scratch):
    rows, depth = sources[0].shape
    planes = scalars[0].shape[0]
    width = weights[0].shape[-1]
    flops = 2 * rows * planes * depth * width
    size = 2 * planes * depth * width + 2 * rows * planes * depth + 4 * rows * width
    return pl.pallas_call(
        kernel,
        grid_spec=pltpu.PrefetchScalarGridSpec(
            num_scalar_prefetch=2,
            grid=(1,),
            in_specs=[pl.BlockSpec(memory_space=pl.ANY) for _ in sources + weights]
            + [whole(v.shape) for v in small],
            out_specs=[whole(o.shape) for o in outs],
            scratch_shapes=scratch + [pltpu.SemaphoreType.DMA((planes, 4))],
        ),
        out_shape=outs,
        compiler_params=pltpu.CompilerParams(vmem_limit_bytes=VMEM_BYTES),
        cost_estimate=pl.CostEstimate(flops=flops, bytes_accessed=size, transcendentals=0),
    )(*scalars, *sources, *weights, *small)


def after(value, *events):
    return lax.optimization_barrier((value,) + events)[0]


def line_body(
    tokens, query_weight, shrink_factors, expand_factors, row_adapter_index, adapter_storage_block
):
    tp = lax.axis_size("tp")
    planes = tp // 2
    own = lax.axis_index("tp")
    z, x = own // 2, own % 2
    r, d = lax.axis_index("rep"), lax.axis_index("dp")
    rows, depth = tokens.shape
    width = query_weight.shape[1]
    holder_columns = shrink_factors.shape[1]
    holder_adapters = holder_columns // ADAPTER_RANK
    half = holder_columns // 2
    across = [(i, i ^ 1) for i in range(tp)]
    swap = [(0, 1), (1, 0)]

    def up(h):
        return [(i, i + 2) for i in range(2 * (h - 1), tp - 2)]

    def down(h):
        return [(i + 2, i) for i in range(0, tp - 2 * h)]

    def place(plane):
        return 2 * ((plane // 2) ^ d) + ((plane % 2) ^ r)

    def plane_at(p):
        return 2 * ((p // 2) ^ d) + ((p % 2) ^ r)

    pieces, starts = [], []
    first = 0
    for count in ROW_CHUNKS:
        starts.append(first)
        pieces.append(tokens[first : first + count])
        first += count
    ups = [{0: p} for p in pieces]
    downs = [{0: p} for p in pieces]

    def hop(c, h):
        if h == planes - 1:
            inner = jnp.where(z == 1, downs[c][h - 1], ups[c][h - 1])
            pairs = [p for p in up(h) + down(h)]
            ups[c][h] = downs[c][h] = lax.ppermute(inner, "tp", pairs)
            return
        ups[c][h] = lax.ppermute(ups[c][h - 1], "tp", up(h))
        downs[c][h] = lax.ppermute(downs[c][h - 1], "tp", down(h))

    def step(values, *events):
        return lax.optimization_barrier((values, events))[0]

    def to_other_core(value):
        return lax.ppermute(value, "dp", swap)

    blocks = query_weight.reshape(planes, depth, width)
    hop(0, 1)
    hop(1, 1)
    near = lax.ppermute(pick(blocks, 2 * r + (1 - x)), "tp", across)

    factors = shrink_factors.reshape(planes, 2, depth, holder_columns)
    leaving = jnp.concatenate([pick(pick(factors, plane_at(p)), 1 - x) for p in range(planes // 2)])
    expand_half = lax.dynamic_slice_in_dim(expand_factors, d * half, half, 0)
    expand_half = expand_half.reshape(half, tp, width).transpose(1, 0, 2)
    (ups[0][1], downs[0][1], ups[1][1], downs[1][1], near, leaving, weights, factors, expand_half) = step(
        (ups[0][1], downs[0][1], ups[1][1], downs[1][1], near, leaving, query_weight, factors, expand_half)
    )
    hop(0, 2)
    far = lax.ppermute(near, "rep", swap)
    shrink_near = lax.ppermute(leaving, "tp", across)
    near_crossed = to_other_core(near)
    pairs = weights.reshape(planes // 2, 2, depth, width)
    own_half = lax.dynamic_index_in_dim(pairs, x, 1, keepdims=False).reshape(-1, width)
    shrink_own = jnp.concatenate([pick(pick(factors, plane_at(p)), x) for p in range(planes)])
    expand_half = lax.all_to_all(expand_half, "tp", split_axis=0, concat_axis=0, tiled=True)
    expand_half = expand_half.reshape(tp * half, width)

    (ups[0][2], downs[0][2], ups[1][1], downs[1][1], shrink_near, far, near_crossed, expand_half, own_half) = step(
        (ups[0][2], downs[0][2], ups[1][1], downs[1][1], shrink_near, far, near_crossed, expand_half, own_half)
    )
    hop(0, 3)
    shrink = [shrink_own, shrink_near, to_other_core(shrink_near)]
    weight_other = [near, far, near_crossed, to_other_core(far)]
    weight_own = [own_half, to_other_core(own_half)]

    known = jnp.arange(adapter_storage_block.shape[0])
    stored = jnp.sum(
        jnp.where(row_adapter_index == known[None, :], adapter_storage_block[None, :], 0),
        axis=1,
        keepdims=True,
    )
    column = jnp.arange(2 * holder_columns)
    column_adapter = (own ^ (column // holder_columns)) * holder_adapters + (
        column % holder_columns
    ) // ADAPTER_RANK
    column_adapter = column_adapter[None, :].astype(jnp.int32)
    fold = (jnp.arange(ADAPTER_RANK)[:, None] == column[None, :] % ADAPTER_RANK).astype(jnp.bfloat16)
    entry = jnp.arange(tp * holder_columns)
    within = entry % (tp * half)
    entry_adapter = (within // half) * holder_adapters + (
        ((entry // (tp * half)) ^ d) * half + within % half
    ) // ADAPTER_RANK
    entry_adapter = entry_adapter[None, :].astype(jnp.int32)
    unfold = (jnp.arange(ADAPTER_RANK)[:, None] == entry[None, :] % ADAPTER_RANK).astype(jnp.bfloat16)

    steps = jnp.arange(planes)
    above = z + steps < planes
    hops = jnp.where(above, steps, planes - steps)
    sel = jnp.where(
        steps == 0, 0, jnp.where(hops == planes - 1, SOURCES - 1, hops + jnp.where(above, planes - 2, 0))
    ).astype(jnp.int32)
    plane = (z + steps) % planes
    places_other = place(plane).astype(jnp.int32)
    places_own = (2 * ((plane // 2) ^ d) + plane % 2).astype(jnp.int32)
    distant = jnp.where(z == 0, planes - 1, 0)
    farthest_other = place(distant).astype(jnp.int32)[None]
    farthest_own = jnp.stack([distant % 2, (distant // 2) ^ d]).astype(jnp.int32)

    def sources(c):
        between = range(1, planes - 1)
        return [pieces[c]] + [ups[c][h] for h in between] + [downs[c][h] for h in between] + [
            ups[c].get(planes - 1)
        ]

    total_columns = width + 2 * holder_columns

    def early_part(c, *events):
        count = ROW_CHUNKS[c]
        return on_line(
            early_kernel,
            [after(sel, *events) if events else sel, places_other],
            sources(c)[:-1],
            weight_other + shrink,
            [],
            [jax.ShapeDtypeStruct((count, total_columns), jnp.float32)],
            [
                pltpu.VMEM((planes, count, depth), jnp.bfloat16),
                pltpu.VMEM((planes, depth, total_columns), jnp.bfloat16),
            ],
        )[0]

    def rest_part(c, total):
        count = ROW_CHUNKS[c]
        small = [stored[starts[c] : starts[c] + count], column_adapter, fold]
        outs = [
            jax.ShapeDtypeStruct((count, width), jnp.bfloat16),
            jax.ShapeDtypeStruct((ADAPTER_RANK, count), jnp.bfloat16),
        ]
        return pl.pallas_call(
            rest_kernel,
            grid_spec=pltpu.PrefetchScalarGridSpec(
                num_scalar_prefetch=1,
                grid=(1,),
                in_specs=[whole(total.shape), whole((count, depth))]
                + [pl.BlockSpec(memory_space=pl.ANY) for _ in range(7)]
                + [whole(v.shape) for v in small],
                out_specs=[whole(o.shape) for o in outs],
                scratch_shapes=[
                    pltpu.VMEM((depth, total_columns), jnp.bfloat16),
                    pltpu.SemaphoreType.DMA((3,)),
                ],
            ),
            out_shape=outs,
            compiler_params=pltpu.CompilerParams(vmem_limit_bytes=VMEM_BYTES),
            cost_estimate=pl.CostEstimate(
                flops=2 * count * depth * total_columns, bytes_accessed=4 * depth * width, transcendentals=0
            ),
        )(farthest_other, total, ups[c][planes - 1], *weight_other, *shrink, *small)

    def own_part(c, *events):
        count = ROW_CHUNKS[c]
        return on_line(
            own_kernel,
            [after(sel, *events) if events else sel, places_own],
            sources(c)[:-1],
            weight_own,
            [],
            [jax.ShapeDtypeStruct((count, width), jnp.float32)],
            [
                pltpu.VMEM((planes, count, depth), jnp.bfloat16),
                pltpu.VMEM((planes, depth, width), jnp.bfloat16),
            ],
        )[0]

    def spread_out(shrunk):
        everyone = jnp.broadcast_to(shrunk[None], (tp,) + shrunk.shape)
        return lax.all_to_all(everyone, "tp", split_axis=0, concat_axis=0, tiled=True)

    def lora_part(c, base, everyone, expand, partial=None):
        count = ROW_CHUNKS[c]
        rows_of = whole((count, width))
        partials = [] if partial is None else [partial]
        out = (count, width, jnp.float32) if partial is None else (rows, width, jnp.bfloat16)
        return pl.pallas_call(
            lora_kernel,
            grid_spec=pltpu.PrefetchScalarGridSpec(
                num_scalar_prefetch=1,
                grid=(1,),
                in_specs=[
                    rows_of,
                    whole(everyone.shape),
                    whole((count, 1)),
                    whole(entry_adapter.shape),
                    whole(unfold.shape),
                    whole(expand[0].shape),
                    whole(expand[1].shape),
                    whole((count, depth)),
                ]
                + [pl.BlockSpec(memory_space=pl.ANY)] * 2
                + [rows_of for _ in partials],
                out_specs=rows_of,
                scratch_shapes=[pltpu.VMEM((depth, width), jnp.bfloat16), pltpu.SemaphoreType.DMA],
            ),
            out_shape=jax.ShapeDtypeStruct(out[:2], out[2]),
            compiler_params=pltpu.CompilerParams(vmem_limit_bytes=VMEM_BYTES),
            cost_estimate=pl.CostEstimate(
                flops=4 * count * width * depth, bytes_accessed=4 * depth * width, transcendentals=0
            ),
        )(
            farthest_own,
            base,
            everyone,
            stored[starts[c] : starts[c] + count],
            entry_adapter,
            unfold,
            *expand,
            ups[c][planes - 1],
            *weight_own,
            *partials,
        )

    def sum_part(c, base, partial, earlier):
        count, step = ROW_CHUNKS[c], ROW_STEP
        here = starts[c] // step
        rows_of = pl.BlockSpec((step, width), lambda i: (i, 0))
        operands = [base, partial, earlier]
        specs = [rows_of, rows_of, pl.BlockSpec(memory_space=pl.ANY)]
        aliases = {2: 0}
        return pl.pallas_call(
            sum_kernel,
            grid=(count // step,),
            in_specs=specs,
            out_specs=pl.BlockSpec((step, width), lambda i: (i + here, 0)),
            out_shape=jax.ShapeDtypeStruct((rows, width), jnp.bfloat16),
            input_output_aliases=aliases,
            compiler_params=pltpu.CompilerParams(vmem_limit_bytes=VMEM_BYTES),
            cost_estimate=pl.CostEstimate(
                flops=2 * count * width, bytes_accessed=8 * count * width, transcendentals=0
            ),
        )(*operands)

    early_a = early_part(0)
    base_a = own_part(0, early_a)
    (ups[0][3], ups[1][1], downs[1][1], expand_half) = step(
        (ups[0][3], ups[1][1], downs[1][1], expand_half), base_a
    )
    hop(1, 2)
    expand = [expand_half, to_other_core(expand_half)]
    partial_a, shrunk_a = rest_part(0, early_a)
    got_a = lax.ppermute(partial_a, "tp", across)
    ups[1][2], downs[1][2] = step((ups[1][2], downs[1][2]), partial_a)
    hop(1, 3)
    everyone_a = spread_out(shrunk_a)
    early_c = early_part(1)
    base_c = own_part(1, early_c, everyone_a)
    ups[1][3] = step(ups[1][3], base_c, got_a)
    partial_c, shrunk_c = rest_part(1, early_c)
    got_c = lax.ppermute(partial_c, "tp", across)
    everyone_c = spread_out(shrunk_c)
    out = lora_part(0, base_a, everyone_a, expand, got_a)
    whole_c = lora_part(1, base_c, everyone_c, expand)
    return sum_part(1, whole_c, got_c, out)


def solution(mesh):
    placed = (
        P(("rep", "dp"), "tp"),
        P("dp", "tp"),
        P(None, ("rep", "tp")),
        P(("rep", "tp"), None),
        P(("rep", "dp"), None),
        P("rep"),
    )
    lined = dict(mesh.shape) == {"rep": 2, "tp": 8, "dp": 2}
    return jax.shard_map(
        line_body if lined else general_body,
        mesh=mesh,
        in_specs=placed,
        out_specs=P(("rep", "dp"), "tp"),
        check_vma=False,
    )
```

time: 286 us -> 250 us (0.87)
  Pallas kernels: 0 us -> 64.8 us
  matrix products: 55.1 us -> 0 us
  starting transfers between devices: 88.1 us -> 42.2 us
  waiting for transfers between devices: 76.6 us -> 112 us
  other arithmetic: 28.7 us -> 9.14 us
  local copies, waits for them, and re-layouts: 35.3 us -> 21.4 us
    pallas_call x0 -> x9, Pallas kernels: none -> 64.8 us  [the longest x4 33.6 us: on_line(): pl.pallas_call(kernel, grid_spec=pltpu.PrefetchScalarGridSpec(num_scalar_...]
    dot_general x17 -> x0, matrix products: 55.1 us -> none  [dot(): return jnp.dot(a, b, preferred_element_type=jnp.float32)]
    ppermute x36 -> x19, starting transfers between devices: 69.9 us -> 27.4 us  [the longest x4 12.5 us: hop(): ups[c][h] = lax.ppermute(ups[c][h - 1], 'tp', up(h))]
    dynamic_update_slice x12 -> x0, other arithmetic: 19.6 us -> none  [line_body(): lax.dynamic_update_slice(line, block, (0, place((z + j) % planes) * depth))]
    ppermute x1, waiting for transfers between devices: 1.62 us -> 16.1 us  [line_body(): shrink_near = lax.ppermute(leaving, 'tp', across)]
    ppermute x36 -> x19, waiting for transfers between devices: 71.9 us -> 84.5 us  [the longest x4 37.4 us: hop(): downs[c][h] = lax.ppermute(downs[c][h - 1], 'tp', down(h))]
    all_to_all x2, waiting for transfers between devices: 3.07 us -> 11 us  [spread_out(): lax.all_to_all(everyone, 'tp', split_axis=0, concat_axis=0, tiled=True)]
    concatenate x4 -> x1, other arithmetic: 8.04 us -> 1.08 us  [line_body(): jnp.concatenate([pick(pick(factors, plane_at(p)), x) for p in range(plane...]
  transfers between devices with their start and end apart: 40 -> 23, of which waited for: 14 -> 10; matrix products, arithmetic and copies ran while one was open for 38% -> 10% of each run, Pallas kernels for 0% -> 25%
where the time goes in v2:
time: 250 us; the launch traced here: 249 us
  waiting for transfers between devices  112 us (45%)
  Pallas kernels  64.8 us (26%)
  starting transfers between devices  42.2 us (17%)
  local copies, waits for them, and re-layouts  21.4 us (9%)
  other arithmetic  9.14 us (4%)
    ppermute x4, waiting for transfers between devices, hop(): downs[c][h] = lax.ppermute(downs[c][h - 1], 'tp', down(h))  37.4 us
    pallas_call x4, Pallas kernels, on_line(): pl.pallas_call(kernel, grid_spec=pltpu.PrefetchScalarGridSpec(num_scalar_...  33.6 us
    ppermute x4, waiting for transfers between devices, hop(): ups[c][h] = lax.ppermute(ups[c][h - 1], 'tp', up(h))  30.8 us
    ppermute x1, waiting for transfers between devices, line_body(): shrink_near = lax.ppermute(leaving, 'tp', across)  16.1 us
    pallas_call x2, Pallas kernels, lora_part(): pl.pallas_call(lora_kernel, grid_spec=pltpu.PrefetchScalarGridSpec(num_sc...  15.4 us
    ppermute x2, waiting for transfers between devices, hop(): ups[c][h] = downs[c][h] = lax.ppermute(inner, 'tp', pairs)  13 us
    ppermute x4, starting transfers between devices, hop(): ups[c][h] = lax.ppermute(ups[c][h - 1], 'tp', up(h))  12.5 us
    pallas_call x2, Pallas kernels, rest_part(): pl.pallas_call(rest_kernel, grid_spec=pltpu.PrefetchScalarGridSpec(num_sc...  12.5 us
  transfers between devices with their start and end apart: 23, of which 10 were waited for; matrix products, arithmetic and copies ran while one was open for 10% of the time, Pallas kernels for 25%

profile of v2, /device:TPU:0, one launch (start us, length us, event | category | flops | bytes accessed | tf_op | source)
XLA Modules:
  0.0 249.5 jit_solution(783229252126029871)
XLA Ops:
  0.0 3.2 %dynamic-slice_bitcast_fusion = bf16[1024,1024]{1,0:T(8,128)(2,1)} fusion(bf16[4,1024,1024]{2,1,0:T(8,128)(2,1)} %bitcast.38, s32[]{:T(128)S(6)} %select_n.261), kind=kLoop, calls=%fused_computation | loop fusion | bytes 4194308 | tf_op jit(solution)/shard_map/jit(dynamic_index_in_dim)/squeeze | solution.py:66
  7.4 4.5 %collective-permute-start = (bf16[640,1024]{1,0:T(8,128)(2,1)}, bf16[640,1024]{1,0:T(8,128)(2,1)}, u32[]{:S(2)}, u32[]{:S(2)}) collective-permute-start(bf16[640,1024]{1,0:T(8,128)(2,1)} %slice.21.refs_0_), channel_id=1, source_target_pairs={{0,4},{2,6},{4,8},{6,10},{8,12},{10,14},{1,5},{3,7},{5,9},{7,11},{... | collective-permute-start | bytes 3932168 | tf_op jit(solution)/shard_map/ppermute | solution.py:297
  13.3 5.4 %collective-permute-start.2 = (bf16[384,1024]{1,0:T(8,128)(2,1)S(1)}, bf16[384,1024]{1,0:T(8,128)(2,1)}, u32[]{:S(2)}, u32[]{:S(2)}) collective-permute-start(bf16[384,1024]{1,0:T(8,128)(2,1)S(1)} %slice.20.refs_0_), channel_id=1, source_target_pairs={{0,4},{2,6},{4,8},{6,10},{8,12},{10,14},{1,5},{3,7},{5,9},{7,11},{... | collective-permute-start | bytes 2359304 | tf_op jit(solution)/shard_map/ppermute | solution.py:297
  24.8 30.8 %collective-permute-done.2.refs_1_ = bf16[384,1024]{1,0:T(8,128)(2,1)} collective-permute-done((bf16[384,1024]{1,0:T(8,128)(2,1)S(1)}, bf16[384,1024]{1,0:T(8,128)(2,1)}, u32[]{:S(2)}, u32[]{:S(2)}) %collective-permute-start.2) | collective-permute-done | bytes 786464 | tf_op jit(solution)/shard_map/ppermute | solution.py:297
  55.7 5.3 %collective-permute-done.3.refs_3_ = bf16[384,1024]{1,0:T(8,128)(2,1)} collective-permute-done((bf16[384,1024]{1,0:T(8,128)(2,1)S(1)}, bf16[384,1024]{1,0:T(8,128)(2,1)}, u32[]{:S(2)}, u32[]{:S(2)}) %collective-permute-start.3) | collective-permute-done | bytes 786464 | tf_op jit(solution)/shard_map/ppermute | solution.py:298
  64.1 3.6 %all-to-all-start = ((bf16[8,64,1024]{2,1,0:T(8,128)(2,1)}), bf16[8,64,1024]{2,1,0:T(8,128)(2,1)S(1)}, u32[]{:S(2)}, u32[]{:S(2)}) async-start(bf16[8,64,1024]{2,1,0:T(8,128)(2,1)} %copy.21), calls=%async_computation | async-start | bytes 2097152 | tf_op jit(solution)/shard_map/all_to_all | solution.py:325
  72.7 4.6 %constant_dynamic-slice_fusion = bf16[2,1,1024,1024]{3,2,1,0:T(8,128)(2,1)} fusion(bf16[2,2,1024,1024]{3,2,1,0:T(8,128)(2,1)} %bitcast.39, s32[]{:T(128)S(6)} %select_n.269), kind=kLoop, calls=%fused_computation.42 | loop fusion | bytes 8388612 | tf_op jit(solution)/shard_map/jit(dynamic_index_in_dim)/dynamic_slice | solution.py:323
  77.4 16.1 %collective-permute-done.7.refs_10_.refs_5_ = bf16[2048,128]{1,0:T(8,128)(2,1)} collective-permute-done((bf16[2048,128]{1,0:T(8,128)(2,1)}, bf16[2048,128]{1,0:T(8,128)(2,1)}, u32[]{:S(2)}, u32[]{:S(2)}) %collective-permute-start.7) | collective-permute-done | bytes 524320 | tf_op jit(solution)/shard_map/ppermute | solution.py:320
  93.4 22.5 %collective-permute-done.6.refs_4_ = bf16[640,1024]{1,0:T(8,128)(2,1)} collective-permute-done((bf16[640,1024]{1,0:T(8,128)(2,1)}, bf16[640,1024]{1,0:T(8,128)(2,1)}, u32[]{:S(2)}, u32[]{:S(2)}) %collective-permute-start.6) | collective-permute-done | bytes 1310752 | tf_op jit(solution)/shard_map/ppermute | solution.py:298
  126.7 10.1 %shard_map.64.total = f32[640,1280]{1,0:T(8,128)} custom-call(s32[4]{0:T(128)} %get-tuple-element.62.sel, s32[4]{0:T(128)} %get-tuple-element.74.place, bf16[640,1024]{1,0:T(8,128)(2,1)} %slice.21.refs_0_, bf16[640,1024]{1,0:T(8,128)(2,1)} %collective-permute-done.refs_1_, bf16[640,1024]{1,0:T(8,128)(2,1)} %collective-permute-done.5.refs_2_, ...), custom_call_target="tpu_custom_call" | custom-call | flops 5368709120 | bytes 16252928 | tf_op jit(solution)/shard_map/pallas_call | solution.py:234
  136.9 9.1 %shard_map.65.base = f32[640,1024]{1,0:T(8,128)} custom-call(s32[4]{0:T(128)} %get-tuple-element.62.sel, s32[4]{0:T(128)} %fusion.14.place, bf16[640,1024]{1,0:T(8,128)(2,1)} %slice.21.refs_0_, bf16[640,1024]{1,0:T(8,128)(2,1)} %collective-permute-done.refs_1_, bf16[640,1024]{1,0:T(8,128)(2,1)} %collective-permute-done.5.refs_2_, ...), custom_call_target="tpu_custom_call" | custom-call | flops 5368709120 | bytes 16252928 | tf_op jit(solution)/shard_map/pallas_call | solution.py:234
  146.0 13.0 %collective-permute-done.10.block.refs_2_ = bf16[640,1024]{1,0:T(8,128)(2,1)S(1)} collective-permute-done((bf16[640,1024]{1,0:T(8,128)(2,1)S(1)}, bf16[640,1024]{1,0:T(8,128)(2,1)S(1)}, u32[]{:S(2)}, u32[]{:S(2)}) %collective-permute-start.10) | collective-permute-done | bytes 1310752 | tf_op jit(solution)/shard_map/ppermute | solution.py:295
  164.1 7.0 %shard_map.66 = (bf16[640,1024]{1,0:T(8,128)(2,1)}, bf16[16,640]{1,0:T(8,128)(2,1)}) custom-call(s32[1]{0:T(128)} %bitcast.15.farthest, f32[640,1280]{1,0:T(8,128)} %shard_map.64.total, bf16[640,1024]{1,0:T(8,128)(2,1)} %copy-done.8, bf16[1024,1024]{1,0:T(8,128)(2,1)} %collective-permute-done.4.refs_5_.refs_0_, bf16[1024,1024]{1,0:T(8,128)(2,1)} %copy-done.2, ...), custom_call_target="tpu_custom_call" | custom-call | flops 1677721600 | bytes 4194304 | tf_op jit(solution)/shard_map/pallas_call | solution.py:399
  172.7 9.6 %collective-permute-done.15.refs_4_ = bf16[384,1024]{1,0:T(8,128)(2,1)S(1)} collective-permute-done((bf16[384,1024]{1,0:T(8,128)(2,1)}, bf16[384,1024]{1,0:T(8,128)(2,1)S(1)}, u32[]{:S(2)}, u32[]{:S(2)}) %collective-permute-start.15) | collective-permute-done | bytes 786464 | tf_op jit(solution)/shard_map/ppermute | solution.py:298
  186.7 5.7 %all-to-all-start.1 = ((bf16[8,16,640]{2,1,0:T(8,128)(2,1)}), bf16[8,16,640]{2,1,0:T(8,128)(2,1)S(1)}, u32[]{:S(2)}, u32[]{:S(2)}) async-start(bf16[8,16,640]{2,1,0:T(8,128)(2,1)} %broadcast_in_dim.52), calls=%async_computation.1 | async-start | bytes 327680 | tf_op jit(solution)/shard_map/all_to_all | solution.py:437
  192.5 7.6 %shard_map.67.total = f32[384,1280]{1,0:T(8,128)} custom-call(s32[4]{0:T(128)} %get-tuple-element.62.sel, s32[4]{0:T(128)} %get-tuple-element.74.place, bf16[384,1024]{1,0:T(8,128)(2,1)} %copy-done.7, bf16[384,1024]{1,0:T(8,128)(2,1)} %collective-permute-done.2.refs_1_, bf16[384,1024]{1,0:T(8,128)(2,1)} %copy-done.5, ...), custom_call_target="tpu_custom_call" | custom-call | flops 3221225472 | bytes 13107200 | tf_op jit(solution)/shard_map/pallas_call | solution.py:234
  200.1 7.5 %all-to-all-done.1.everyone = bf16[8,16,640]{2,1,0:T(8,128)(2,1)S(1)} async-done(((bf16[8,16,640]{2,1,0:T(8,128)(2,1)}), bf16[8,16,640]{2,1,0:T(8,128)(2,1)S(1)}, u32[]{:S(2)}, u32[]{:S(2)}) %all-to-all-start.1) | async-done | bytes 163872 | tf_op jit(solution)/shard_map/all_to_all | solution.py:437
  207.6 6.8 %shard_map.68.base = f32[384,1024]{1,0:T(8,128)} custom-call(s32[4]{0:T(128)} %get-tuple-element.62.sel, s32[4]{0:T(128)} %fusion.14.place, bf16[384,1024]{1,0:T(8,128)(2,1)} %copy-done.7, bf16[384,1024]{1,0:T(8,128)(2,1)} %collective-permute-done.2.refs_1_, bf16[384,1024]{1,0:T(8,128)(2,1)} %copy-done.5, bf16[384,1024]{1,0:T(8,128)(2,1)} %collective-permute-done.3.refs_3_, ...), custom_call_target="tpu_custom_call" | custom-call | flops 3221225472 | bytes 13107200 | tf_op jit(solution)/shard_map/pallas_call | solution.py:234
  214.4 5.5 %shard_map.69 = (bf16[384,1024]{1,0:T(8,128)(2,1)}, bf16[16,384]{1,0:T(8,128)(2,1)}) custom-call(s32[1]{0:T(128)} %bitcast.15.farthest, f32[384,1280]{1,0:T(8,128)} %shard_map.67.total, bf16[384,1024]{1,0:T(8,128)(2,1)} %collective-permute-done.16.block.refs_2_, bf16[1024,1024]{1,0:T(8,128)(2,1)} %collective-permute-done.4.refs_5_.refs_0_, ...), custom_call_target="tpu_custom_call" | custom-call | flops 1006632960 | bytes 4194304 | tf_op jit(solution)/shard_map/pallas_call | solution.py:399
  223.0 3.6 %all-to-all-start.2 = ((bf16[8,16,384]{2,1,0:T(8,128)(2,1)}), bf16[8,16,384]{2,1,0:T(8,128)(2,1)S(1)}, u32[]{:S(2)}, u32[]{:S(2)}) async-start(bf16[8,16,384]{2,1,0:T(8,128)(2,1)} %broadcast_in_dim.53), calls=%async_computation.2 | async-start | bytes 196608 | tf_op jit(solution)/shard_map/all_to_all | solution.py:437
  226.6 8.5 %shard_map.71.refs_0_ = bf16[1024,1024]{1,0:T(8,128)(2,1)} custom-call(s32[2]{0:T(128)} %pad_add_fusion.farthest, f32[640,1024]{1,0:T(8,128)} %shard_map.65.base, bf16[8,16,640]{2,1,0:T(8,128)(2,1)} %copy-done.10, s32[640,1]{1,0:T(8,128)} %slice.26.refs_7_.stored, s32[1,1024]{1,0:T(1,128)} %fusion.7.adapter, bf16[16,1024]{1,0:T(8,128)(2,1)} %fusion.unfold, ...), custom_call_target="tpu_custom_call" | custom-call | flops 2684354560 | bytes 4194304 | tf_op jit(solution)/shard_map/pallas_call | solution.py:444
  235.1 3.5 %all-to-all-done.2.everyone = bf16[8,16,384]{2,1,0:T(8,128)(2,1)S(1)} async-done(((bf16[8,16,384]{2,1,0:T(8,128)(2,1)}), bf16[8,16,384]{2,1,0:T(8,128)(2,1)S(1)}, u32[]{:S(2)}, u32[]{:S(2)}) %all-to-all-start.2) | async-done | bytes 98336 | tf_op jit(solution)/shard_map/all_to_all | solution.py:437
  239.3 6.9 %shard_map.70.base = f32[384,1024]{1,0:T(8,128)} custom-call(s32[2]{0:T(128)} %pad_add_fusion.farthest, f32[384,1024]{1,0:T(8,128)} %shard_map.68.base, bf16[8,16,384]{2,1,0:T(8,128)(2,1)} %copy-done.11, s32[384,1]{1,0:T(8,128)} %slice.27.refs_7_.stored, s32[1,1024]{1,0:T(1,128)} %fusion.7.adapter, bf16[16,1024]{1,0:T(8,128)(2,1)} %fusion.unfold, ...), custom_call_target="tpu_custom_call" | custom-call | flops 1610612736 | bytes 4194304 | tf_op jit(solution)/shard_map/pallas_call | solution.py:444
  246.2 3.3 %shard_map.72 = bf16[1024,1024]{1,0:T(8,128)(2,1)} custom-call(f32[384,1024]{1,0:T(8,128)} %shard_map.70.base, bf16[384,1024]{1,0:T(8,128)(2,1)} %collective-permute-done.19.partial, bf16[1024,1024]{1,0:T(8,128)(2,1)} %shard_map.71.refs_0_), custom_call_target="tpu_custom_call", output_to_operand_aliasing={{}: (2, {})} | custom-call | flops 786432 | bytes 3145728 | tf_op jit(solution)/shard_map/pallas_call | solution.py:489
  (89 shorter events, 45.4 us)
Async XLA Ops:
  3.2 57.7 %collective-permute-start.4 = (bf16[1024,1024]{1,0:T(8,128)(2,1)}, bf16[1024,1024]{1,0:T(8,128)(2,1)}, u32[]{:S(2)}, u32[]{:S(2)}) collective-permute-start(bf16[1024,1024]{1,0:T(8,128)(2,1)} %dynamic-slice_bitcast_fusion), channel_id=1, source_target_pairs={{0,2},{2,0},{4,6},{6,4},{8,10},{10,8},{12,14},{14,12},{1,3},{3,1},... | collective-permute-start | bytes 6291464 | tf_op jit(solution)/shard_map/ppermute | solution.py:309
  7.4 53.6 %collective-permute-start = (bf16[640,1024]{1,0:T(8,128)(2,1)}, bf16[640,1024]{1,0:T(8,128)(2,1)}, u32[]{:S(2)}, u32[]{:S(2)}) collective-permute-start(bf16[640,1024]{1,0:T(8,128)(2,1)} %slice.21.refs_0_), channel_id=1, source_target_pairs={{0,4},{2,6},{4,8},{6,10},{8,12},{10,14},{1,5},{3,7},{5,9},{7,11},{... | collective-permute-start | bytes 3932168 | tf_op jit(solution)/shard_map/ppermute | solution.py:297
  11.9 49.0 %collective-permute-start.1 = (bf16[640,1024]{1,0:T(8,128)(2,1)}, bf16[640,1024]{1,0:T(8,128)(2,1)}, u32[]{:S(2)}, u32[]{:S(2)}) collective-permute-start(bf16[640,1024]{1,0:T(8,128)(2,1)} %slice.21.refs_0_), channel_id=1, source_target_pairs={{4,0},{6,2},{8,4},{10,6},{12,8},{14,10},{5,1},{7,3},{9,5},{11,7},{... | collective-permute-start | bytes 3932168 | tf_op jit(solution)/shard_map/ppermute | solution.py:298
  13.3 42.4 %collective-permute-start.2 = (bf16[384,1024]{1,0:T(8,128)(2,1)S(1)}, bf16[384,1024]{1,0:T(8,128)(2,1)}, u32[]{:S(2)}, u32[]{:S(2)}) collective-permute-start(bf16[384,1024]{1,0:T(8,128)(2,1)S(1)} %slice.20.refs_0_), channel_id=1, source_target_pairs={{0,4},{2,6},{4,8},{6,10},{8,12},{10,14},{1,5},{3,7},{5,9},{7,11},{... | collective-permute-start | bytes 2359304 | tf_op jit(solution)/shard_map/ppermute | solution.py:297
  18.7 42.2 %collective-permute-start.3 = (bf16[384,1024]{1,0:T(8,128)(2,1)S(1)}, bf16[384,1024]{1,0:T(8,128)(2,1)}, u32[]{:S(2)}, u32[]{:S(2)}) collective-permute-start(bf16[384,1024]{1,0:T(8,128)(2,1)S(1)} %slice.20.refs_0_), channel_id=1, source_target_pairs={{4,0},{6,2},{8,4},{10,6},{12,8},{14,10},{5,1},{7,3},{9,5},{11,7},{... | collective-permute-start | bytes 2359304 | tf_op jit(solution)/shard_map/ppermute | solution.py:298
  61.0 55.0 %collective-permute-start.8 = (bf16[1024,1024]{1,0:T(8,128)(2,1)}, bf16[1024,1024]{1,0:T(8,128)(2,1)S(1)}, u32[]{:S(2)}, u32[]{:S(2)}) collective-permute-start(bf16[1024,1024]{1,0:T(8,128)(2,1)} %collective-permute-done.4.refs_5_.refs_0_), channel_id=1, source_target_pairs={{0,16},{16,0},{1,17},{17,1},{2,18},{18,2},{3,19},{19,3},{4,20},{20... | collective-permute-start | bytes 6291464 | tf_op jit(solution)/shard_map/ppermute | solution.py:319
  62.5 53.4 %collective-permute-start.9 = (bf16[1024,1024]{1,0:T(8,128)(2,1)}, bf16[1024,1024]{1,0:T(8,128)(2,1)}, u32[]{:S(2)}, u32[]{:S(2)}) collective-permute-start(bf16[1024,1024]{1,0:T(8,128)(2,1)} %collective-permute-done.4.refs_5_.refs_0_), channel_id=1, source_target_pairs={{0,1},{1,0},{2,3},{3,2},{4,5},{5,4},{6,7},{7,6},{8,9},{9,8},{10,11... | collective-permute-start | bytes 6291464 | tf_op jit(solution)/shard_map/ppermute | solution.py:304
  64.1 51.9 %all-to-all-start = ((bf16[8,64,1024]{2,1,0:T(8,128)(2,1)}), bf16[8,64,1024]{2,1,0:T(8,128)(2,1)S(1)}, u32[]{:S(2)}, u32[]{:S(2)}) async-start(bf16[8,64,1024]{2,1,0:T(8,128)(2,1)} %copy.21), calls=%async_computation | async-start | bytes 2097152 | tf_op jit(solution)/shard_map/all_to_all | solution.py:325
  67.7 25.8 %collective-permute-start.5 = (bf16[640,1024]{1,0:T(8,128)(2,1)}, bf16[640,1024]{1,0:T(8,128)(2,1)}, u32[]{:S(2)}, u32[]{:S(2)}) collective-permute-start(bf16[640,1024]{1,0:T(8,128)(2,1)} %collective-permute-done.refs_1_), channel_id=1, source_target_pairs={{4,8},{6,10},{8,12},{10,14},{5,9},{7,11},{9,13},{11,15},{20,24},{2... | collective-permute-start | bytes 3932168 | tf_op jit(solution)/shard_map/ppermute | solution.py:297
  69.5 46.5 %collective-permute-start.6 = (bf16[640,1024]{1,0:T(8,128)(2,1)}, bf16[640,1024]{1,0:T(8,128)(2,1)}, u32[]{:S(2)}, u32[]{:S(2)}) collective-permute-start(bf16[640,1024]{1,0:T(8,128)(2,1)} %collective-permute-done.1.refs_3_), channel_id=1, source_target_pairs={{4,0},{6,2},{8,4},{10,6},{5,1},{7,3},{9,5},{11,7},{20,16},{22,18},... | collective-permute-start | bytes 3932168 | tf_op jit(solution)/shard_map/ppermute | solution.py:298
  70.8 22.7 %collective-permute-start.7 = (bf16[2048,128]{1,0:T(8,128)(2,1)}, bf16[2048,128]{1,0:T(8,128)(2,1)}, u32[]{:S(2)}, u32[]{:S(2)}) collective-permute-start(bf16[2048,128]{1,0:T(8,128)(2,1)} %pad_maximum_fusion.1), channel_id=1, source_target_pairs={{0,2},{2,0},{4,6},{6,4},{8,10},{10,8},{12,14},{14,12},{1,3},{3,1},... | collective-permute-start | bytes 1572872 | tf_op jit(solution)/shard_map/ppermute | solution.py:320
  116.0 76.4 %copy-start.3 = (bf16[8,64,1024]{2,1,0:T(8,128)(2,1)}, bf16[8,64,1024]{2,1,0:T(8,128)(2,1)S(1)}, u32[]{:S(2)}) copy-start(bf16[8,64,1024]{2,1,0:T(8,128)(2,1)S(1)} %all-to-all-done) | copy-start | bytes 3145732
  116.0 20.9 %collective-permute-start.13 = (bf16[2048,1024]{1,0:T(8,128)(2,1)}, bf16[2048,1024]{1,0:T(8,128)(2,1)}, u32[]{:S(2)}, u32[]{:S(2)}) collective-permute-start(bf16[2048,1024]{1,0:T(8,128)(2,1)} %bitcast.30), channel_id=1, source_target_pairs={{0,1},{1,0},{2,3},{3,2},{4,5},{5,4},{6,7},{7,6},{8,9},{9,8},{10,11... | collective-permute-start | bytes 12582920 | tf_op jit(solution)/shard_map/ppermute | solution.py:304
  116.1 10.7 %collective-permute-start.11 = (bf16[1024,1024]{1,0:T(8,128)(2,1)S(1)}, bf16[1024,1024]{1,0:T(8,128)(2,1)}, u32[]{:S(2)}, u32[]{:S(2)}) collective-permute-start(bf16[1024,1024]{1,0:T(8,128)(2,1)S(1)} %collective-permute-done.8.refs_6_.refs_1_), channel_id=1, source_target_pairs={{0,1},{1,0},{2,3},{3,2},{4,5},{5,4},{6,7},{7,6},{8,9},{9,8},{10,11... | collective-permute-start | bytes 6291464 | tf_op jit(solution)/shard_map/ppermute | solution.py:304
  119.5 6.2 %collective-permute-start.12 = (bf16[2048,128]{1,0:T(8,128)(2,1)}, bf16[2048,128]{1,0:T(8,128)(2,1)S(1)}, u32[]{:S(2)}, u32[]{:S(2)}) collective-permute-start(bf16[2048,128]{1,0:T(8,128)(2,1)} %collective-permute-done.7.refs_10_.refs_5_), channel_id=1, source_target_pairs={{0,1},{1,0},{2,3},{3,2},{4,5},{5,4},{6,7},{7,6},{8,9},{9,8},{10,11... | collective-permute-start | bytes 1572872 | tf_op jit(solution)/shard_map/ppermute | solution.py:304
  121.1 37.9 %collective-permute-start.10 = (bf16[640,1024]{1,0:T(8,128)(2,1)S(1)}, bf16[640,1024]{1,0:T(8,128)(2,1)S(1)}, u32[]{:S(2)}, u32[]{:S(2)}) collective-permute-start(bf16[640,1024]{1,0:T(8,128)(2,1)S(1)} %broadcast_select_fusion), channel_id=1, source_target_pairs={{8,12},{10,14},{4,0},{6,2},{9,13},{11,15},{5,1},{7,3},{24,28},{26,... | collective-permute-start | bytes 3932168 | tf_op jit(solution)/shard_map/ppermute | solution.py:295
  160.1 12.6 %collective-permute-start.14 = (bf16[384,1024]{1,0:T(8,128)(2,1)}, bf16[384,1024]{1,0:T(8,128)(2,1)S(1)}, u32[]{:S(2)}, u32[]{:S(2)}) collective-permute-start(bf16[384,1024]{1,0:T(8,128)(2,1)} %collective-permute-done.2.refs_1_), channel_id=1, source_target_pairs={{4,8},{6,10},{8,12},{10,14},{5,9},{7,11},{9,13},{11,15},{20,24},{2... | collective-permute-start | bytes 2359304 | tf_op jit(solution)/shard_map/ppermute | solution.py:297
  160.8 21.5 %collective-permute-start.15 = (bf16[384,1024]{1,0:T(8,128)(2,1)}, bf16[384,1024]{1,0:T(8,128)(2,1)S(1)}, u32[]{:S(2)}, u32[]{:S(2)}) collective-permute-start(bf16[384,1024]{1,0:T(8,128)(2,1)} %collective-permute-done.3.refs_3_), channel_id=1, source_target_pairs={{4,0},{6,2},{8,4},{10,6},{5,1},{7,3},{9,5},{11,7},{20,16},{22,18},... | collective-permute-start | bytes 2359304 | tf_op jit(solution)/shard_map/ppermute | solution.py:298
  171.1 43.3 %collective-permute-start.17 = (bf16[640,1024]{1,0:T(8,128)(2,1)}, bf16[640,1024]{1,0:T(8,128)(2,1)}, u32[]{:S(2)}, u32[]{:S(2)}) collective-permute-start(bf16[640,1024]{1,0:T(8,128)(2,1)} %get-tuple-element.58), channel_id=1, source_target_pairs={{0,2},{2,0},{4,6},{6,4},{8,10},{10,8},{12,14},{14,12},{1,3},{3,1},... | collective-permute-start | bytes 3932168 | tf_op jit(solution)/shard_map/ppermute | solution.py:510
  183.3 31.1 %collective-permute-start.16 = (bf16[384,1024]{1,0:T(8,128)(2,1)}, bf16[384,1024]{1,0:T(8,128)(2,1)}, u32[]{:S(2)}, u32[]{:S(2)}) collective-permute-start(bf16[384,1024]{1,0:T(8,128)(2,1)} %broadcast_select_fusion.1), channel_id=1, source_target_pairs={{8,12},{10,14},{4,0},{6,2},{9,13},{11,15},{5,1},{7,3},{24,28},{26,... | collective-permute-start | bytes 2359304 | tf_op jit(solution)/shard_map/ppermute | solution.py:295
  186.7 20.8 %all-to-all-start.1 = ((bf16[8,16,640]{2,1,0:T(8,128)(2,1)}), bf16[8,16,640]{2,1,0:T(8,128)(2,1)S(1)}, u32[]{:S(2)}, u32[]{:S(2)}) async-start(bf16[8,16,640]{2,1,0:T(8,128)(2,1)} %broadcast_in_dim.52), calls=%async_computation.1 | async-start | bytes 327680 | tf_op jit(solution)/shard_map/all_to_all | solution.py:437
  192.4 34.2 %collective-permute-start.18 = (bf16[512,1024]{1,0:T(8,128)(2,1)S(1)}, bf16[512,1024]{1,0:T(8,128)(2,1)}, u32[]{:S(2)}, u32[]{:S(2)}) collective-permute-start(bf16[512,1024]{1,0:T(8,128)(2,1)S(1)} %bitcast.35), channel_id=1, source_target_pairs={{0,1},{1,0},{2,3},{3,2},{4,5},{5,4},{6,7},{7,6},{8,9},{9,8},{10,11... | collective-permute-start | bytes 3145736 | tf_op jit(solution)/shard_map/ppermute | solution.py:304
  219.9 26.3 %collective-permute-start.19 = (bf16[384,1024]{1,0:T(8,128)(2,1)}, bf16[384,1024]{1,0:T(8,128)(2,1)}, u32[]{:S(2)}, u32[]{:S(2)}) collective-permute-start(bf16[384,1024]{1,0:T(8,128)(2,1)} %get-tuple-element.66), channel_id=1, source_target_pairs={{0,2},{2,0},{4,6},{6,4},{8,10},{10,8},{12,14},{14,12},{1,3},{3,1},... | collective-permute-start | bytes 2359304 | tf_op jit(solution)/shard_map/ppermute | solution.py:518
  223.0 15.7 %all-to-all-start.2 = ((bf16[8,16,384]{2,1,0:T(8,128)(2,1)}), bf16[8,16,384]{2,1,0:T(8,128)(2,1)S(1)}, u32[]{:S(2)}, u32[]{:S(2)}) async-start(bf16[8,16,384]{2,1,0:T(8,128)(2,1)} %broadcast_in_dim.53), calls=%async_computation.2 | async-start | bytes 196608 | tf_op jit(solution)/shard_map/all_to_all | solution.py:437
  (14 other events, 196.5 us)

commit v3 on v2

--- a/solution.py
+++ b/solution.py
@@ -115,7 +115,7 @@
                 total[...] += term
 
 
-def rest_kernel(farthest, total, block, *refs):
+def rest_kernel(farthest, total, block, other, *refs):
     pieces, refs = refs[:4], refs[4:]
     factors, refs = refs[:3], refs[3:]
     stored, adapter, fold, partial, shrunk, weight, sems = refs
@@ -144,7 +144,7 @@
 
     for copy in arrive(pieces[0], factors[1]):
         copy.wait()
-    full = total[...] + dot(block[...], weight[...])
+    full = total[...] + dot(block[...] + other[...], weight[...])
     partial[...] = full[:, :width].astype(partial.dtype)
     kept = jnp.where(stored[...] == adapter[...], full[:, width:], 0.0).astype(jnp.bfloat16)
     across = (((1,), (1,)), ((), ()))
@@ -193,7 +193,7 @@
 
 
 def lora_kernel(farthest, base, everyone, stored, adapter, unfold, *refs):
-    expand, block, weights, refs = refs[:2], refs[2], refs[3:5], refs[5:]
+    expand, (block, other), weights, refs = refs[:2], refs[2:4], refs[4:6], refs[6:]
     partials, (out, weight, sem) = refs[:-3], refs[-3:]
     depth = weight.shape[0]
     rows = pl.ds(pl.multiple_of(farthest[0] * depth, depth), depth)
@@ -211,7 +211,7 @@
     half = spread.shape[1] // 2
     added = dot(spread[:, :half], expand[0][...]) + dot(spread[:, half:], expand[1][...])
     pltpu.make_async_copy(weights[0].at[rows], weight, sem).wait()
-    added = base[...] + added + dot(block[...], weight[...])
+    added = base[...] + added + dot(block[...] + other[...], weight[...])
     for partial in partials:
         added += partial[...].astype(jnp.float32)
     out[...] = added.astype(out.dtype)
@@ -289,11 +289,6 @@
     downs = [{0: p} for p in pieces]
 
     def hop(c, h):
-        if h == planes - 1:
-            inner = jnp.where(z == 1, downs[c][h - 1], ups[c][h - 1])
-            pairs = [p for p in up(h) + down(h)]
-            ups[c][h] = downs[c][h] = lax.ppermute(inner, "tp", pairs)
-            return
         ups[c][h] = lax.ppermute(ups[c][h - 1], "tp", up(h))
         downs[c][h] = lax.ppermute(downs[c][h - 1], "tp", down(h))
 
@@ -302,6 +297,19 @@
 
     def to_other_core(value):
         return lax.ppermute(value, "dp", swap)
+
+    steps = jnp.arange(planes)
+    above = z + steps < planes
+    hops = jnp.where(above, steps, planes - steps)
+    sel = jnp.where(
+        steps == 0, 0, jnp.where(hops == planes - 1, SOURCES - 1, hops + jnp.where(above, planes - 2, 0))
+    ).astype(jnp.int32)
+    plane = (z + steps) % planes
+    places_other = place(plane).astype(jnp.int32)
+    places_own = (2 * ((plane // 2) ^ d) + plane % 2).astype(jnp.int32)
+    distant = jnp.where(z == 0, planes - 1, 0)
+    farthest_other = place(distant).astype(jnp.int32)[None]
+    farthest_own = jnp.stack([distant % 2, (distant // 2) ^ d]).astype(jnp.int32)
 
     blocks = query_weight.reshape(planes, depth, width)
     hop(0, 1)
@@ -325,8 +333,8 @@
     expand_half = lax.all_to_all(expand_half, "tp", split_axis=0, concat_axis=0, tiled=True)
     expand_half = expand_half.reshape(tp * half, width)
 
-    (ups[0][2], downs[0][2], ups[1][1], downs[1][1], shrink_near, far, near_crossed, expand_half, own_half) = step(
-        (ups[0][2], downs[0][2], ups[1][1], downs[1][1], shrink_near, far, near_crossed, expand_half, own_half)
+    (ups[0][2], downs[0][2], ups[1][1], downs[1][1], shrink_near, far, near_crossed, expand_half, own_half, shrink_own, sel, places_other, places_own) = step(
+        (ups[0][2], downs[0][2], ups[1][1], downs[1][1], shrink_near, far, near_crossed, expand_half, own_half, shrink_own, sel, places_other, places_own)
     )
     hop(0, 3)
     shrink = [shrink_own, shrink_near, to_other_core(shrink_near)]
@@ -353,24 +361,14 @@
     entry_adapter = entry_adapter[None, :].astype(jnp.int32)
     unfold = (jnp.arange(ADAPTER_RANK)[:, None] == entry[None, :] % ADAPTER_RANK).astype(jnp.bfloat16)
 
-    steps = jnp.arange(planes)
-    above = z + steps < planes
-    hops = jnp.where(above, steps, planes - steps)
-    sel = jnp.where(
-        steps == 0, 0, jnp.where(hops == planes - 1, SOURCES - 1, hops + jnp.where(above, planes - 2, 0))
-    ).astype(jnp.int32)
-    plane = (z + steps) % planes
-    places_other = place(plane).astype(jnp.int32)
-    places_own = (2 * ((plane // 2) ^ d) + plane % 2).astype(jnp.int32)
-    distant = jnp.where(z == 0, planes - 1, 0)
-    farthest_other = place(distant).astype(jnp.int32)[None]
-    farthest_own = jnp.stack([distant % 2, (distant // 2) ^ d]).astype(jnp.int32)
-
     def sources(c):
         between = range(1, planes - 1)
         return [pieces[c]] + [ups[c][h] for h in between] + [downs[c][h] for h in between] + [
-            ups[c].get(planes - 1)
+            None
         ]
+
+    def longest(c):
+        return ups[c][planes - 1], downs[c][planes - 1]
 
     total_columns = width + 2 * holder_columns
 
@@ -401,7 +399,7 @@
             grid_spec=pltpu.PrefetchScalarGridSpec(
                 num_scalar_prefetch=1,
                 grid=(1,),
-                in_specs=[whole(total.shape), whole((count, depth))]
+                in_specs=[whole(total.shape), whole((count, depth)), whole((count, depth))]
                 + [pl.BlockSpec(memory_space=pl.ANY) for _ in range(7)]
                 + [whole(v.shape) for v in small],
                 out_specs=[whole(o.shape) for o in outs],
@@ -415,7 +413,7 @@
             cost_estimate=pl.CostEstimate(
                 flops=2 * count * depth * total_columns, bytes_accessed=4 * depth * width, transcendentals=0
             ),
-        )(farthest_other, total, ups[c][planes - 1], *weight_other, *shrink, *small)
+        )(farthest_other, total, *longest(c), *weight_other, *shrink, *small)
 
     def own_part(c, *events):
         count = ROW_CHUNKS[c]
@@ -455,6 +453,7 @@
                     whole(expand[0].shape),
                     whole(expand[1].shape),
                     whole((count, depth)),
+                    whole((count, depth)),
                 ]
                 + [pl.BlockSpec(memory_space=pl.ANY)] * 2
                 + [rows_of for _ in partials],
@@ -474,7 +473,7 @@
             entry_adapter,
             unfold,
             *expand,
-            ups[c][planes - 1],
+            *longest(c),
             *weight_own,
             *partials,
         )
@@ -512,8 +511,8 @@
     hop(1, 3)
     everyone_a = spread_out(shrunk_a)
     early_c = early_part(1)
-    base_c = own_part(1, early_c, everyone_a)
-    ups[1][3] = step(ups[1][3], base_c, got_a)
+    base_c = own_part(1, early_c)
+    ups[1][3], downs[1][3] = step((ups[1][3], downs[1][3]), base_c, got_a, everyone_a)
     partial_c, shrunk_c = rest_part(1, early_c)
     got_c = lax.ppermute(partial_c, "tp", across)
     everyone_c = spread_out(shrunk_c)

time: 250 us -> 246 us (0.984)
  waiting for transfers between devices: 112 us -> 101 us
  starting transfers between devices: 42.2 us -> 47.5 us
  other arithmetic: 9.14 us -> 6.22 us
    ppermute x2 -> x0, waiting for transfers between devices: 13 us -> none  [hop(): ups[c][h] = downs[c][h] = lax.ppermute(inner, 'tp', pairs)]
    ppermute x4 -> x6, waiting for transfers between devices: 37.4 us -> 48.2 us  [hop(): downs[c][h] = lax.ppermute(downs[c][h - 1], 'tp', down(h))]
    all_to_all x2, waiting for transfers between devices: 11 us -> 1.08 us  [spread_out(): lax.all_to_all(everyone, 'tp', split_axis=0, concat_axis=0, tiled=True)]
    ppermute x5, waiting for transfers between devices: 3.28 us -> 6.92 us  [to_other_core(): return lax.ppermute(value, 'dp', swap)]
    ppermute x2 -> x0, starting transfers between devices: 2.57 us -> none  [hop(): ups[c][h] = downs[c][h] = lax.ppermute(inner, 'tp', pairs)]
    ppermute x4 -> x6, starting transfers between devices: 5.13 us -> 7.7 us  [hop(): downs[c][h] = lax.ppermute(downs[c][h - 1], 'tp', down(h))]
    select_n x2 -> x0, other arithmetic: 2.51 us -> none  [hop(): inner = jnp.where(z == 1, downs[c][h - 1], ups[c][h - 1])]
    ppermute x4 -> x6, starting transfers between devices: 12.5 us -> 14.7 us  [hop(): ups[c][h] = lax.ppermute(ups[c][h - 1], 'tp', up(h))]
  transfers between devices with their start and end apart: 23 -> 25, of which waited for: 10 -> 8; matrix products, arithmetic and copies ran while one was open for 10% -> 9% of each run, Pallas kernels for 25% -> 26%
where the time goes in v3:
time: 246 us; the launch traced here: 244 us
  waiting for transfers between devices  101 us (41%)
  Pallas kernels  66.1 us (27%)
  starting transfers between devices  47.5 us (19%)
  local copies, waits for them, and re-layouts  22.2 us (9%)
  other arithmetic  6.22 us (3%)
    ppermute x6, waiting for transfers between devices, hop(): downs[c][h] = lax.ppermute(downs[c][h - 1], 'tp', down(h))  48.2 us
    pallas_call x4, Pallas kernels, on_line(): pl.pallas_call(kernel, grid_spec=pltpu.PrefetchScalarGridSpec(num_scalar_...  33.6 us
    ppermute x6, waiting for transfers between devices, hop(): ups[c][h] = lax.ppermute(ups[c][h - 1], 'tp', up(h))  30.8 us
    pallas_call x2, Pallas kernels, lora_part(): pl.pallas_call(lora_kernel, grid_spec=pltpu.PrefetchScalarGridSpec(num_sc...  16 us
    ppermute x6, starting transfers between devices, hop(): ups[c][h] = lax.ppermute(ups[c][h - 1], 'tp', up(h))  14.7 us
    ppermute x1, waiting for transfers between devices, line_body(): shrink_near = lax.ppermute(leaving, 'tp', across)  14.2 us
    pallas_call x2, Pallas kernels, rest_part(): pl.pallas_call(rest_kernel, grid_spec=pltpu.PrefetchScalarGridSpec(num_sc...  13.2 us
    all_to_all x2, starting transfers between devices, spread_out(): lax.all_to_all(everyone, 'tp', split_axis=0, concat_axis=0, tiled=True)  10.8 us
  transfers between devices with their start and end apart: 25, of which 8 were waited for; matrix products, arithmetic and copies ran while one was open for 9% of the time, Pallas kernels for 26%

profile of v3, /device:TPU:0, one launch (start us, length us, event | category | flops | bytes accessed | tf_op | source)
XLA Modules:
  0.0 243.8 jit_solution(15089527445418105487)
XLA Ops:
  0.0 3.2 %dynamic-slice_bitcast_fusion = bf16[1024,1024]{1,0:T(8,128)(2,1)} fusion(bf16[4,1024,1024]{2,1,0:T(8,128)(2,1)} %bitcast.38, s32[]{:T(128)S(6)} %select_n.237), kind=kLoop, calls=%fused_computation | loop fusion | bytes 4194308 | tf_op jit(solution)/shard_map/jit(dynamic_index_in_dim)/squeeze | solution.py:66
  3.2 2.9 %collective-permute-start.4 = (bf16[1024,1024]{1,0:T(8,128)(2,1)}, bf16[1024,1024]{1,0:T(8,128)(2,1)}, u32[]{:S(2)}, u32[]{:S(2)}) collective-permute-start(bf16[1024,1024]{1,0:T(8,128)(2,1)} %dynamic-slice_bitcast_fusion), channel_id=1, source_target_pairs={{0,2},{2,0},{4,6},{6,4},{8,10},{10,8},{12,14},{14,12},{1,3},{3,1},... | collective-permute-start | bytes 6291464 | tf_op jit(solution)/shard_map/ppermute | solution.py:317
  7.4 4.5 %collective-permute-start = (bf16[640,1024]{1,0:T(8,128)(2,1)}, bf16[640,1024]{1,0:T(8,128)(2,1)}, u32[]{:S(2)}, u32[]{:S(2)}) collective-permute-start(bf16[640,1024]{1,0:T(8,128)(2,1)} %slice.20.refs_0_), channel_id=1, source_target_pairs={{0,4},{2,6},{4,8},{6,10},{8,12},{10,14},{1,5},{3,7},{5,9},{7,11},{... | collective-permute-start | bytes 3932168 | tf_op jit(solution)/shard_map/ppermute | solution.py:292
  13.3 5.4 %collective-permute-start.2 = (bf16[384,1024]{1,0:T(8,128)(2,1)S(1)}, bf16[384,1024]{1,0:T(8,128)(2,1)}, u32[]{:S(2)}, u32[]{:S(2)}) collective-permute-start(bf16[384,1024]{1,0:T(8,128)(2,1)S(1)} %slice.21.refs_0_), channel_id=1, source_target_pairs={{0,4},{2,6},{4,8},{6,10},{8,12},{10,14},{1,5},{3,7},{5,9},{7,11},{... | collective-permute-start | bytes 2359304 | tf_op jit(solution)/shard_map/ppermute | solution.py:292
  24.9 30.8 %collective-permute-done.2.refs_1_ = bf16[384,1024]{1,0:T(8,128)(2,1)} collective-permute-done((bf16[384,1024]{1,0:T(8,128)(2,1)S(1)}, bf16[384,1024]{1,0:T(8,128)(2,1)}, u32[]{:S(2)}, u32[]{:S(2)}) %collective-permute-start.2) | collective-permute-done | bytes 786464 | tf_op jit(solution)/shard_map/ppermute | solution.py:292
  55.7 5.3 %collective-permute-done.3.refs_3_ = bf16[384,1024]{1,0:T(8,128)(2,1)} collective-permute-done((bf16[384,1024]{1,0:T(8,128)(2,1)S(1)}, bf16[384,1024]{1,0:T(8,128)(2,1)}, u32[]{:S(2)}, u32[]{:S(2)}) %collective-permute-start.3) | collective-permute-done | bytes 786464 | tf_op jit(solution)/shard_map/ppermute | solution.py:293
  64.1 3.6 %all-to-all-start = ((bf16[8,64,1024]{2,1,0:T(8,128)(2,1)}), bf16[8,64,1024]{2,1,0:T(8,128)(2,1)S(1)}, u32[]{:S(2)}, u32[]{:S(2)}) async-start(bf16[8,64,1024]{2,1,0:T(8,128)(2,1)} %copy.21), calls=%async_computation | async-start | bytes 2097152 | tf_op jit(solution)/shard_map/all_to_all | solution.py:333
  73.8 4.7 %constant_dynamic-slice_fusion = bf16[2,1,1024,1024]{3,2,1,0:T(8,128)(2,1)} fusion(bf16[2,2,1024,1024]{3,2,1,0:T(8,128)(2,1)} %bitcast.39, s32[]{:T(128)S(6)} %select_n.245), kind=kLoop, calls=%fused_computation.40 | loop fusion | bytes 8388612 | tf_op jit(solution)/shard_map/jit(dynamic_index_in_dim)/dynamic_slice | solution.py:331
  79.7 14.2 %collective-permute-done.7.refs_10_.refs_5_ = bf16[2048,128]{1,0:T(8,128)(2,1)} collective-permute-done((bf16[2048,128]{1,0:T(8,128)(2,1)}, bf16[2048,128]{1,0:T(8,128)(2,1)}, u32[]{:S(2)}, u32[]{:S(2)}) %collective-permute-start.7) | collective-permute-done | bytes 524320 | tf_op jit(solution)/shard_map/ppermute | solution.py:328
  93.9 22.0 %collective-permute-done.6.refs_4_ = bf16[640,1024]{1,0:T(8,128)(2,1)} collective-permute-done((bf16[640,1024]{1,0:T(8,128)(2,1)}, bf16[640,1024]{1,0:T(8,128)(2,1)}, u32[]{:S(2)}, u32[]{:S(2)}) %collective-permute-start.6) | collective-permute-done | bytes 1310752 | tf_op jit(solution)/shard_map/ppermute | solution.py:293
  120.4 6.9 %collective-permute-done.12.refs_11_.refs_6_ = bf16[2048,128]{1,0:T(8,128)(2,1)} collective-permute-done((bf16[2048,128]{1,0:T(8,128)(2,1)}, bf16[2048,128]{1,0:T(8,128)(2,1)}, u32[]{:S(2)}, u32[]{:S(2)}) %collective-permute-start.12) | collective-permute-done | bytes 524320 | tf_op jit(solution)/shard_map/ppermute | solution.py:299
  127.3 10.1 %shard_map.64.total = f32[640,1280]{1,0:T(8,128)} custom-call(s32[4]{0:T(128)} %get-tuple-element.70.sel, s32[4]{0:T(128)} %get-tuple-element.51.place, bf16[640,1024]{1,0:T(8,128)(2,1)} %slice.20.refs_0_, bf16[640,1024]{1,0:T(8,128)(2,1)} %collective-permute-done.refs_1_, bf16[640,1024]{1,0:T(8,128)(2,1)} %collective-permute-done.5.refs_2_, ...), custom_call_target="tpu_custom_call" | custom-call | flops 5368709120 | bytes 16252928 | tf_op jit(solution)/shard_map/pallas_call | solution.py:234
  137.4 9.1 %shard_map.65.base = f32[640,1024]{1,0:T(8,128)} custom-call(s32[4]{0:T(128)} %get-tuple-element.70.sel, s32[4]{0:T(128)} %fusion.14.place, bf16[640,1024]{1,0:T(8,128)(2,1)} %slice.20.refs_0_, bf16[640,1024]{1,0:T(8,128)(2,1)} %collective-permute-done.refs_1_, bf16[640,1024]{1,0:T(8,128)(2,1)} %collective-permute-done.5.refs_2_, ...), custom_call_target="tpu_custom_call" | custom-call | flops 5368709120 | bytes 16252928 | tf_op jit(solution)/shard_map/pallas_call | solution.py:234
  149.2 7.3 %collective-permute-done.16.other.refs_3_ = bf16[640,1024]{1,0:T(8,128)(2,1)S(1)} collective-permute-done((bf16[640,1024]{1,0:T(8,128)(2,1)}, bf16[640,1024]{1,0:T(8,128)(2,1)S(1)}, u32[]{:S(2)}, u32[]{:S(2)}) %collective-permute-start.16) | collective-permute-done | bytes 1310752 | tf_op jit(solution)/shard_map/ppermute | solution.py:293
  157.6 7.4 %shard_map.66 = (bf16[640,1024]{1,0:T(8,128)(2,1)}, bf16[16,640]{1,0:T(8,128)(2,1)}) custom-call(s32[1]{0:T(128)} %bitcast.15.farthest, f32[640,1280]{1,0:T(8,128)} %shard_map.64.total, bf16[640,1024]{1,0:T(8,128)(2,1)} %copy-done.5, bf16[640,1024]{1,0:T(8,128)(2,1)} %copy-done.6, bf16[1024,1024]{1,0:T(8,128)(2,1)} %collective-permute-done.4.refs_5_.refs_0_, ...), custom_call_target="tpu_custom_call" | custom-call | flops 1677721600 | bytes 4194304 | tf_op jit(solution)/shard_map/pallas_call | solution.py:397
  166.6 13.6 %collective-permute-done.15.refs_4_ = bf16[384,1024]{1,0:T(8,128)(2,1)} collective-permute-done((bf16[384,1024]{1,0:T(8,128)(2,1)}, bf16[384,1024]{1,0:T(8,128)(2,1)}, u32[]{:S(2)}, u32[]{:S(2)}) %collective-permute-start.15) | collective-permute-done | bytes 786464 | tf_op jit(solution)/shard_map/ppermute | solution.py:293
  185.9 5.0 %all-to-all-start.1 = ((bf16[8,16,640]{2,1,0:T(8,128)(2,1)}), bf16[8,16,640]{2,1,0:T(8,128)(2,1)S(1)}, u32[]{:S(2)}, u32[]{:S(2)}) async-start(bf16[8,16,640]{2,1,0:T(8,128)(2,1)} %broadcast_in_dim.52), calls=%async_computation.1 | async-start | bytes 327680 | tf_op jit(solution)/shard_map/all_to_all | solution.py:435
  191.0 7.6 %shard_map.67.total = f32[384,1280]{1,0:T(8,128)} custom-call(s32[4]{0:T(128)} %get-tuple-element.70.sel, s32[4]{0:T(128)} %get-tuple-element.51.place, bf16[384,1024]{1,0:T(8,128)(2,1)} %copy-done.4, bf16[384,1024]{1,0:T(8,128)(2,1)} %collective-permute-done.2.refs_1_, bf16[384,1024]{1,0:T(8,128)(2,1)} %copy-done.8, ...), custom_call_target="tpu_custom_call" | custom-call | flops 3221225472 | bytes 13107200 | tf_op jit(solution)/shard_map/pallas_call | solution.py:234
  198.6 6.8 %shard_map.68.base = f32[384,1024]{1,0:T(8,128)} custom-call(s32[4]{0:T(128)} %get-tuple-element.70.sel, s32[4]{0:T(128)} %fusion.14.place, bf16[384,1024]{1,0:T(8,128)(2,1)} %copy-done.4, bf16[384,1024]{1,0:T(8,128)(2,1)} %collective-permute-done.2.refs_1_, bf16[384,1024]{1,0:T(8,128)(2,1)} %copy-done.8, bf16[384,1024]{1,0:T(8,128)(2,1)} %collective-permute-done.3.refs_3_, ...), custom_call_target="tpu_custom_call" | custom-call | flops 3221225472 | bytes 13107200 | tf_op jit(solution)/shard_map/pallas_call | solution.py:234
  205.5 5.8 %shard_map.69 = (bf16[384,1024]{1,0:T(8,128)(2,1)}, bf16[16,384]{1,0:T(8,128)(2,1)}) custom-call(s32[1]{0:T(128)} %bitcast.15.farthest, f32[384,1280]{1,0:T(8,128)} %shard_map.67.total, bf16[384,1024]{1,0:T(8,128)(2,1)} %collective-permute-done.17.block.refs_2_, bf16[384,1024]{1,0:T(8,128)(2,1)} %collective-permute-done.18.other.refs_3_, ...), custom_call_target="tpu_custom_call" | custom-call | flops 1006632960 | bytes 4194304 | tf_op jit(solution)/shard_map/pallas_call | solution.py:397
  215.9 5.8 %all-to-all-start.2 = ((bf16[8,16,384]{2,1,0:T(8,128)(2,1)}), bf16[8,16,384]{2,1,0:T(8,128)(2,1)S(1)}, u32[]{:S(2)}, u32[]{:S(2)}) async-start(bf16[8,16,384]{2,1,0:T(8,128)(2,1)} %broadcast_in_dim.53), calls=%async_computation.2 | async-start | bytes 196608 | tf_op jit(solution)/shard_map/all_to_all | solution.py:435
  222.7 8.9 %shard_map.71.refs_0_ = bf16[1024,1024]{1,0:T(8,128)(2,1)} custom-call(s32[2]{0:T(128)} %pad_add_fusion.farthest, f32[640,1024]{1,0:T(8,128)} %shard_map.65.base, bf16[8,16,640]{2,1,0:T(8,128)(2,1)} %copy-done.11, s32[640,1]{1,0:T(8,128)} %slice.26.refs_7_.stored, s32[1,1024]{1,0:T(1,128)} %fusion.7.adapter, bf16[16,1024]{1,0:T(8,128)(2,1)} %fusion.unfold, ...), custom_call_target="tpu_custom_call" | custom-call | flops 2684354560 | bytes 4194304 | tf_op jit(solution)/shard_map/pallas_call | solution.py:442
  233.3 7.1 %shard_map.70.base = f32[384,1024]{1,0:T(8,128)} custom-call(s32[2]{0:T(128)} %pad_add_fusion.farthest, f32[384,1024]{1,0:T(8,128)} %shard_map.68.base, bf16[8,16,384]{2,1,0:T(8,128)(2,1)} %copy-done.12, s32[384,1]{1,0:T(8,128)} %slice.27.refs_7_.stored, s32[1,1024]{1,0:T(1,128)} %fusion.7.adapter, bf16[16,1024]{1,0:T(8,128)(2,1)} %fusion.unfold, ...), custom_call_target="tpu_custom_call" | custom-call | flops 1610612736 | bytes 4194304 | tf_op jit(solution)/shard_map/pallas_call | solution.py:442
  240.5 3.3 %shard_map.72 = bf16[1024,1024]{1,0:T(8,128)(2,1)} custom-call(f32[384,1024]{1,0:T(8,128)} %shard_map.70.base, bf16[384,1024]{1,0:T(8,128)(2,1)} %collective-permute-done.21.partial, bf16[1024,1024]{1,0:T(8,128)(2,1)} %shard_map.71.refs_0_), custom_call_target="tpu_custom_call", output_to_operand_aliasing={{}: (2, {})} | custom-call | flops 786432 | bytes 3145728 | tf_op jit(solution)/shard_map/pallas_call | solution.py:488
  (91 shorter events, 41.8 us)
Async XLA Ops:
  3.2 57.7 %collective-permute-start.4 = (bf16[1024,1024]{1,0:T(8,128)(2,1)}, bf16[1024,1024]{1,0:T(8,128)(2,1)}, u32[]{:S(2)}, u32[]{:S(2)}) collective-permute-start(bf16[1024,1024]{1,0:T(8,128)(2,1)} %dynamic-slice_bitcast_fusion), channel_id=1, source_target_pairs={{0,2},{2,0},{4,6},{6,4},{8,10},{10,8},{12,14},{14,12},{1,3},{3,1},... | collective-permute-start | bytes 6291464 | tf_op jit(solution)/shard_map/ppermute | solution.py:317
  7.4 53.6 %collective-permute-start = (bf16[640,1024]{1,0:T(8,128)(2,1)}, bf16[640,1024]{1,0:T(8,128)(2,1)}, u32[]{:S(2)}, u32[]{:S(2)}) collective-permute-start(bf16[640,1024]{1,0:T(8,128)(2,1)} %slice.20.refs_0_), channel_id=1, source_target_pairs={{0,4},{2,6},{4,8},{6,10},{8,12},{10,14},{1,5},{3,7},{5,9},{7,11},{... | collective-permute-start | bytes 3932168 | tf_op jit(solution)/shard_map/ppermute | solution.py:292
  11.9 49.0 %collective-permute-start.1 = (bf16[640,1024]{1,0:T(8,128)(2,1)}, bf16[640,1024]{1,0:T(8,128)(2,1)}, u32[]{:S(2)}, u32[]{:S(2)}) collective-permute-start(bf16[640,1024]{1,0:T(8,128)(2,1)} %slice.20.refs_0_), channel_id=1, source_target_pairs={{4,0},{6,2},{8,4},{10,6},{12,8},{14,10},{5,1},{7,3},{9,5},{11,7},{... | collective-permute-start | bytes 3932168 | tf_op jit(solution)/shard_map/ppermute | solution.py:293
  13.3 42.4 %collective-permute-start.2 = (bf16[384,1024]{1,0:T(8,128)(2,1)S(1)}, bf16[384,1024]{1,0:T(8,128)(2,1)}, u32[]{:S(2)}, u32[]{:S(2)}) collective-permute-start(bf16[384,1024]{1,0:T(8,128)(2,1)S(1)} %slice.21.refs_0_), channel_id=1, source_target_pairs={{0,4},{2,6},{4,8},{6,10},{8,12},{10,14},{1,5},{3,7},{5,9},{7,11},{... | collective-permute-start | bytes 2359304 | tf_op jit(solution)/shard_map/ppermute | solution.py:292
  18.7 42.2 %collective-permute-start.3 = (bf16[384,1024]{1,0:T(8,128)(2,1)S(1)}, bf16[384,1024]{1,0:T(8,128)(2,1)}, u32[]{:S(2)}, u32[]{:S(2)}) collective-permute-start(bf16[384,1024]{1,0:T(8,128)(2,1)S(1)} %slice.21.refs_0_), channel_id=1, source_target_pairs={{4,0},{6,2},{8,4},{10,6},{12,8},{14,10},{5,1},{7,3},{9,5},{11,7},{... | collective-permute-start | bytes 2359304 | tf_op jit(solution)/shard_map/ppermute | solution.py:293
  61.0 55.0 %collective-permute-start.8 = (bf16[1024,1024]{1,0:T(8,128)(2,1)}, bf16[1024,1024]{1,0:T(8,128)(2,1)S(1)}, u32[]{:S(2)}, u32[]{:S(2)}) collective-permute-start(bf16[1024,1024]{1,0:T(8,128)(2,1)} %collective-permute-done.4.refs_5_.refs_0_), channel_id=1, source_target_pairs={{0,16},{16,0},{1,17},{17,1},{2,18},{18,2},{3,19},{19,3},{4,20},{20... | collective-permute-start | bytes 6291464 | tf_op jit(solution)/shard_map/ppermute | solution.py:327
  62.5 53.4 %collective-permute-start.9 = (bf16[1024,1024]{1,0:T(8,128)(2,1)}, bf16[1024,1024]{1,0:T(8,128)(2,1)}, u32[]{:S(2)}, u32[]{:S(2)}) collective-permute-start(bf16[1024,1024]{1,0:T(8,128)(2,1)} %collective-permute-done.4.refs_5_.refs_0_), channel_id=1, source_target_pairs={{0,1},{1,0},{2,3},{3,2},{4,5},{5,4},{6,7},{7,6},{8,9},{9,8},{10,11... | collective-permute-start | bytes 6291464 | tf_op jit(solution)/shard_map/ppermute | solution.py:299
  64.1 51.9 %all-to-all-start = ((bf16[8,64,1024]{2,1,0:T(8,128)(2,1)}), bf16[8,64,1024]{2,1,0:T(8,128)(2,1)S(1)}, u32[]{:S(2)}, u32[]{:S(2)}) async-start(bf16[8,64,1024]{2,1,0:T(8,128)(2,1)} %copy.21), calls=%async_computation | async-start | bytes 2097152 | tf_op jit(solution)/shard_map/all_to_all | solution.py:333
  67.7 26.3 %collective-permute-start.5 = (bf16[640,1024]{1,0:T(8,128)(2,1)}, bf16[640,1024]{1,0:T(8,128)(2,1)}, u32[]{:S(2)}, u32[]{:S(2)}) collective-permute-start(bf16[640,1024]{1,0:T(8,128)(2,1)} %collective-permute-done.refs_1_), channel_id=1, source_target_pairs={{4,8},{6,10},{8,12},{10,14},{5,9},{7,11},{9,13},{11,15},{20,24},{2... | collective-permute-start | bytes 3932168 | tf_op jit(solution)/shard_map/ppermute | solution.py:292
  69.4 46.6 %collective-permute-start.6 = (bf16[640,1024]{1,0:T(8,128)(2,1)}, bf16[640,1024]{1,0:T(8,128)(2,1)}, u32[]{:S(2)}, u32[]{:S(2)}) collective-permute-start(bf16[640,1024]{1,0:T(8,128)(2,1)} %collective-permute-done.1.refs_3_), channel_id=1, source_target_pairs={{4,0},{6,2},{8,4},{10,6},{5,1},{7,3},{9,5},{11,7},{20,16},{22,18},... | collective-permute-start | bytes 3932168 | tf_op jit(solution)/shard_map/ppermute | solution.py:293
  71.9 22.1 %collective-permute-start.7 = (bf16[2048,128]{1,0:T(8,128)(2,1)}, bf16[2048,128]{1,0:T(8,128)(2,1)}, u32[]{:S(2)}, u32[]{:S(2)}) collective-permute-start(bf16[2048,128]{1,0:T(8,128)(2,1)} %pad_maximum_fusion.1), channel_id=1, source_target_pairs={{0,2},{2,0},{4,6},{6,4},{8,10},{10,8},{12,14},{14,12},{1,3},{3,1},... | collective-permute-start | bytes 1572872 | tf_op jit(solution)/shard_map/ppermute | solution.py:328
  116.0 21.4 %collective-permute-start.13 = (bf16[2048,1024]{1,0:T(8,128)(2,1)}, bf16[2048,1024]{1,0:T(8,128)(2,1)}, u32[]{:S(2)}, u32[]{:S(2)}) collective-permute-start(bf16[2048,1024]{1,0:T(8,128)(2,1)} %bitcast.30), channel_id=1, source_target_pairs={{0,1},{1,0},{2,3},{3,2},{4,5},{5,4},{6,7},{7,6},{8,9},{9,8},{10,11... | collective-permute-start | bytes 12582920 | tf_op jit(solution)/shard_map/ppermute | solution.py:299
  116.1 11.2 %collective-permute-start.11 = (bf16[1024,1024]{1,0:T(8,128)(2,1)S(1)}, bf16[1024,1024]{1,0:T(8,128)(2,1)}, u32[]{:S(2)}, u32[]{:S(2)}) collective-permute-start(bf16[1024,1024]{1,0:T(8,128)(2,1)S(1)} %collective-permute-done.8.refs_6_.refs_1_), channel_id=1, source_target_pairs={{0,1},{1,0},{2,3},{3,2},{4,5},{5,4},{6,7},{7,6},{8,9},{9,8},{10,11... | collective-permute-start | bytes 6291464 | tf_op jit(solution)/shard_map/ppermute | solution.py:299
  117.7 28.8 %collective-permute-start.10 = (bf16[640,1024]{1,0:T(8,128)(2,1)}, bf16[640,1024]{1,0:T(8,128)(2,1)S(1)}, u32[]{:S(2)}, u32[]{:S(2)}) collective-permute-start(bf16[640,1024]{1,0:T(8,128)(2,1)} %collective-permute-done.5.refs_2_), channel_id=1, source_target_pairs={{8,12},{10,14},{9,13},{11,15},{24,28},{26,30},{25,29},{27,31}} | collective-permute-start | bytes 3932168 | tf_op jit(solution)/shard_map/ppermute | solution.py:292
  118.5 38.0 %collective-permute-start.16 = (bf16[640,1024]{1,0:T(8,128)(2,1)}, bf16[640,1024]{1,0:T(8,128)(2,1)S(1)}, u32[]{:S(2)}, u32[]{:S(2)}) collective-permute-start(bf16[640,1024]{1,0:T(8,128)(2,1)} %collective-permute-done.6.refs_4_), channel_id=1, source_target_pairs={{4,0},{6,2},{5,1},{7,3},{20,16},{22,18},{21,17},{23,19}} | collective-permute-start | bytes 3932168 | tf_op jit(solution)/shard_map/ppermute | solution.py:293
  146.6 20.0 %collective-permute-start.14 = (bf16[384,1024]{1,0:T(8,128)(2,1)}, bf16[384,1024]{1,0:T(8,128)(2,1)S(1)}, u32[]{:S(2)}, u32[]{:S(2)}) collective-permute-start(bf16[384,1024]{1,0:T(8,128)(2,1)} %collective-permute-done.2.refs_1_), channel_id=1, source_target_pairs={{4,8},{6,10},{8,12},{10,14},{5,9},{7,11},{9,13},{11,15},{20,24},{2... | collective-permute-start | bytes 2359304 | tf_op jit(solution)/shard_map/ppermute | solution.py:292
  147.3 33.0 %collective-permute-start.15 = (bf16[384,1024]{1,0:T(8,128)(2,1)}, bf16[384,1024]{1,0:T(8,128)(2,1)}, u32[]{:S(2)}, u32[]{:S(2)}) collective-permute-start(bf16[384,1024]{1,0:T(8,128)(2,1)} %collective-permute-done.3.refs_3_), channel_id=1, source_target_pairs={{4,0},{6,2},{8,4},{10,6},{5,1},{7,3},{9,5},{11,7},{20,16},{22,18},... | collective-permute-start | bytes 2359304 | tf_op jit(solution)/shard_map/ppermute | solution.py:293
  165.0 40.4 %collective-permute-start.19 = (bf16[640,1024]{1,0:T(8,128)(2,1)}, bf16[640,1024]{1,0:T(8,128)(2,1)}, u32[]{:S(2)}, u32[]{:S(2)}) collective-permute-start(bf16[640,1024]{1,0:T(8,128)(2,1)} %get-tuple-element.67), channel_id=1, source_target_pairs={{0,2},{2,0},{4,6},{6,4},{8,10},{10,8},{12,14},{14,12},{1,3},{3,1},... | collective-permute-start | bytes 3932168 | tf_op jit(solution)/shard_map/ppermute | solution.py:509
  180.2 25.2 %collective-permute-start.17 = (bf16[384,1024]{1,0:T(8,128)(2,1)S(1)}, bf16[384,1024]{1,0:T(8,128)(2,1)}, u32[]{:S(2)}, u32[]{:S(2)}) collective-permute-start(bf16[384,1024]{1,0:T(8,128)(2,1)S(1)} %collective-permute-done.14.refs_2_), channel_id=1, source_target_pairs={{8,12},{10,14},{9,13},{11,15},{24,28},{26,30},{25,29},{27,31}} | collective-permute-start | bytes 2359304 | tf_op jit(solution)/shard_map/ppermute | solution.py:292
  181.8 23.6 %collective-permute-start.18 = (bf16[384,1024]{1,0:T(8,128)(2,1)}, bf16[384,1024]{1,0:T(8,128)(2,1)}, u32[]{:S(2)}, u32[]{:S(2)}) collective-permute-start(bf16[384,1024]{1,0:T(8,128)(2,1)} %collective-permute-done.15.refs_4_), channel_id=1, source_target_pairs={{4,0},{6,2},{5,1},{7,3},{20,16},{22,18},{21,17},{23,19}} | collective-permute-start | bytes 2359304 | tf_op jit(solution)/shard_map/ppermute | solution.py:293
  185.9 19.5 %all-to-all-start.1 = ((bf16[8,16,640]{2,1,0:T(8,128)(2,1)}), bf16[8,16,640]{2,1,0:T(8,128)(2,1)S(1)}, u32[]{:S(2)}, u32[]{:S(2)}) async-start(bf16[8,16,640]{2,1,0:T(8,128)(2,1)} %broadcast_in_dim.52), calls=%async_computation.1 | async-start | bytes 327680 | tf_op jit(solution)/shard_map/all_to_all | solution.py:435
  190.9 30.8 %collective-permute-start.20 = (bf16[512,1024]{1,0:T(8,128)(2,1)S(1)}, bf16[512,1024]{1,0:T(8,128)(2,1)S(1)}, u32[]{:S(2)}, u32[]{:S(2)}) collective-permute-start(bf16[512,1024]{1,0:T(8,128)(2,1)S(1)} %bitcast.35), channel_id=1, source_target_pairs={{0,1},{1,0},{2,3},{3,2},{4,5},{5,4},{6,7},{7,6},{8,9},{9,8},{10,11... | collective-permute-start | bytes 3145736 | tf_op jit(solution)/shard_map/ppermute | solution.py:299
  211.3 29.2 %collective-permute-start.21 = (bf16[384,1024]{1,0:T(8,128)(2,1)}, bf16[384,1024]{1,0:T(8,128)(2,1)}, u32[]{:S(2)}, u32[]{:S(2)}) collective-permute-start(bf16[384,1024]{1,0:T(8,128)(2,1)} %get-tuple-element.76), channel_id=1, source_target_pairs={{0,2},{2,0},{4,6},{6,4},{8,10},{10,8},{12,14},{14,12},{1,3},{3,1},... | collective-permute-start | bytes 2359304 | tf_op jit(solution)/shard_map/ppermute | solution.py:517
  215.9 16.8 %all-to-all-start.2 = ((bf16[8,16,384]{2,1,0:T(8,128)(2,1)}), bf16[8,16,384]{2,1,0:T(8,128)(2,1)S(1)}, u32[]{:S(2)}, u32[]{:S(2)}) async-start(bf16[8,16,384]{2,1,0:T(8,128)(2,1)} %broadcast_in_dim.53), calls=%async_computation.2 | async-start | bytes 196608 | tf_op jit(solution)/shard_map/all_to_all | solution.py:435
  (16 other events, 267.2 us)

commit v4 on v3

--- a/solution.py
+++ b/solution.py
@@ -1,3 +1,5 @@
+import functools
+
 import jax
 import jax.numpy as jnp
 from jax import lax
@@ -7,7 +9,6 @@
 
 ADAPTER_RANK = 16
 ROW_CHUNKS = (640, 384)
-ROW_STEP = 128
 SOURCES = 6
 VMEM_BYTES = 56 * 1024 * 1024
 
@@ -115,26 +116,28 @@
                 total[...] += term
 
 
-def rest_kernel(farthest, total, block, other, *refs):
-    pieces, refs = refs[:4], refs[4:]
-    factors, refs = refs[:3], refs[3:]
-    stored, adapter, fold, partial, shrunk, weight, sems = refs
+def rest_kernel(farthest, *refs):
+    total, blocks, pieces, factors, refs = refs[0], refs[1:3], refs[3:7], refs[7:10], refs[10:]
+    stored, adapter, fold, partial, shrunk, sums, line, weight, sems = refs
     depth, width = pieces[0].shape
     columns = factors[0].shape[1]
     own_rows = pl.ds(pl.multiple_of(farthest[0] * depth, depth), depth)
     tail_rows = pl.ds(pl.multiple_of(lax.rem(farthest[0], 2) * depth, depth), depth)
+    lines = [pltpu.make_async_copy(v, line.at[q], sems.at[q]) for q, v in enumerate(blocks)]
 
     def arrive(piece, tail):
         return [
-            pltpu.make_async_copy(piece, weight.at[:, pl.ds(0, width)], sems.at[0]),
+            pltpu.make_async_copy(piece, weight.at[:, pl.ds(0, width)], sems.at[2]),
             pltpu.make_async_copy(
-                factors[0].at[own_rows], weight.at[:, pl.ds(width, columns)], sems.at[1]
+                factors[0].at[own_rows], weight.at[:, pl.ds(width, columns)], sems.at[3]
             ),
             pltpu.make_async_copy(
-                tail.at[tail_rows], weight.at[:, pl.ds(width + columns, columns)], sems.at[2]
+                tail.at[tail_rows], weight.at[:, pl.ds(width + columns, columns)], sems.at[4]
             ),
         ]
 
+    for copy in lines:
+        copy.start()
     for number, piece in enumerate(pieces):
 
         @pl.when(farthest[0] == number)
@@ -142,15 +145,19 @@
             for copy in arrive(piece, factors[1 + number // 2]):
                 copy.start()
 
-    for copy in arrive(pieces[0], factors[1]):
+    before = pltpu.make_async_copy(total, sums, sems.at[5])
+    before.start()
+    for copy in lines + arrive(pieces[0], factors[1]):
         copy.wait()
-    full = total[...] + dot(block[...] + other[...], weight[...])
+    term = dot(line[0] + line[1], weight[...])
+    before.wait()
+    full = sums[...] + term
     partial[...] = full[:, :width].astype(partial.dtype)
     kept = jnp.where(stored[...] == adapter[...], full[:, width:], 0.0).astype(jnp.bfloat16)
     across = (((1,), (1,)), ((), ()))
-    shrunk[...] = lax.dot_general(
-        fold[...], kept, across, preferred_element_type=jnp.float32
-    ).astype(shrunk.dtype)
+    small = lax.dot_general(fold[...], kept, across, preferred_element_type=jnp.float32)
+    for q in range(shrunk.shape[0]):
+        shrunk[q] = small.astype(shrunk.dtype)
 
 
 def own_kernel(sel, place, *refs):
@@ -192,33 +199,48 @@
                 base[...] += term
 
 
-def lora_kernel(farthest, base, everyone, stored, adapter, unfold, *refs):
-    expand, (block, other), weights, refs = refs[:2], refs[2:4], refs[4:6], refs[6:]
-    partials, (out, weight, sem) = refs[:-3], refs[-3:]
+def last_kernel(start, farthest, everyone, stored, adapter, unfold, *refs):
+    base, partial, expand, blocks, weights, refs = (
+        refs[0], refs[1], refs[2:4], refs[4:6], refs[6:8], refs[8:],
+    )
+    out, sums, added, factor, line, weight, result, sems = refs[-8:]
     depth = weight.shape[0]
     rows = pl.ds(pl.multiple_of(farthest[0] * depth, depth), depth)
+    factors = [pltpu.make_async_copy(v, factor.at[q], sems.at[q]) for q, v in enumerate(expand)]
+    lines = [pltpu.make_async_copy(v, line.at[q], sems.at[2 + q]) for q, v in enumerate(blocks)]
+    others = [
+        pltpu.make_async_copy(base, sums, sems.at[5]),
+        pltpu.make_async_copy(partial, added, sems.at[6]),
+    ]
+    for copy in factors + lines:
+        copy.start()
     for number, half in enumerate(weights):
 
         @pl.when(farthest[1] == number)
         def _():
-            pltpu.make_async_copy(half.at[rows], weight, sem).start()
-
+            pltpu.make_async_copy(half.at[rows], weight, sems.at[4]).start()
+
+    for copy in others:
+        copy.start()
     shrunk = jnp.sum(everyone[...].astype(jnp.float32), axis=0).astype(jnp.bfloat16)
     spread = lax.dot_general(
         shrunk, unfold[...], (((0,), (0,)), ((), ())), preferred_element_type=jnp.float32
     )
     spread = jnp.where(stored[...] == adapter[...], spread, 0.0).astype(jnp.bfloat16)
     half = spread.shape[1] // 2
-    added = dot(spread[:, :half], expand[0][...]) + dot(spread[:, half:], expand[1][...])
-    pltpu.make_async_copy(weights[0].at[rows], weight, sem).wait()
-    added = base[...] + added + dot(block[...] + other[...], weight[...])
-    for partial in partials:
-        added += partial[...].astype(jnp.float32)
-    out[...] = added.astype(out.dtype)
-
-
-def sum_kernel(base, partial, *refs):
-    refs[-1][...] = (base[...] + partial[...].astype(jnp.float32)).astype(jnp.bfloat16)
+    for copy in factors:
+        copy.wait()
+    total = dot(spread[:, :half], factor[0]) + dot(spread[:, half:], factor[1])
+    for copy in lines:
+        copy.wait()
+    pltpu.make_async_copy(weights[0].at[rows], weight, sems.at[4]).wait()
+    total += dot(line[0] + line[1], weight[...])
+    for copy in others:
+        copy.wait()
+    result[...] = (total + sums[...] + added[...].astype(jnp.float32)).astype(result.dtype)
+    copy = pltpu.make_async_copy(result, out.at[pl.ds(start, result.shape[0])], sems.at[7])
+    copy.start()
+    copy.wait()
 
 
 def whole(shape):
@@ -392,20 +414,21 @@
         small = [stored[starts[c] : starts[c] + count], column_adapter, fold]
         outs = [
             jax.ShapeDtypeStruct((count, width), jnp.bfloat16),
-            jax.ShapeDtypeStruct((ADAPTER_RANK, count), jnp.bfloat16),
+            jax.ShapeDtypeStruct((tp, ADAPTER_RANK, count), jnp.bfloat16),
         ]
         return pl.pallas_call(
             rest_kernel,
             grid_spec=pltpu.PrefetchScalarGridSpec(
                 num_scalar_prefetch=1,
                 grid=(1,),
-                in_specs=[whole(total.shape), whole((count, depth)), whole((count, depth))]
-                + [pl.BlockSpec(memory_space=pl.ANY) for _ in range(7)]
+                in_specs=[pl.BlockSpec(memory_space=pl.ANY) for _ in range(10)]
                 + [whole(v.shape) for v in small],
                 out_specs=[whole(o.shape) for o in outs],
                 scratch_shapes=[
+                    pltpu.VMEM((count, total_columns), jnp.float32),
+                    pltpu.VMEM((2, count, depth), jnp.bfloat16),
                     pltpu.VMEM((depth, total_columns), jnp.bfloat16),
-                    pltpu.SemaphoreType.DMA((3,)),
+                    pltpu.SemaphoreType.DMA((6,)),
                 ],
             ),
             out_shape=outs,
@@ -431,72 +454,52 @@
         )[0]
 
     def spread_out(shrunk):
-        everyone = jnp.broadcast_to(shrunk[None], (tp,) + shrunk.shape)
-        return lax.all_to_all(everyone, "tp", split_axis=0, concat_axis=0, tiled=True)
-
-    def lora_part(c, base, everyone, expand, partial=None):
+        return lax.all_to_all(shrunk, "tp", split_axis=0, concat_axis=0, tiled=True)
+
+    def last_part(c, base, partial, everyone, expand, earlier):
         count = ROW_CHUNKS[c]
-        rows_of = whole((count, width))
-        partials = [] if partial is None else [partial]
-        out = (count, width, jnp.float32) if partial is None else (rows, width, jnp.bfloat16)
+        hbm = [base, partial, *expand, *longest(c), *weight_own]
+        aliases = {}
+        if earlier is not None:
+            aliases = {5 + len(hbm): 0}
+            hbm.append(earlier)
         return pl.pallas_call(
-            lora_kernel,
+            functools.partial(last_kernel, starts[c]),
             grid_spec=pltpu.PrefetchScalarGridSpec(
                 num_scalar_prefetch=1,
                 grid=(1,),
                 in_specs=[
-                    rows_of,
                     whole(everyone.shape),
                     whole((count, 1)),
                     whole(entry_adapter.shape),
                     whole(unfold.shape),
-                    whole(expand[0].shape),
-                    whole(expand[1].shape),
-                    whole((count, depth)),
-                    whole((count, depth)),
                 ]
-                + [pl.BlockSpec(memory_space=pl.ANY)] * 2
-                + [rows_of for _ in partials],
-                out_specs=rows_of,
-                scratch_shapes=[pltpu.VMEM((depth, width), jnp.bfloat16), pltpu.SemaphoreType.DMA],
-            ),
-            out_shape=jax.ShapeDtypeStruct(out[:2], out[2]),
+                + [pl.BlockSpec(memory_space=pl.ANY) for _ in hbm],
+                out_specs=pl.BlockSpec(memory_space=pl.ANY),
+                scratch_shapes=[
+                    pltpu.VMEM((count, width), jnp.float32),
+                    pltpu.VMEM((count, width), jnp.bfloat16),
+                    pltpu.VMEM((2,) + expand[0].shape, jnp.bfloat16),
+                    pltpu.VMEM((2, count, depth), jnp.bfloat16),
+                    pltpu.VMEM((depth, width), jnp.bfloat16),
+                    pltpu.VMEM((count, width), jnp.bfloat16),
+                    pltpu.SemaphoreType.DMA((8,)),
+                ],
+            ),
+            out_shape=jax.ShapeDtypeStruct((rows, width), jnp.bfloat16),
+            input_output_aliases=aliases,
             compiler_params=pltpu.CompilerParams(vmem_limit_bytes=VMEM_BYTES),
             cost_estimate=pl.CostEstimate(
                 flops=4 * count * width * depth, bytes_accessed=4 * depth * width, transcendentals=0
             ),
         )(
             farthest_own,
-            base,
             everyone,
             stored[starts[c] : starts[c] + count],
             entry_adapter,
             unfold,
-            *expand,
-            *longest(c),
-            *weight_own,
-            *partials,
+            *hbm,
         )
-
-    def sum_part(c, base, partial, earlier):
-        count, step = ROW_CHUNKS[c], ROW_STEP
-        here = starts[c] // step
-        rows_of = pl.BlockSpec((step, width), lambda i: (i, 0))
-        operands = [base, partial, earlier]
-        specs = [rows_of, rows_of, pl.BlockSpec(memory_space=pl.ANY)]
-        aliases = {2: 0}
-        return pl.pallas_call(
-            sum_kernel,
-            grid=(count // step,),
-            in_specs=specs,
-            out_specs=pl.BlockSpec((step, width), lambda i: (i + here, 0)),
-            out_shape=jax.ShapeDtypeStruct((rows, width), jnp.bfloat16),
-            input_output_aliases=aliases,
-            compiler_params=pltpu.CompilerParams(vmem_limit_bytes=VMEM_BYTES),
-            cost_estimate=pl.CostEstimate(
-                flops=2 * count * width, bytes_accessed=8 * count * width, transcendentals=0
-            ),
-        )(*operands)
 
     early_a = early_part(0)
     base_a = own_part(0, early_a)
@@ -516,9 +519,8 @@
     partial_c, shrunk_c = rest_part(1, early_c)
     got_c = lax.ppermute(partial_c, "tp", across)
     everyone_c = spread_out(shrunk_c)
-    out = lora_part(0, base_a, everyone_a, expand, got_a)
-    whole_c = lora_part(1, base_c, everyone_c, expand)
-    return sum_part(1, whole_c, got_c, out)
+    out = last_part(0, base_a, got_a, everyone_a, expand, None)
+    return last_part(1, base_c, got_c, everyone_c, expand, out)
 
 
 def solution(mesh):

time: 246 us -> 240 us (0.976)
  Pallas kernels: 66.1 us -> 61.1 us
  waiting for transfers between devices: 101 us -> 105 us
  local copies, waits for them, and re-layouts: 22.2 us -> 19.4 us
    pallas_call x3 -> x2, Pallas kernels: 19.3 us -> 14.3 us  [last_part(): pl.pallas_call(functools.partial(last_kernel, starts[c]), grid_spec=pltpu...]
    all_to_all x2, waiting for transfers between devices: 1.08 us -> 4.96 us  [spread_out(): return lax.all_to_all(shrunk, 'tp', split_axis=0, concat_axis=0, tiled=True)]
    broadcast_in_dim x2 -> x0, local copies, waits for them, and re-layouts: 2.76 us -> none  [spread_out(): everyone = jnp.broadcast_to(shrunk[None], (tp,) + shrunk.shape)]
  transfers between devices with their start and end apart: 25 -> 25, of which waited for: 8 -> 9; matrix products, arithmetic and copies ran while one was open for 9% -> 8% of each run, Pallas kernels for 26% -> 23%
where the time goes in v4:
time: 240 us; the launch traced here: 238 us
  waiting for transfers between devices  105 us (44%)
  Pallas kernels  61.1 us (25%)
  starting transfers between devices  45.6 us (19%)
  local copies, waits for them, and re-layouts  19.4 us (8%)
  other arithmetic  6.23 us (3%)
    ppermute x6, waiting for transfers between devices, hop(): downs[c][h] = lax.ppermute(downs[c][h - 1], 'tp', down(h))  48.4 us
    pallas_call x4, Pallas kernels, on_line(): pl.pallas_call(kernel, grid_spec=pltpu.PrefetchScalarGridSpec(num_scalar_...  33.8 us
    ppermute x6, waiting for transfers between devices, hop(): ups[c][h] = lax.ppermute(ups[c][h - 1], 'tp', up(h))  30.8 us
    ppermute x6, starting transfers between devices, hop(): ups[c][h] = lax.ppermute(ups[c][h - 1], 'tp', up(h))  14.7 us
    pallas_call x2, Pallas kernels, last_part(): pl.pallas_call(functools.partial(last_kernel, starts[c]), grid_spec=pltpu...  14.3 us
    ppermute x1, waiting for transfers between devices, line_body(): shrink_near = lax.ppermute(leaving, 'tp', across)  14.2 us
    pallas_call x2, Pallas kernels, rest_part(): pl.pallas_call(rest_kernel, grid_spec=pltpu.PrefetchScalarGridSpec(num_sc...  13 us
    all_to_all x2, starting transfers between devices, spread_out(): return lax.all_to_all(shrunk, 'tp', split_axis=0, concat_axis=0, tiled=True)  9.69 us
  transfers between devices with their start and end apart: 25, of which 9 were waited for; matrix products, arithmetic and copies ran while one was open for 8% of the time, Pallas kernels for 23%

profile of v4, /device:TPU:0, one launch (start us, length us, event | category | flops | bytes accessed | tf_op | source)
XLA Modules:
  0.0 238.3 jit_solution(3309381012077965753)
XLA Ops:
  0.0 3.2 %dynamic-slice_bitcast_fusion = bf16[1024,1024]{1,0:T(8,128)(2,1)} fusion(bf16[4,1024,1024]{2,1,0:T(8,128)(2,1)} %bitcast.38, s32[]{:T(128)S(6)} %select_n.237), kind=kLoop, calls=%fused_computation | loop fusion | bytes 4194308 | tf_op jit(solution)/shard_map/jit(dynamic_index_in_dim)/squeeze | solution.py:67
  3.2 2.9 %collective-permute-start.4 = (bf16[1024,1024]{1,0:T(8,128)(2,1)}, bf16[1024,1024]{1,0:T(8,128)(2,1)}, u32[]{:S(2)}, u32[]{:S(2)}) collective-permute-start(bf16[1024,1024]{1,0:T(8,128)(2,1)} %dynamic-slice_bitcast_fusion), channel_id=1, source_target_pairs={{0,2},{2,0},{4,6},{6,4},{8,10},{10,8},{12,14},{14,12},{1,3},{3,1},... | collective-permute-start | bytes 6291464 | tf_op jit(solution)/shard_map/ppermute | solution.py:339
  7.4 4.5 %collective-permute-start = (bf16[640,1024]{1,0:T(8,128)(2,1)}, bf16[640,1024]{1,0:T(8,128)(2,1)}, u32[]{:S(2)}, u32[]{:S(2)}) collective-permute-start(bf16[640,1024]{1,0:T(8,128)(2,1)} %slice.20.refs_0_), channel_id=1, source_target_pairs={{0,4},{2,6},{4,8},{6,10},{8,12},{10,14},{1,5},{3,7},{5,9},{7,11},{... | collective-permute-start | bytes 3932168 | tf_op jit(solution)/shard_map/ppermute | solution.py:314
  13.3 5.4 %collective-permute-start.2 = (bf16[384,1024]{1,0:T(8,128)(2,1)S(1)}, bf16[384,1024]{1,0:T(8,128)(2,1)}, u32[]{:S(2)}, u32[]{:S(2)}) collective-permute-start(bf16[384,1024]{1,0:T(8,128)(2,1)S(1)} %slice.21.refs_0_), channel_id=1, source_target_pairs={{0,4},{2,6},{4,8},{6,10},{8,12},{10,14},{1,5},{3,7},{5,9},{7,11},{... | collective-permute-start | bytes 2359304 | tf_op jit(solution)/shard_map/ppermute | solution.py:314
  24.8 30.8 %collective-permute-done.2.refs_1_ = bf16[384,1024]{1,0:T(8,128)(2,1)} collective-permute-done((bf16[384,1024]{1,0:T(8,128)(2,1)S(1)}, bf16[384,1024]{1,0:T(8,128)(2,1)}, u32[]{:S(2)}, u32[]{:S(2)}) %collective-permute-start.2) | collective-permute-done | bytes 786464 | tf_op jit(solution)/shard_map/ppermute | solution.py:314
  55.7 5.3 %collective-permute-done.3.refs_3_ = bf16[384,1024]{1,0:T(8,128)(2,1)} collective-permute-done((bf16[384,1024]{1,0:T(8,128)(2,1)S(1)}, bf16[384,1024]{1,0:T(8,128)(2,1)}, u32[]{:S(2)}, u32[]{:S(2)}) %collective-permute-start.3) | collective-permute-done | bytes 786464 | tf_op jit(solution)/shard_map/ppermute | solution.py:315
  64.1 3.6 %all-to-all-start = ((bf16[8,64,1024]{2,1,0:T(8,128)(2,1)}), bf16[8,64,1024]{2,1,0:T(8,128)(2,1)S(1)}, u32[]{:S(2)}, u32[]{:S(2)}) async-start(bf16[8,64,1024]{2,1,0:T(8,128)(2,1)} %copy.21), calls=%async_computation | async-start | bytes 2097152 | tf_op jit(solution)/shard_map/all_to_all | solution.py:355
  73.8 4.7 %constant_dynamic-slice_fusion = bf16[2,1,1024,1024]{3,2,1,0:T(8,128)(2,1)} fusion(bf16[2,2,1024,1024]{3,2,1,0:T(8,128)(2,1)} %bitcast.39, s32[]{:T(128)S(6)} %select_n.245), kind=kLoop, calls=%fused_computation.40 | loop fusion | bytes 8388612 | tf_op jit(solution)/shard_map/jit(dynamic_index_in_dim)/dynamic_slice | solution.py:353
  79.7 14.2 %collective-permute-done.7.refs_10_.refs_8_ = bf16[2048,128]{1,0:T(8,128)(2,1)} collective-permute-done((bf16[2048,128]{1,0:T(8,128)(2,1)}, bf16[2048,128]{1,0:T(8,128)(2,1)}, u32[]{:S(2)}, u32[]{:S(2)}) %collective-permute-start.7) | collective-permute-done | bytes 524320 | tf_op jit(solution)/shard_map/ppermute | solution.py:350
  94.0 22.0 %collective-permute-done.6.refs_4_ = bf16[640,1024]{1,0:T(8,128)(2,1)} collective-permute-done((bf16[640,1024]{1,0:T(8,128)(2,1)}, bf16[640,1024]{1,0:T(8,128)(2,1)}, u32[]{:S(2)}, u32[]{:S(2)}) %collective-permute-start.6) | collective-permute-done | bytes 1310752 | tf_op jit(solution)/shard_map/ppermute | solution.py:315
  120.4 6.9 %collective-permute-done.12.refs_11_.refs_9_ = bf16[2048,128]{1,0:T(8,128)(2,1)} collective-permute-done((bf16[2048,128]{1,0:T(8,128)(2,1)}, bf16[2048,128]{1,0:T(8,128)(2,1)}, u32[]{:S(2)}, u32[]{:S(2)}) %collective-permute-start.12) | collective-permute-done | bytes 524320 | tf_op jit(solution)/shard_map/ppermute | solution.py:321
  127.3 10.1 %shard_map.64.refs_0_ = f32[640,1280]{1,0:T(8,128)} custom-call(s32[4]{0:T(128)} %get-tuple-element.70.sel, s32[4]{0:T(128)} %get-tuple-element.51.place, bf16[640,1024]{1,0:T(8,128)(2,1)} %slice.20.refs_0_, bf16[640,1024]{1,0:T(8,128)(2,1)} %collective-permute-done.refs_1_, bf16[640,1024]{1,0:T(8,128)(2,1)} %collective-permute-done.5.refs_2_, ...), custom_call_target="tpu_custom_call" | custom-call | flops 5368709120 | bytes 16252928 | tf_op jit(solution)/shard_map/pallas_call | solution.py:256
  137.4 9.1 %shard_map.65.refs_0_ = f32[640,1024]{1,0:T(8,128)} custom-call(s32[4]{0:T(128)} %get-tuple-element.70.sel, s32[4]{0:T(128)} %fusion.14.place, bf16[640,1024]{1,0:T(8,128)(2,1)} %slice.20.refs_0_, bf16[640,1024]{1,0:T(8,128)(2,1)} %collective-permute-done.refs_1_, bf16[640,1024]{1,0:T(8,128)(2,1)} %collective-permute-done.5.refs_2_, ...), custom_call_target="tpu_custom_call" | custom-call | flops 5368709120 | bytes 16252928 | tf_op jit(solution)/shard_map/pallas_call | solution.py:256
  149.2 7.3 %collective-permute-done.16.refs_2_.refs_5_ = bf16[640,1024]{1,0:T(8,128)(2,1)S(1)} collective-permute-done((bf16[640,1024]{1,0:T(8,128)(2,1)}, bf16[640,1024]{1,0:T(8,128)(2,1)S(1)}, u32[]{:S(2)}, u32[]{:S(2)}) %collective-permute-start.16) | collective-permute-done | bytes 1310752 | tf_op jit(solution)/shard_map/ppermute | solution.py:315
  157.6 7.2 %shard_map.66 = (bf16[640,1024]{1,0:T(8,128)(2,1)}, bf16[8,16,640]{2,1,0:T(8,128)(2,1)}) custom-call(s32[1]{0:T(128)} %bitcast.2.farthest, f32[640,1280]{1,0:T(8,128)} %shard_map.64.refs_0_, bf16[640,1024]{1,0:T(8,128)(2,1)} %copy-done.5, bf16[640,1024]{1,0:T(8,128)(2,1)} %copy-done.6, bf16[1024,1024]{1,0:T(8,128)(2,1)} %collective-permute-done.4.refs_5_.refs_3_, ...), custom_call_target="tpu_custom_call" | custom-call | flops 1677721600 | bytes 4194304 | tf_op jit(solution)/shard_map/pallas_call | solution.py:419
  166.4 13.8 %collective-permute-done.15.refs_4_ = bf16[384,1024]{1,0:T(8,128)(2,1)} collective-permute-done((bf16[384,1024]{1,0:T(8,128)(2,1)}, bf16[384,1024]{1,0:T(8,128)(2,1)}, u32[]{:S(2)}, u32[]{:S(2)}) %collective-permute-start.15) | collective-permute-done | bytes 786464 | tf_op jit(solution)/shard_map/ppermute | solution.py:315
  183.9 4.9 %all-to-all-start.1 = ((bf16[8,16,640]{2,1,0:T(8,128)(2,1)}), bf16[8,16,640]{2,1,0:T(8,128)(2,1)S(1)}, u32[]{:S(2)}, u32[]{:S(2)}) async-start(bf16[8,16,640]{2,1,0:T(8,128)(2,1)} %get-tuple-element.71), calls=%async_computation.1 | async-start | bytes 327680 | tf_op jit(solution)/shard_map/all_to_all | solution.py:457
  188.9 7.6 %shard_map.67.refs_0_ = f32[384,1280]{1,0:T(8,128)} custom-call(s32[4]{0:T(128)} %get-tuple-element.70.sel, s32[4]{0:T(128)} %get-tuple-element.51.place, bf16[384,1024]{1,0:T(8,128)(2,1)} %copy-done.4, bf16[384,1024]{1,0:T(8,128)(2,1)} %collective-permute-done.2.refs_1_, bf16[384,1024]{1,0:T(8,128)(2,1)} %copy-done.8, ...), custom_call_target="tpu_custom_call" | custom-call | flops 3221225472 | bytes 13107200 | tf_op jit(solution)/shard_map/pallas_call | solution.py:256
  196.5 7.0 %shard_map.68.refs_0_ = f32[384,1024]{1,0:T(8,128)} custom-call(s32[4]{0:T(128)} %get-tuple-element.70.sel, s32[4]{0:T(128)} %fusion.14.place, bf16[384,1024]{1,0:T(8,128)(2,1)} %copy-done.4, bf16[384,1024]{1,0:T(8,128)(2,1)} %collective-permute-done.2.refs_1_, bf16[384,1024]{1,0:T(8,128)(2,1)} %copy-done.8, ...), custom_call_target="tpu_custom_call" | custom-call | flops 3221225472 | bytes 13107200 | tf_op jit(solution)/shard_map/pallas_call | solution.py:256
  205.4 5.7 %shard_map.69 = (bf16[384,1024]{1,0:T(8,128)(2,1)}, bf16[8,16,384]{2,1,0:T(8,128)(2,1)}) custom-call(s32[1]{0:T(128)} %bitcast.2.farthest, f32[384,1280]{1,0:T(8,128)} %shard_map.67.refs_0_, bf16[384,1024]{1,0:T(8,128)(2,1)} %collective-permute-done.17.refs_1_.refs_4_, bf16[384,1024]{1,0:T(8,128)(2,1)} %collective-permute-done.18.refs_2_.refs_5_, ...), custom_call_target="tpu_custom_call" | custom-call | flops 1006632960 | bytes 4194304 | tf_op jit(solution)/shard_map/pallas_call | solution.py:419
  214.2 4.8 %all-to-all-start.2 = ((bf16[8,16,384]{2,1,0:T(8,128)(2,1)}), bf16[8,16,384]{2,1,0:T(8,128)(2,1)S(1)}, u32[]{:S(2)}, u32[]{:S(2)}) async-start(bf16[8,16,384]{2,1,0:T(8,128)(2,1)} %get-tuple-element.74), calls=%async_computation.2 | async-start | bytes 196608 | tf_op jit(solution)/shard_map/all_to_all | solution.py:457
  220.0 7.7 %shard_map.70.refs_8_ = bf16[1024,1024]{1,0:T(8,128)(2,1)} custom-call(s32[2]{0:T(128)} %pad_add_fusion.farthest, bf16[8,16,640]{2,1,0:T(8,128)(2,1)} %copy-done.11, s32[640,1]{1,0:T(8,128)} %slice.26.refs_10_.stored, s32[1,1024]{1,0:T(1,128)} %fusion.7.adapter, bf16[16,1024]{1,0:T(8,128)(2,1)} %fusion.unfold, f32[640,1024]{1,0:T(8,128)} %shard_map.65.refs_0_, ...), custom_call_target="tpu_custom_call" | custom-call | flops 2684354560 | bytes 4194304 | tf_op jit(solution)/shard_map/pallas_call | solution.py:466
  227.7 3.1 %all-to-all-done.2.everyone = bf16[8,16,384]{2,1,0:T(8,128)(2,1)S(1)} async-done(((bf16[8,16,384]{2,1,0:T(8,128)(2,1)}), bf16[8,16,384]{2,1,0:T(8,128)(2,1)S(1)}, u32[]{:S(2)}, u32[]{:S(2)}) %all-to-all-start.2) | async-done | bytes 98336 | tf_op jit(solution)/shard_map/all_to_all | solution.py:457
  231.5 6.6 %shard_map.71 = bf16[1024,1024]{1,0:T(8,128)(2,1)} custom-call(s32[2]{0:T(128)} %pad_add_fusion.farthest, bf16[8,16,384]{2,1,0:T(8,128)(2,1)} %copy-done.12, s32[384,1]{1,0:T(8,128)} %slice.27.refs_10_.stored, s32[1,1024]{1,0:T(1,128)} %fusion.7.adapter, bf16[16,1024]{1,0:T(8,128)(2,1)} %fusion.unfold, ...), custom_call_target="tpu_custom_call", output_to_operand_aliasing={{}: (13, {})} | custom-call | flops 1610612736 | bytes 4194304 | tf_op jit(solution)/shard_map/pallas_call | solution.py:466
  (88 shorter events, 39.0 us)
Async XLA Ops:
  3.2 57.7 %collective-permute-start.4 = (bf16[1024,1024]{1,0:T(8,128)(2,1)}, bf16[1024,1024]{1,0:T(8,128)(2,1)}, u32[]{:S(2)}, u32[]{:S(2)}) collective-permute-start(bf16[1024,1024]{1,0:T(8,128)(2,1)} %dynamic-slice_bitcast_fusion), channel_id=1, source_target_pairs={{0,2},{2,0},{4,6},{6,4},{8,10},{10,8},{12,14},{14,12},{1,3},{3,1},... | collective-permute-start | bytes 6291464 | tf_op jit(solution)/shard_map/ppermute | solution.py:339
  7.4 53.6 %collective-permute-start = (bf16[640,1024]{1,0:T(8,128)(2,1)}, bf16[640,1024]{1,0:T(8,128)(2,1)}, u32[]{:S(2)}, u32[]{:S(2)}) collective-permute-start(bf16[640,1024]{1,0:T(8,128)(2,1)} %slice.20.refs_0_), channel_id=1, source_target_pairs={{0,4},{2,6},{4,8},{6,10},{8,12},{10,14},{1,5},{3,7},{5,9},{7,11},{... | collective-permute-start | bytes 3932168 | tf_op jit(solution)/shard_map/ppermute | solution.py:314
  11.9 49.0 %collective-permute-start.1 = (bf16[640,1024]{1,0:T(8,128)(2,1)}, bf16[640,1024]{1,0:T(8,128)(2,1)}, u32[]{:S(2)}, u32[]{:S(2)}) collective-permute-start(bf16[640,1024]{1,0:T(8,128)(2,1)} %slice.20.refs_0_), channel_id=1, source_target_pairs={{4,0},{6,2},{8,4},{10,6},{12,8},{14,10},{5,1},{7,3},{9,5},{11,7},{... | collective-permute-start | bytes 3932168 | tf_op jit(solution)/shard_map/ppermute | solution.py:315
  13.3 42.4 %collective-permute-start.2 = (bf16[384,1024]{1,0:T(8,128)(2,1)S(1)}, bf16[384,1024]{1,0:T(8,128)(2,1)}, u32[]{:S(2)}, u32[]{:S(2)}) collective-permute-start(bf16[384,1024]{1,0:T(8,128)(2,1)S(1)} %slice.21.refs_0_), channel_id=1, source_target_pairs={{0,4},{2,6},{4,8},{6,10},{8,12},{10,14},{1,5},{3,7},{5,9},{7,11},{... | collective-permute-start | bytes 2359304 | tf_op jit(solution)/shard_map/ppermute | solution.py:314
  18.7 42.2 %collective-permute-start.3 = (bf16[384,1024]{1,0:T(8,128)(2,1)S(1)}, bf16[384,1024]{1,0:T(8,128)(2,1)}, u32[]{:S(2)}, u32[]{:S(2)}) collective-permute-start(bf16[384,1024]{1,0:T(8,128)(2,1)S(1)} %slice.21.refs_0_), channel_id=1, source_target_pairs={{4,0},{6,2},{8,4},{10,6},{12,8},{14,10},{5,1},{7,3},{9,5},{11,7},{... | collective-permute-start | bytes 2359304 | tf_op jit(solution)/shard_map/ppermute | solution.py:315
  61.0 55.0 %collective-permute-start.8 = (bf16[1024,1024]{1,0:T(8,128)(2,1)}, bf16[1024,1024]{1,0:T(8,128)(2,1)S(1)}, u32[]{:S(2)}, u32[]{:S(2)}) collective-permute-start(bf16[1024,1024]{1,0:T(8,128)(2,1)} %collective-permute-done.4.refs_5_.refs_3_), channel_id=1, source_target_pairs={{0,16},{16,0},{1,17},{17,1},{2,18},{18,2},{3,19},{19,3},{4,20},{20... | collective-permute-start | bytes 6291464 | tf_op jit(solution)/shard_map/ppermute | solution.py:349
  62.5 53.4 %collective-permute-start.9 = (bf16[1024,1024]{1,0:T(8,128)(2,1)}, bf16[1024,1024]{1,0:T(8,128)(2,1)}, u32[]{:S(2)}, u32[]{:S(2)}) collective-permute-start(bf16[1024,1024]{1,0:T(8,128)(2,1)} %collective-permute-done.4.refs_5_.refs_3_), channel_id=1, source_target_pairs={{0,1},{1,0},{2,3},{3,2},{4,5},{5,4},{6,7},{7,6},{8,9},{9,8},{10,11... | collective-permute-start | bytes 6291464 | tf_op jit(solution)/shard_map/ppermute | solution.py:321
  64.1 51.9 %all-to-all-start = ((bf16[8,64,1024]{2,1,0:T(8,128)(2,1)}), bf16[8,64,1024]{2,1,0:T(8,128)(2,1)S(1)}, u32[]{:S(2)}, u32[]{:S(2)}) async-start(bf16[8,64,1024]{2,1,0:T(8,128)(2,1)} %copy.21), calls=%async_computation | async-start | bytes 2097152 | tf_op jit(solution)/shard_map/all_to_all | solution.py:355
  67.7 26.3 %collective-permute-start.5 = (bf16[640,1024]{1,0:T(8,128)(2,1)}, bf16[640,1024]{1,0:T(8,128)(2,1)}, u32[]{:S(2)}, u32[]{:S(2)}) collective-permute-start(bf16[640,1024]{1,0:T(8,128)(2,1)} %collective-permute-done.refs_1_), channel_id=1, source_target_pairs={{4,8},{6,10},{8,12},{10,14},{5,9},{7,11},{9,13},{11,15},{20,24},{2... | collective-permute-start | bytes 3932168 | tf_op jit(solution)/shard_map/ppermute | solution.py:314
  69.4 46.6 %collective-permute-start.6 = (bf16[640,1024]{1,0:T(8,128)(2,1)}, bf16[640,1024]{1,0:T(8,128)(2,1)}, u32[]{:S(2)}, u32[]{:S(2)}) collective-permute-start(bf16[640,1024]{1,0:T(8,128)(2,1)} %collective-permute-done.1.refs_3_), channel_id=1, source_target_pairs={{4,0},{6,2},{8,4},{10,6},{5,1},{7,3},{9,5},{11,7},{20,16},{22,18},... | collective-permute-start | bytes 3932168 | tf_op jit(solution)/shard_map/ppermute | solution.py:315
  71.9 22.1 %collective-permute-start.7 = (bf16[2048,128]{1,0:T(8,128)(2,1)}, bf16[2048,128]{1,0:T(8,128)(2,1)}, u32[]{:S(2)}, u32[]{:S(2)}) collective-permute-start(bf16[2048,128]{1,0:T(8,128)(2,1)} %pad_maximum_fusion.1), channel_id=1, source_target_pairs={{0,2},{2,0},{4,6},{6,4},{8,10},{10,8},{12,14},{14,12},{1,3},{3,1},... | collective-permute-start | bytes 1572872 | tf_op jit(solution)/shard_map/ppermute | solution.py:350
  116.0 21.4 %collective-permute-start.13 = (bf16[2048,1024]{1,0:T(8,128)(2,1)}, bf16[2048,1024]{1,0:T(8,128)(2,1)}, u32[]{:S(2)}, u32[]{:S(2)}) collective-permute-start(bf16[2048,1024]{1,0:T(8,128)(2,1)} %bitcast.30), channel_id=1, source_target_pairs={{0,1},{1,0},{2,3},{3,2},{4,5},{5,4},{6,7},{7,6},{8,9},{9,8},{10,11... | collective-permute-start | bytes 12582920 | tf_op jit(solution)/shard_map/ppermute | solution.py:321
  116.1 11.2 %collective-permute-start.11 = (bf16[1024,1024]{1,0:T(8,128)(2,1)S(1)}, bf16[1024,1024]{1,0:T(8,128)(2,1)}, u32[]{:S(2)}, u32[]{:S(2)}) collective-permute-start(bf16[1024,1024]{1,0:T(8,128)(2,1)S(1)} %collective-permute-done.8.refs_6_.refs_4_), channel_id=1, source_target_pairs={{0,1},{1,0},{2,3},{3,2},{4,5},{5,4},{6,7},{7,6},{8,9},{9,8},{10,11... | collective-permute-start | bytes 6291464 | tf_op jit(solution)/shard_map/ppermute | solution.py:321
  117.7 28.8 %collective-permute-start.10 = (bf16[640,1024]{1,0:T(8,128)(2,1)}, bf16[640,1024]{1,0:T(8,128)(2,1)S(1)}, u32[]{:S(2)}, u32[]{:S(2)}) collective-permute-start(bf16[640,1024]{1,0:T(8,128)(2,1)} %collective-permute-done.5.refs_2_), channel_id=1, source_target_pairs={{8,12},{10,14},{9,13},{11,15},{24,28},{26,30},{25,29},{27,31}} | collective-permute-start | bytes 3932168 | tf_op jit(solution)/shard_map/ppermute | solution.py:314
  118.5 38.0 %collective-permute-start.16 = (bf16[640,1024]{1,0:T(8,128)(2,1)}, bf16[640,1024]{1,0:T(8,128)(2,1)S(1)}, u32[]{:S(2)}, u32[]{:S(2)}) collective-permute-start(bf16[640,1024]{1,0:T(8,128)(2,1)} %collective-permute-done.6.refs_4_), channel_id=1, source_target_pairs={{4,0},{6,2},{5,1},{7,3},{20,16},{22,18},{21,17},{23,19}} | collective-permute-start | bytes 3932168 | tf_op jit(solution)/shard_map/ppermute | solution.py:315
  146.6 19.8 %collective-permute-start.14 = (bf16[384,1024]{1,0:T(8,128)(2,1)}, bf16[384,1024]{1,0:T(8,128)(2,1)S(1)}, u32[]{:S(2)}, u32[]{:S(2)}) collective-permute-start(bf16[384,1024]{1,0:T(8,128)(2,1)} %collective-permute-done.2.refs_1_), channel_id=1, source_target_pairs={{4,8},{6,10},{8,12},{10,14},{5,9},{7,11},{9,13},{11,15},{20,24},{2... | collective-permute-start | bytes 2359304 | tf_op jit(solution)/shard_map/ppermute | solution.py:314
  147.3 33.0 %collective-permute-start.15 = (bf16[384,1024]{1,0:T(8,128)(2,1)}, bf16[384,1024]{1,0:T(8,128)(2,1)}, u32[]{:S(2)}, u32[]{:S(2)}) collective-permute-start(bf16[384,1024]{1,0:T(8,128)(2,1)} %collective-permute-done.3.refs_3_), channel_id=1, source_target_pairs={{4,0},{6,2},{8,4},{10,6},{5,1},{7,3},{9,5},{11,7},{20,16},{22,18},... | collective-permute-start | bytes 2359304 | tf_op jit(solution)/shard_map/ppermute | solution.py:315
  164.8 40.6 %collective-permute-start.19 = (bf16[640,1024]{1,0:T(8,128)(2,1)}, bf16[640,1024]{1,0:T(8,128)(2,1)}, u32[]{:S(2)}, u32[]{:S(2)}) collective-permute-start(bf16[640,1024]{1,0:T(8,128)(2,1)} %get-tuple-element.67), channel_id=1, source_target_pairs={{0,2},{2,0},{4,6},{6,4},{8,10},{10,8},{12,14},{14,12},{1,3},{3,1},... | collective-permute-start | bytes 3932168 | tf_op jit(solution)/shard_map/ppermute | solution.py:512
  180.2 25.2 %collective-permute-start.17 = (bf16[384,1024]{1,0:T(8,128)(2,1)S(1)}, bf16[384,1024]{1,0:T(8,128)(2,1)}, u32[]{:S(2)}, u32[]{:S(2)}) collective-permute-start(bf16[384,1024]{1,0:T(8,128)(2,1)S(1)} %collective-permute-done.14.refs_2_), channel_id=1, source_target_pairs={{8,12},{10,14},{9,13},{11,15},{24,28},{26,30},{25,29},{27,31}} | collective-permute-start | bytes 2359304 | tf_op jit(solution)/shard_map/ppermute | solution.py:314
  181.8 23.6 %collective-permute-start.18 = (bf16[384,1024]{1,0:T(8,128)(2,1)}, bf16[384,1024]{1,0:T(8,128)(2,1)}, u32[]{:S(2)}, u32[]{:S(2)}) collective-permute-start(bf16[384,1024]{1,0:T(8,128)(2,1)} %collective-permute-done.15.refs_4_), channel_id=1, source_target_pairs={{4,0},{6,2},{5,1},{7,3},{20,16},{22,18},{21,17},{23,19}} | collective-permute-start | bytes 2359304 | tf_op jit(solution)/shard_map/ppermute | solution.py:315
  183.9 21.5 %all-to-all-start.1 = ((bf16[8,16,640]{2,1,0:T(8,128)(2,1)}), bf16[8,16,640]{2,1,0:T(8,128)(2,1)S(1)}, u32[]{:S(2)}, u32[]{:S(2)}) async-start(bf16[8,16,640]{2,1,0:T(8,128)(2,1)} %get-tuple-element.71), calls=%async_computation.1 | async-start | bytes 327680 | tf_op jit(solution)/shard_map/all_to_all | solution.py:457
  188.8 30.2 %collective-permute-start.21 = (bf16[512,1024]{1,0:T(8,128)(2,1)S(1)}, bf16[512,1024]{1,0:T(8,128)(2,1)S(1)}, u32[]{:S(2)}, u32[]{:S(2)}) collective-permute-start(bf16[512,1024]{1,0:T(8,128)(2,1)S(1)} %bitcast.35), channel_id=1, source_target_pairs={{0,1},{1,0},{2,3},{3,2},{4,5},{5,4},{6,7},{7,6},{8,9},{9,8},{10,11... | collective-permute-start | bytes 3145736 | tf_op jit(solution)/shard_map/ppermute | solution.py:321
  211.2 19.6 %collective-permute-start.20 = (bf16[384,1024]{1,0:T(8,128)(2,1)}, bf16[384,1024]{1,0:T(8,128)(2,1)}, u32[]{:S(2)}, u32[]{:S(2)}) collective-permute-start(bf16[384,1024]{1,0:T(8,128)(2,1)} %get-tuple-element.75), channel_id=1, source_target_pairs={{0,2},{2,0},{4,6},{6,4},{8,10},{10,8},{12,14},{14,12},{1,3},{3,1},... | collective-permute-start | bytes 2359304 | tf_op jit(solution)/shard_map/ppermute | solution.py:520
  214.2 16.6 %all-to-all-start.2 = ((bf16[8,16,384]{2,1,0:T(8,128)(2,1)}), bf16[8,16,384]{2,1,0:T(8,128)(2,1)S(1)}, u32[]{:S(2)}, u32[]{:S(2)}) async-start(bf16[8,16,384]{2,1,0:T(8,128)(2,1)} %get-tuple-element.74), calls=%async_computation.2 | async-start | bytes 196608 | tf_op jit(solution)/shard_map/all_to_all | solution.py:457
  (16 other events, 259.3 us)

commit v5 on v4

--- a/solution.py
+++ b/solution.py
@@ -510,15 +510,17 @@
     expand = [expand_half, to_other_core(expand_half)]
     partial_a, shrunk_a = rest_part(0, early_a)
     got_a = lax.ppermute(partial_a, "tp", across)
-    ups[1][2], downs[1][2] = step((ups[1][2], downs[1][2]), partial_a)
+    ready = (ups[1][2], downs[1][2], farthest_own, entry_adapter, unfold)
+    ready = step(ready, partial_a)
+    ups[1][2], downs[1][2], farthest_own, entry_adapter, unfold = ready
     hop(1, 3)
     everyone_a = spread_out(shrunk_a)
     early_c = early_part(1)
-    base_c = own_part(1, early_c)
-    ups[1][3], downs[1][3] = step((ups[1][3], downs[1][3]), base_c, got_a, everyone_a)
+    ups[1][3], downs[1][3] = step((ups[1][3], downs[1][3]), early_c, got_a)
     partial_c, shrunk_c = rest_part(1, early_c)
     got_c = lax.ppermute(partial_c, "tp", across)
     everyone_c = spread_out(shrunk_c)
+    base_c = own_part(1, partial_c, everyone_a)
     out = last_part(0, base_a, got_a, everyone_a, expand, None)
     return last_part(1, base_c, got_c, everyone_c, expand, out)
 

time: 240 us -> 239 us (level)
    ppermute x6, waiting for transfers between devices: 48.4 us -> 54.9 us  [hop(): downs[c][h] = lax.ppermute(downs[c][h - 1], 'tp', down(h))]
    all_to_all x2, waiting for transfers between devices: 4.96 us -> 0.29 us  [spread_out(): return lax.all_to_all(shrunk, 'tp', split_axis=0, concat_axis=0, tiled=True)]
where the time goes in v5:
time: 239 us
  waiting for transfers between devices  107 us (45%)
  Pallas kernels  60.9 us (25%)
  starting transfers between devices  43.8 us (18%)
  local copies, waits for them, and re-layouts  20 us (8%)
  other arithmetic  6.19 us (3%)
    ppermute x6, waiting for transfers between devices, hop(): downs[c][h] = lax.ppermute(downs[c][h - 1], 'tp', down(h))  54.9 us
    pallas_call x4, Pallas kernels, on_line(): pl.pallas_call(kernel, grid_spec=pltpu.PrefetchScalarGridSpec(num_scalar_...  33.8 us
    ppermute x6, waiting for transfers between devices, hop(): ups[c][h] = lax.ppermute(ups[c][h - 1], 'tp', up(h))  30.8 us
    ppermute x6, starting transfers between devices, hop(): ups[c][h] = lax.ppermute(ups[c][h - 1], 'tp', up(h))  14.8 us
    pallas_call x2, Pallas kernels, last_part(): pl.pallas_call(functools.partial(last_kernel, starts[c]), grid_spec=pltpu...  14.3 us
    ppermute x1, waiting for transfers between devices, line_body(): shrink_near = lax.ppermute(leaving, 'tp', across)  14.2 us
    pallas_call x2, Pallas kernels, rest_part(): pl.pallas_call(rest_kernel, grid_spec=pltpu.PrefetchScalarGridSpec(num_sc...  12.8 us
    all_to_all x2, starting transfers between devices, spread_out(): return lax.all_to_all(shrunk, 'tp', split_axis=0, concat_axis=0, tiled=True)  8.22 us
  transfers between devices with their start and end apart: 25, of which 9 were waited for; matrix products, arithmetic and copies ran while one was open for 8% of the time, Pallas kernels for 23%

profile of v5, /device:TPU:0, one launch (start us, length us, event | category | flops | bytes accessed | tf_op | source)
XLA Modules:
  0.0 238.6 jit_solution(8176167712406000332)
XLA Ops:
  0.0 3.2 %dynamic-slice_bitcast_fusion = bf16[1024,1024]{1,0:T(8,128)(2,1)} fusion(bf16[4,1024,1024]{2,1,0:T(8,128)(2,1)} %bitcast.38, s32[]{:T(128)S(6)} %select_n.231), kind=kLoop, calls=%fused_computation | loop fusion | bytes 4194308 | tf_op jit(solution)/shard_map/jit(dynamic_index_in_dim)/squeeze | solution.py:67
  3.2 2.9 %collective-permute-start.4 = (bf16[1024,1024]{1,0:T(8,128)(2,1)}, bf16[1024,1024]{1,0:T(8,128)(2,1)}, u32[]{:S(2)}, u32[]{:S(2)}) collective-permute-start(bf16[1024,1024]{1,0:T(8,128)(2,1)} %dynamic-slice_bitcast_fusion), channel_id=1, source_target_pairs={{0,2},{2,0},{4,6},{6,4},{8,10},{10,8},{12,14},{14,12},{1,3},{3,1},... | collective-permute-start | bytes 6291464 | tf_op jit(solution)/shard_map/ppermute | solution.py:339
  7.4 4.5 %collective-permute-start = (bf16[640,1024]{1,0:T(8,128)(2,1)}, bf16[640,1024]{1,0:T(8,128)(2,1)}, u32[]{:S(2)}, u32[]{:S(2)}) collective-permute-start(bf16[640,1024]{1,0:T(8,128)(2,1)} %slice.20.refs_0_), channel_id=1, source_target_pairs={{0,4},{2,6},{4,8},{6,10},{8,12},{10,14},{1,5},{3,7},{5,9},{7,11},{... | collective-permute-start | bytes 3932168 | tf_op jit(solution)/shard_map/ppermute | solution.py:314
  13.3 5.4 %collective-permute-start.2 = (bf16[384,1024]{1,0:T(8,128)(2,1)S(1)}, bf16[384,1024]{1,0:T(8,128)(2,1)}, u32[]{:S(2)}, u32[]{:S(2)}) collective-permute-start(bf16[384,1024]{1,0:T(8,128)(2,1)S(1)} %slice.21.refs_0_), channel_id=1, source_target_pairs={{0,4},{2,6},{4,8},{6,10},{8,12},{10,14},{1,5},{3,7},{5,9},{7,11},{... | collective-permute-start | bytes 2359304 | tf_op jit(solution)/shard_map/ppermute | solution.py:314
  24.8 30.8 %collective-permute-done.2.refs_1_ = bf16[384,1024]{1,0:T(8,128)(2,1)} collective-permute-done((bf16[384,1024]{1,0:T(8,128)(2,1)S(1)}, bf16[384,1024]{1,0:T(8,128)(2,1)}, u32[]{:S(2)}, u32[]{:S(2)}) %collective-permute-start.2) | collective-permute-done | bytes 786464 | tf_op jit(solution)/shard_map/ppermute | solution.py:314
  55.7 5.3 %collective-permute-done.3.refs_3_ = bf16[384,1024]{1,0:T(8,128)(2,1)} collective-permute-done((bf16[384,1024]{1,0:T(8,128)(2,1)S(1)}, bf16[384,1024]{1,0:T(8,128)(2,1)}, u32[]{:S(2)}, u32[]{:S(2)}) %collective-permute-start.3) | collective-permute-done | bytes 786464 | tf_op jit(solution)/shard_map/ppermute | solution.py:315
  64.1 3.6 %all-to-all-start = ((bf16[8,64,1024]{2,1,0:T(8,128)(2,1)}), bf16[8,64,1024]{2,1,0:T(8,128)(2,1)S(1)}, u32[]{:S(2)}, u32[]{:S(2)}) async-start(bf16[8,64,1024]{2,1,0:T(8,128)(2,1)} %copy.21), calls=%async_computation | async-start | bytes 2097152 | tf_op jit(solution)/shard_map/all_to_all | solution.py:355
  73.8 4.7 %constant_dynamic-slice_fusion = bf16[2,1,1024,1024]{3,2,1,0:T(8,128)(2,1)} fusion(bf16[2,2,1024,1024]{3,2,1,0:T(8,128)(2,1)} %bitcast.39, s32[]{:T(128)S(6)} %select_n.239), kind=kLoop, calls=%fused_computation.40 | loop fusion | bytes 8388612 | tf_op jit(solution)/shard_map/jit(dynamic_index_in_dim)/dynamic_slice | solution.py:353
  79.7 14.2 %collective-permute-done.7.refs_10_.refs_8_ = bf16[2048,128]{1,0:T(8,128)(2,1)} collective-permute-done((bf16[2048,128]{1,0:T(8,128)(2,1)}, bf16[2048,128]{1,0:T(8,128)(2,1)}, u32[]{:S(2)}, u32[]{:S(2)}) %collective-permute-start.7) | collective-permute-done | bytes 524320 | tf_op jit(solution)/shard_map/ppermute | solution.py:350
  94.0 22.0 %collective-permute-done.6.refs_4_ = bf16[640,1024]{1,0:T(8,128)(2,1)} collective-permute-done((bf16[640,1024]{1,0:T(8,128)(2,1)}, bf16[640,1024]{1,0:T(8,128)(2,1)}, u32[]{:S(2)}, u32[]{:S(2)}) %collective-permute-start.6) | collective-permute-done | bytes 1310752 | tf_op jit(solution)/shard_map/ppermute | solution.py:315
  120.4 6.9 %collective-permute-done.12.refs_11_.refs_9_ = bf16[2048,128]{1,0:T(8,128)(2,1)} collective-permute-done((bf16[2048,128]{1,0:T(8,128)(2,1)}, bf16[2048,128]{1,0:T(8,128)(2,1)}, u32[]{:S(2)}, u32[]{:S(2)}) %collective-permute-start.12) | collective-permute-done | bytes 524320 | tf_op jit(solution)/shard_map/ppermute | solution.py:321
  127.3 10.1 %shard_map.64.refs_0_ = f32[640,1280]{1,0:T(8,128)} custom-call(s32[4]{0:T(128)} %get-tuple-element.81.sel, s32[4]{0:T(128)} %get-tuple-element.58.place, bf16[640,1024]{1,0:T(8,128)(2,1)} %slice.20.refs_0_, bf16[640,1024]{1,0:T(8,128)(2,1)} %collective-permute-done.refs_1_, bf16[640,1024]{1,0:T(8,128)(2,1)} %collective-permute-done.5.refs_2_, ...), custom_call_target="tpu_custom_call" | custom-call | flops 5368709120 | bytes 16252928 | tf_op jit(solution)/shard_map/pallas_call | solution.py:256
  137.4 9.1 %shard_map.65.refs_0_ = f32[640,1024]{1,0:T(8,128)} custom-call(s32[4]{0:T(128)} %get-tuple-element.81.sel, s32[4]{0:T(128)} %fusion.14.place, bf16[640,1024]{1,0:T(8,128)(2,1)} %slice.20.refs_0_, bf16[640,1024]{1,0:T(8,128)(2,1)} %collective-permute-done.refs_1_, bf16[640,1024]{1,0:T(8,128)(2,1)} %collective-permute-done.5.refs_2_, ...), custom_call_target="tpu_custom_call" | custom-call | flops 5368709120 | bytes 16252928 | tf_op jit(solution)/shard_map/pallas_call | solution.py:256
  149.1 7.3 %collective-permute-done.16.refs_2_.refs_5_ = bf16[640,1024]{1,0:T(8,128)(2,1)S(1)} collective-permute-done((bf16[640,1024]{1,0:T(8,128)(2,1)}, bf16[640,1024]{1,0:T(8,128)(2,1)S(1)}, u32[]{:S(2)}, u32[]{:S(2)}) %collective-permute-start.16) | collective-permute-done | bytes 1310752 | tf_op jit(solution)/shard_map/ppermute | solution.py:315
  157.5 7.2 %shard_map.66 = (bf16[640,1024]{1,0:T(8,128)(2,1)}, bf16[8,16,640]{2,1,0:T(8,128)(2,1)}) custom-call(s32[1]{0:T(128)} %bitcast.15.farthest, f32[640,1280]{1,0:T(8,128)} %shard_map.64.refs_0_, bf16[640,1024]{1,0:T(8,128)(2,1)} %copy-done.5, bf16[640,1024]{1,0:T(8,128)(2,1)} %copy-done.6, bf16[1024,1024]{1,0:T(8,128)(2,1)} %collective-permute-done.4.refs_5_.refs_3_, ...), custom_call_target="tpu_custom_call" | custom-call | flops 1677721600 | bytes 4194304 | tf_op jit(solution)/shard_map/pallas_call | solution.py:419
  168.2 12.1 %collective-permute-done.15.refs_4_ = bf16[384,1024]{1,0:T(8,128)(2,1)} collective-permute-done((bf16[384,1024]{1,0:T(8,128)(2,1)}, bf16[384,1024]{1,0:T(8,128)(2,1)}, u32[]{:S(2)}, u32[]{:S(2)}) %collective-permute-start.15) | collective-permute-done | bytes 786464 | tf_op jit(solution)/shard_map/ppermute | solution.py:315
  184.0 4.9 %all-to-all-start.2 = ((bf16[8,16,640]{2,1,0:T(8,128)(2,1)}), bf16[8,16,640]{2,1,0:T(8,128)(2,1)S(1)}, u32[]{:S(2)}, u32[]{:S(2)}) async-start(bf16[8,16,640]{2,1,0:T(8,128)(2,1)} %get-tuple-element.80), calls=%async_computation.2 | async-start | bytes 327680 | tf_op jit(solution)/shard_map/all_to_all | solution.py:457
  188.9 7.8 %shard_map.67.refs_0_ = f32[384,1280]{1,0:T(8,128)} custom-call(s32[4]{0:T(128)} %get-tuple-element.81.sel, s32[4]{0:T(128)} %get-tuple-element.58.place, bf16[384,1024]{1,0:T(8,128)(2,1)} %copy-done.4, bf16[384,1024]{1,0:T(8,128)(2,1)} %collective-permute-done.2.refs_1_, bf16[384,1024]{1,0:T(8,128)(2,1)} %copy-done.8, ...), custom_call_target="tpu_custom_call" | custom-call | flops 3221225472 | bytes 13107200 | tf_op jit(solution)/shard_map/pallas_call | solution.py:256
  196.7 8.3 %collective-permute-done.18.refs_2_.refs_5_ = bf16[384,1024]{1,0:T(8,128)(2,1)} collective-permute-done((bf16[384,1024]{1,0:T(8,128)(2,1)}, bf16[384,1024]{1,0:T(8,128)(2,1)}, u32[]{:S(2)}, u32[]{:S(2)}) %collective-permute-start.18) | collective-permute-done | bytes 786464 | tf_op jit(solution)/shard_map/ppermute | solution.py:315
  205.0 5.6 %shard_map.68 = (bf16[384,1024]{1,0:T(8,128)(2,1)}, bf16[8,16,384]{2,1,0:T(8,128)(2,1)}) custom-call(s32[1]{0:T(128)} %bitcast.15.farthest, f32[384,1280]{1,0:T(8,128)} %shard_map.67.refs_0_, bf16[384,1024]{1,0:T(8,128)(2,1)} %collective-permute-done.17.refs_1_.refs_4_, bf16[384,1024]{1,0:T(8,128)(2,1)} %collective-permute-done.18.refs_2_.refs_5_, ...), custom_call_target="tpu_custom_call" | custom-call | flops 1006632960 | bytes 4194304 | tf_op jit(solution)/shard_map/pallas_call | solution.py:419
  213.0 7.7 %shard_map.70.refs_8_ = bf16[1024,1024]{1,0:T(8,128)(2,1)} custom-call(s32[2]{0:T(128)} %pad_add_fusion.farthest, bf16[8,16,640]{2,1,0:T(8,128)(2,1)} %copy-done.11, s32[640,1]{1,0:T(8,128)} %slice.26.refs_10_.stored, s32[1,1024]{1,0:T(1,128)} %fusion.7.adapter, bf16[16,1024]{1,0:T(8,128)(2,1)} %fusion.unfold, f32[640,1024]{1,0:T(8,128)} %shard_map.65.refs_0_, ...), custom_call_target="tpu_custom_call" | custom-call | flops 2684354560 | bytes 4194304 | tf_op jit(solution)/shard_map/pallas_call | solution.py:466
  220.7 3.4 %all-to-all-start.1 = ((bf16[8,16,384]{2,1,0:T(8,128)(2,1)}), bf16[8,16,384]{2,1,0:T(8,128)(2,1)S(1)}, u32[]{:S(2)}, u32[]{:S(2)}) async-start(bf16[8,16,384]{2,1,0:T(8,128)(2,1)} %get-tuple-element.76), calls=%async_computation.1 | async-start | bytes 196608 | tf_op jit(solution)/shard_map/all_to_all | solution.py:457
  224.1 6.8 %shard_map.69.refs_0_ = f32[384,1024]{1,0:T(8,128)} custom-call(s32[4]{0:T(128)} %get-tuple-element.81.sel, s32[4]{0:T(128)} %fusion.14.place, bf16[384,1024]{1,0:T(8,128)(2,1)} %copy-done.4, bf16[384,1024]{1,0:T(8,128)(2,1)} %collective-permute-done.2.refs_1_, bf16[384,1024]{1,0:T(8,128)(2,1)} %copy-done.8, ...), custom_call_target="tpu_custom_call" | custom-call | flops 3221225472 | bytes 13107200 | tf_op jit(solution)/shard_map/pallas_call | solution.py:256
  231.8 6.6 %shard_map.71 = bf16[1024,1024]{1,0:T(8,128)(2,1)} custom-call(s32[2]{0:T(128)} %pad_add_fusion.farthest, bf16[8,16,384]{2,1,0:T(8,128)(2,1)} %copy-done.12, s32[384,1]{1,0:T(8,128)} %slice.27.refs_10_.stored, s32[1,1024]{1,0:T(1,128)} %fusion.7.adapter, bf16[16,1024]{1,0:T(8,128)(2,1)} %fusion.unfold, ...), custom_call_target="tpu_custom_call", output_to_operand_aliasing={{}: (13, {})} | custom-call | flops 1610612736 | bytes 4194304 | tf_op jit(solution)/shard_map/pallas_call | solution.py:466
  (88 shorter events, 37.6 us)
Async XLA Ops:
  3.2 57.7 %collective-permute-start.4 = (bf16[1024,1024]{1,0:T(8,128)(2,1)}, bf16[1024,1024]{1,0:T(8,128)(2,1)}, u32[]{:S(2)}, u32[]{:S(2)}) collective-permute-start(bf16[1024,1024]{1,0:T(8,128)(2,1)} %dynamic-slice_bitcast_fusion), channel_id=1, source_target_pairs={{0,2},{2,0},{4,6},{6,4},{8,10},{10,8},{12,14},{14,12},{1,3},{3,1},... | collective-permute-start | bytes 6291464 | tf_op jit(solution)/shard_map/ppermute | solution.py:339
  7.4 53.6 %collective-permute-start = (bf16[640,1024]{1,0:T(8,128)(2,1)}, bf16[640,1024]{1,0:T(8,128)(2,1)}, u32[]{:S(2)}, u32[]{:S(2)}) collective-permute-start(bf16[640,1024]{1,0:T(8,128)(2,1)} %slice.20.refs_0_), channel_id=1, source_target_pairs={{0,4},{2,6},{4,8},{6,10},{8,12},{10,14},{1,5},{3,7},{5,9},{7,11},{... | collective-permute-start | bytes 3932168 | tf_op jit(solution)/shard_map/ppermute | solution.py:314
  11.9 49.0 %collective-permute-start.1 = (bf16[640,1024]{1,0:T(8,128)(2,1)}, bf16[640,1024]{1,0:T(8,128)(2,1)}, u32[]{:S(2)}, u32[]{:S(2)}) collective-permute-start(bf16[640,1024]{1,0:T(8,128)(2,1)} %slice.20.refs_0_), channel_id=1, source_target_pairs={{4,0},{6,2},{8,4},{10,6},{12,8},{14,10},{5,1},{7,3},{9,5},{11,7},{... | collective-permute-start | bytes 3932168 | tf_op jit(solution)/shard_map/ppermute | solution.py:315
  13.3 42.4 %collective-permute-start.2 = (bf16[384,1024]{1,0:T(8,128)(2,1)S(1)}, bf16[384,1024]{1,0:T(8,128)(2,1)}, u32[]{:S(2)}, u32[]{:S(2)}) collective-permute-start(bf16[384,1024]{1,0:T(8,128)(2,1)S(1)} %slice.21.refs_0_), channel_id=1, source_target_pairs={{0,4},{2,6},{4,8},{6,10},{8,12},{10,14},{1,5},{3,7},{5,9},{7,11},{... | collective-permute-start | bytes 2359304 | tf_op jit(solution)/shard_map/ppermute | solution.py:314
  18.7 42.2 %collective-permute-start.3 = (bf16[384,1024]{1,0:T(8,128)(2,1)S(1)}, bf16[384,1024]{1,0:T(8,128)(2,1)}, u32[]{:S(2)}, u32[]{:S(2)}) collective-permute-start(bf16[384,1024]{1,0:T(8,128)(2,1)S(1)} %slice.21.refs_0_), channel_id=1, source_target_pairs={{4,0},{6,2},{8,4},{10,6},{12,8},{14,10},{5,1},{7,3},{9,5},{11,7},{... | collective-permute-start | bytes 2359304 | tf_op jit(solution)/shard_map/ppermute | solution.py:315
  61.0 55.0 %collective-permute-start.8 = (bf16[1024,1024]{1,0:T(8,128)(2,1)}, bf16[1024,1024]{1,0:T(8,128)(2,1)S(1)}, u32[]{:S(2)}, u32[]{:S(2)}) collective-permute-start(bf16[1024,1024]{1,0:T(8,128)(2,1)} %collective-permute-done.4.refs_5_.refs_3_), channel_id=1, source_target_pairs={{0,16},{16,0},{1,17},{17,1},{2,18},{18,2},{3,19},{19,3},{4,20},{20... | collective-permute-start | bytes 6291464 | tf_op jit(solution)/shard_map/ppermute | solution.py:349
  62.5 53.4 %collective-permute-start.9 = (bf16[1024,1024]{1,0:T(8,128)(2,1)}, bf16[1024,1024]{1,0:T(8,128)(2,1)}, u32[]{:S(2)}, u32[]{:S(2)}) collective-permute-start(bf16[1024,1024]{1,0:T(8,128)(2,1)} %collective-permute-done.4.refs_5_.refs_3_), channel_id=1, source_target_pairs={{0,1},{1,0},{2,3},{3,2},{4,5},{5,4},{6,7},{7,6},{8,9},{9,8},{10,11... | collective-permute-start | bytes 6291464 | tf_op jit(solution)/shard_map/ppermute | solution.py:321
  64.1 51.9 %all-to-all-start = ((bf16[8,64,1024]{2,1,0:T(8,128)(2,1)}), bf16[8,64,1024]{2,1,0:T(8,128)(2,1)S(1)}, u32[]{:S(2)}, u32[]{:S(2)}) async-start(bf16[8,64,1024]{2,1,0:T(8,128)(2,1)} %copy.21), calls=%async_computation | async-start | bytes 2097152 | tf_op jit(solution)/shard_map/all_to_all | solution.py:355
  67.7 26.3 %collective-permute-start.5 = (bf16[640,1024]{1,0:T(8,128)(2,1)}, bf16[640,1024]{1,0:T(8,128)(2,1)}, u32[]{:S(2)}, u32[]{:S(2)}) collective-permute-start(bf16[640,1024]{1,0:T(8,128)(2,1)} %collective-permute-done.refs_1_), channel_id=1, source_target_pairs={{4,8},{6,10},{8,12},{10,14},{5,9},{7,11},{9,13},{11,15},{20,24},{2... | collective-permute-start | bytes 3932168 | tf_op jit(solution)/shard_map/ppermute | solution.py:314
  69.4 46.6 %collective-permute-start.6 = (bf16[640,1024]{1,0:T(8,128)(2,1)}, bf16[640,1024]{1,0:T(8,128)(2,1)}, u32[]{:S(2)}, u32[]{:S(2)}) collective-permute-start(bf16[640,1024]{1,0:T(8,128)(2,1)} %collective-permute-done.1.refs_3_), channel_id=1, source_target_pairs={{4,0},{6,2},{8,4},{10,6},{5,1},{7,3},{9,5},{11,7},{20,16},{22,18},... | collective-permute-start | bytes 3932168 | tf_op jit(solution)/shard_map/ppermute | solution.py:315
  71.9 22.1 %collective-permute-start.7 = (bf16[2048,128]{1,0:T(8,128)(2,1)}, bf16[2048,128]{1,0:T(8,128)(2,1)}, u32[]{:S(2)}, u32[]{:S(2)}) collective-permute-start(bf16[2048,128]{1,0:T(8,128)(2,1)} %pad_maximum_fusion.1), channel_id=1, source_target_pairs={{0,2},{2,0},{4,6},{6,4},{8,10},{10,8},{12,14},{14,12},{1,3},{3,1},... | collective-permute-start | bytes 1572872 | tf_op jit(solution)/shard_map/ppermute | solution.py:350
  116.0 21.4 %collective-permute-start.13 = (bf16[2048,1024]{1,0:T(8,128)(2,1)}, bf16[2048,1024]{1,0:T(8,128)(2,1)}, u32[]{:S(2)}, u32[]{:S(2)}) collective-permute-start(bf16[2048,1024]{1,0:T(8,128)(2,1)} %bitcast.30), channel_id=1, source_target_pairs={{0,1},{1,0},{2,3},{3,2},{4,5},{5,4},{6,7},{7,6},{8,9},{9,8},{10,11... | collective-permute-start | bytes 12582920 | tf_op jit(solution)/shard_map/ppermute | solution.py:321
  116.1 11.2 %collective-permute-start.11 = (bf16[1024,1024]{1,0:T(8,128)(2,1)S(1)}, bf16[1024,1024]{1,0:T(8,128)(2,1)}, u32[]{:S(2)}, u32[]{:S(2)}) collective-permute-start(bf16[1024,1024]{1,0:T(8,128)(2,1)S(1)} %collective-permute-done.8.refs_6_.refs_4_), channel_id=1, source_target_pairs={{0,1},{1,0},{2,3},{3,2},{4,5},{5,4},{6,7},{7,6},{8,9},{9,8},{10,11... | collective-permute-start | bytes 6291464 | tf_op jit(solution)/shard_map/ppermute | solution.py:321
  116.6 10.7 %collective-permute-start.12 = (bf16[2048,128]{1,0:T(8,128)(2,1)}, bf16[2048,128]{1,0:T(8,128)(2,1)}, u32[]{:S(2)}, u32[]{:S(2)}) collective-permute-start(bf16[2048,128]{1,0:T(8,128)(2,1)} %collective-permute-done.7.refs_10_.refs_8_), channel_id=1, source_target_pairs={{0,1},{1,0},{2,3},{3,2},{4,5},{5,4},{6,7},{7,6},{8,9},{9,8},{10,11... | collective-permute-start | bytes 1572872 | tf_op jit(solution)/shard_map/ppermute | solution.py:321
  117.7 28.8 %collective-permute-start.10 = (bf16[640,1024]{1,0:T(8,128)(2,1)}, bf16[640,1024]{1,0:T(8,128)(2,1)S(1)}, u32[]{:S(2)}, u32[]{:S(2)}) collective-permute-start(bf16[640,1024]{1,0:T(8,128)(2,1)} %collective-permute-done.5.refs_2_), channel_id=1, source_target_pairs={{8,12},{10,14},{9,13},{11,15},{24,28},{26,30},{25,29},{27,31}} | collective-permute-start | bytes 3932168 | tf_op jit(solution)/shard_map/ppermute | solution.py:314
  118.5 38.0 %collective-permute-start.16 = (bf16[640,1024]{1,0:T(8,128)(2,1)}, bf16[640,1024]{1,0:T(8,128)(2,1)S(1)}, u32[]{:S(2)}, u32[]{:S(2)}) collective-permute-start(bf16[640,1024]{1,0:T(8,128)(2,1)} %collective-permute-done.6.refs_4_), channel_id=1, source_target_pairs={{4,0},{6,2},{5,1},{7,3},{20,16},{22,18},{21,17},{23,19}} | collective-permute-start | bytes 3932168 | tf_op jit(solution)/shard_map/ppermute | solution.py:315
  146.6 21.6 %collective-permute-start.14 = (bf16[384,1024]{1,0:T(8,128)(2,1)}, bf16[384,1024]{1,0:T(8,128)(2,1)S(1)}, u32[]{:S(2)}, u32[]{:S(2)}) collective-permute-start(bf16[384,1024]{1,0:T(8,128)(2,1)} %collective-permute-done.2.refs_1_), channel_id=1, source_target_pairs={{4,8},{6,10},{8,12},{10,14},{5,9},{7,11},{9,13},{11,15},{20,24},{2... | collective-permute-start | bytes 2359304 | tf_op jit(solution)/shard_map/ppermute | solution.py:314
  147.3 33.0 %collective-permute-start.15 = (bf16[384,1024]{1,0:T(8,128)(2,1)}, bf16[384,1024]{1,0:T(8,128)(2,1)}, u32[]{:S(2)}, u32[]{:S(2)}) collective-permute-start(bf16[384,1024]{1,0:T(8,128)(2,1)} %collective-permute-done.3.refs_3_), channel_id=1, source_target_pairs={{4,0},{6,2},{8,4},{10,6},{5,1},{7,3},{9,5},{11,7},{20,16},{22,18},... | collective-permute-start | bytes 2359304 | tf_op jit(solution)/shard_map/ppermute | solution.py:315
  164.7 32.0 %collective-permute-start.19 = (bf16[640,1024]{1,0:T(8,128)(2,1)}, bf16[640,1024]{1,0:T(8,128)(2,1)}, u32[]{:S(2)}, u32[]{:S(2)}) collective-permute-start(bf16[640,1024]{1,0:T(8,128)(2,1)} %get-tuple-element.70), channel_id=1, source_target_pairs={{0,2},{2,0},{4,6},{6,4},{8,10},{10,8},{12,14},{14,12},{1,3},{3,1},... | collective-permute-start | bytes 3932168 | tf_op jit(solution)/shard_map/ppermute | solution.py:512
  180.2 16.5 %collective-permute-start.17 = (bf16[384,1024]{1,0:T(8,128)(2,1)S(1)}, bf16[384,1024]{1,0:T(8,128)(2,1)}, u32[]{:S(2)}, u32[]{:S(2)}) collective-permute-start(bf16[384,1024]{1,0:T(8,128)(2,1)S(1)} %collective-permute-done.14.refs_2_), channel_id=1, source_target_pairs={{8,12},{10,14},{9,13},{11,15},{24,28},{26,30},{25,29},{27,31}} | collective-permute-start | bytes 2359304 | tf_op jit(solution)/shard_map/ppermute | solution.py:314
  181.8 23.2 %collective-permute-start.18 = (bf16[384,1024]{1,0:T(8,128)(2,1)}, bf16[384,1024]{1,0:T(8,128)(2,1)}, u32[]{:S(2)}, u32[]{:S(2)}) collective-permute-start(bf16[384,1024]{1,0:T(8,128)(2,1)} %collective-permute-done.15.refs_4_), channel_id=1, source_target_pairs={{4,0},{6,2},{5,1},{7,3},{20,16},{22,18},{21,17},{23,19}} | collective-permute-start | bytes 2359304 | tf_op jit(solution)/shard_map/ppermute | solution.py:315
  183.1 28.2 %collective-permute-start.21 = (bf16[512,1024]{1,0:T(8,128)(2,1)S(1)}, bf16[512,1024]{1,0:T(8,128)(2,1)S(1)}, u32[]{:S(2)}, u32[]{:S(2)}) collective-permute-start(bf16[512,1024]{1,0:T(8,128)(2,1)S(1)} %bitcast.35), channel_id=1, source_target_pairs={{0,1},{1,0},{2,3},{3,2},{4,5},{5,4},{6,7},{7,6},{8,9},{9,8},{10,11... | collective-permute-start | bytes 3145736 | tf_op jit(solution)/shard_map/ppermute | solution.py:321
  184.0 27.3 %all-to-all-start.2 = ((bf16[8,16,640]{2,1,0:T(8,128)(2,1)}), bf16[8,16,640]{2,1,0:T(8,128)(2,1)S(1)}, u32[]{:S(2)}, u32[]{:S(2)}) async-start(bf16[8,16,640]{2,1,0:T(8,128)(2,1)} %get-tuple-element.80), calls=%async_computation.2 | async-start | bytes 327680 | tf_op jit(solution)/shard_map/all_to_all | solution.py:457
  210.6 20.6 %collective-permute-start.20 = (bf16[384,1024]{1,0:T(8,128)(2,1)}, bf16[384,1024]{1,0:T(8,128)(2,1)}, u32[]{:S(2)}, u32[]{:S(2)}) collective-permute-start(bf16[384,1024]{1,0:T(8,128)(2,1)} %get-tuple-element.79), channel_id=1, source_target_pairs={{0,2},{2,0},{4,6},{6,4},{8,10},{10,8},{12,14},{14,12},{1,3},{3,1},... | collective-permute-start | bytes 2359304 | tf_op jit(solution)/shard_map/ppermute | solution.py:521
  (16 other events, 246.3 us)
